TPU v7x, 32 devices: a whole 2x2x4 slice. The times are simulated.
32 devices in a mesh: grp: 8 (over z, x), psg: 4 (over y, core).
Axes of the slice: x: 2, y: 2, z: 4, core: 2. Of those that a mesh axis runs over, the one named last changes fastest.
Arguments:
- query_ids: int32 [256, 32], P(('grp', 'psg')), may hold values from 0 to 30719
- passage_ids: int32 [32, 1024], P(('grp', 'psg')), may hold values from 0 to 30719
- passage_lengths: int32 [32, 32], P(('grp', 'psg')), may hold values from 1 to 64, 1024 in all within a row
- positives: int32 [256], P(('grp', 'psg')), may hold values from 0 to 127
- negatives: int32 [256, 8], P(('grp', 'psg')), may hold values from 0 to 127
- pair_mask: int32 [256, 8], P(('grp', 'psg')), may hold values 0 or 1
- assignments: int32 [32, 1024], P(('grp', 'psg')), may hold values from 0 to 1023
- step_count: int32 [1], replicated, may hold values from 1 to 20
- embed_table: float32 [30720, 768], P(('grp', 'psg')), may hold values from -1.75 to 1.75
- embed_table_moment: float32 [30720, 768], P(('grp', 'psg')), may hold values from -6.1035156e-05 to 6.1035156e-05
- embed_table_second: float32 [30720, 768], P(('grp', 'psg')), may hold values from 1.0625e-11 to 4.25e-11
- attention_weight: float32 [768, 3072], P(None, ('grp', 'psg')), may hold values from -0.21875 to 0.21875
- attention_weight_moment: float32 [768, 3072], P(None, ('grp', 'psg')), may hold values from -0.0017089844 to 0.0017089844
- attention_weight_second: float32 [768, 3072], P(None, ('grp', 'psg')), may hold values from 6.875e-09 to 2.75e-08
- up_weight: float32 [768, 3072], P(None, ('grp', 'psg')), may hold values from -0.21875 to 0.21875
- up_weight_moment: float32 [768, 3072], P(None, ('grp', 'psg')), may hold values from -0.0007324219 to 0.0007324219
- up_weight_second: float32 [768, 3072], P(None, ('grp', 'psg')), may hold values from 1.4375e-09 to 5.75e-09
- down_weight: float32 [3072, 768], P(('grp', 'psg')), may hold values from -0.109375 to 0.109375
- down_weight_moment: float32 [3072, 768], P(('grp', 'psg')), may hold values from -0.0017089844 to 0.0017089844
- down_weight_second: float32 [3072, 768], P(('grp', 'psg')), may hold values from 7.5e-09 to 2.875e-08
- head_weight: float32 [768, 128], P(('grp', 'psg')), may hold values from -0.21875 to 0.21875
- head_weight_moment: float32 [768, 128], P(('grp', 'psg')), may hold values from -0.0048828125 to 0.0048828125
- head_weight_second: float32 [768, 128], P(('grp', 'psg')), may hold values from 6.25e-08 to 2.5e-07
- small_params: float32 [59904], P(('grp', 'psg')), may hold values from -1.75 to 1.75
- small_params_moment: float32 [59904], P(('grp', 'psg')), may hold values from -0.0024414062 to 0.0024414062
- small_params_second: float32 [59904], P(('grp', 'psg')), may hold values from 1.5625e-08 to 6.25e-08
Outputs:
- loss: float32 [], replicated
- centroid_sums: float32 [1024, 128], P(('grp', 'psg'))
- centroid_counts: float32 [1024], P(('grp', 'psg'))
- embed_table_new: float32 [30720, 768], P(('grp', 'psg'))
- embed_table_grad: float32 [30720, 768], P(('grp', 'psg'))
- embed_table_second_new: float32 [30720, 768], P(('grp', 'psg'))
- attention_weight_new: float32 [768, 3072], P(None, ('grp', 'psg'))
- attention_weight_grad: float32 [768, 3072], P(None, ('grp', 'psg'))
- attention_weight_second_new: float32 [768, 3072], P(None, ('grp', 'psg'))
- up_weight_new: float32 [768, 3072], P(None, ('grp', 'psg'))
- up_weight_grad: float32 [768, 3072], P(None, ('grp', 'psg'))
- up_weight_second_new: float32 [768, 3072], P(None, ('grp', 'psg'))
- down_weight_new: float32 [3072, 768], P(('grp', 'psg'))
- down_weight_grad: float32 [3072, 768], P(('grp', 'psg'))
- down_weight_second_new: float32 [3072, 768], P(('grp', 'psg'))
- head_weight_new: float32 [768, 128], P(('grp', 'psg'))
- head_weight_grad: float32 [768, 128], P(('grp', 'psg'))
- head_weight_second_new: float32 [768, 128], P(('grp', 'psg'))
- small_params_new: float32 [59904], P(('grp', 'psg'))
- small_params_grad: float32 [59904], P(('grp', 'psg'))
- small_params_second_new: float32 [59904], P(('grp', 'psg'))
Inputs may be any that keep to these rules, and one draw needn't show every extreme that they name: `passage_lengths`: each row's 32 lengths add up to 1024; the longest in every row is exactly 64.
All inputs are finite; a program needn't handle non-finite values. No bound on the sum of `pair_mask` on one device may be relied on, other than what follows from the above.
Results may differ from a plain program's by a relative error of at most 0.011.
Values may be sent and summed in bfloat16 or wider, within the bound.
A program may use at most 384 MiB of HBM per device.

v0:
```python
import math

import jax
import jax.numpy as jnp
from jax import lax
from jax.sharding import PartitionSpec as P

D = 768
HEADS = 12
HD = 64
SEG = 32
PMAX = 64
ROW = 1024
PPD = 32
QDEV = 8
NCENT = 1024


HIGHEST = lax.Precision.HIGHEST
TEMPER = 0.2
MARGIN = 1.0
NORM_EPS = 1e-06
BETA_ONE = 0.9
BETA_TWO = 0.999
ADAM_EPS = 1e-08
WEIGHT_DECAY = 0.01
RATE_MATRIX = 0.01
RATE_TABLE = 0.1


def matmul(lhs_mat, rhs_mat):
    return jnp.dot(lhs_mat, rhs_mat, preferred_element_type=jnp.float32)


def contract_rows(lhs_mat, rhs_mat):
    return lax.dot_general(
        lhs_mat, rhs_mat, (((0,), (0,)), ((), ())), preferred_element_type=jnp.float32
    )


def contract_cols(lhs_mat, rhs_mat):
    return lax.dot_general(
        lhs_mat, rhs_mat, (((1,), (1,)), ((), ())), preferred_element_type=jnp.float32
    )


def layer_norm(values, scale_gain, shift_bias):
    average = jnp.mean(values, axis=-1, keepdims=True)
    centered = values - average
    inverse = lax.rsqrt(jnp.mean(centered * centered, axis=-1, keepdims=True) + NORM_EPS)
    normed = centered * inverse
    return (normed * (1.0 + scale_gain) + shift_bias, (normed, inverse))


def norm_back(upstream, stored, scale_gain):
    normed, inverse = stored
    scaled = upstream * (1.0 + scale_gain)
    back = inverse * (
        scaled
        - jnp.mean(scaled, axis=-1, keepdims=True)
        - normed * jnp.mean(scaled * normed, axis=-1, keepdims=True)
    )
    return (back, jnp.sum(upstream * normed, axis=0), jnp.sum(upstream, axis=0))


def split_vector(vector):
    positions = vector[: PMAX * D].reshape(PMAX, D)
    remainder = vector[PMAX * D :]
    return (
        positions,
        [remainder[i * D : (i + 1) * D].astype(jnp.float32) for i in range(10)],
        remainder[10 * D :],
    )


def passage_layout(lengths):
    starts = jnp.cumsum(lengths, axis=-1) - lengths
    place = jnp.arange(ROW, dtype=jnp.int32)
    above = (place[None, :, None] >= starts[:, None, :]).astype(jnp.int32)
    segment = jnp.sum(above, axis=-1) - 1
    chosen = (segment[:, :, None] == jnp.arange(PPD, dtype=jnp.int32)).astype(jnp.int32)
    position = place[None, :] - jnp.sum(chosen * starts[:, None, :], axis=-1)
    return (segment, position)


def score_block(query, key_heads, allowed):
    raw = jnp.einsum("rhd,chd->hrc", query, key_heads, preferred_element_type=jnp.float32) * HD ** (
        -0.5
    )
    return jnp.where(allowed[None], raw, -1000000000.0)


def log_totals(scores):
    top = jnp.max(scores, axis=-1, keepdims=True)
    return top + jnp.log(jnp.sum(jnp.exp(scores - top), axis=-1, keepdims=True))


def encode_forward(weights, token_ids, position, segment):
    embed_table, attention_weight, up_weight, down_weight, head_weight, small_params = weights
    positions, pieces, bias_up = split_vector(small_params)
    count_rows = token_ids.shape[0]
    embedded = embed_table[token_ids].astype(jnp.float32) + positions[position].astype(jnp.float32)
    hidden_zero, norm_zero = layer_norm(embedded, pieces[0], pieces[1])
    input_zero = hidden_zero.astype(jnp.bfloat16)
    blank = jnp.zeros((D,), jnp.float32)
    mixed = matmul(input_zero, attention_weight[:, : 3 * D]) + jnp.concatenate(
        [pieces[2], blank, pieces[3]]
    )
    triple = mixed.astype(jnp.bfloat16).reshape(count_rows, 3, HEADS, HD)
    allowed = segment[:, None] == segment[None, :]
    scores = score_block(triple[:, 0], triple[:, 1], allowed)
    log_total = log_totals(scores)
    probs = jnp.exp(scores - log_total)
    context = (
        jnp.einsum(
            "hrc,chd->rhd",
            probs.astype(jnp.bfloat16),
            triple[:, 2],
            preferred_element_type=jnp.float32,
        )
        .reshape(count_rows, D)
        .astype(jnp.bfloat16)
    )
    hidden_one, norm_one = layer_norm(
        hidden_zero + matmul(context, attention_weight[:, 3 * D :]) + pieces[4],
        pieces[5],
        pieces[6],
    )
    input_one = hidden_one.astype(jnp.bfloat16)
    inner = matmul(input_one, up_weight) + bias_up.astype(jnp.float32)
    activated = jax.nn.gelu(inner, approximate=False).astype(jnp.bfloat16)
    hidden_two, norm_two = layer_norm(
        hidden_one + matmul(activated, down_weight) + pieces[7], pieces[8], pieces[9]
    )
    input_two = hidden_two.astype(jnp.bfloat16)
    projected = matmul(input_two, head_weight)
    scale_inverse = lax.rsqrt(jnp.sum(projected * projected, axis=-1, keepdims=True) + NORM_EPS)
    unit = projected * scale_inverse
    stored = (
        norm_zero,
        input_zero,
        triple,
        allowed,
        log_total,
        context,
        norm_one,
        input_one,
        inner,
        activated,
        norm_two,
        input_two,
        unit,
        scale_inverse,
    )
    return (unit.astype(jnp.bfloat16), stored)


def encode_backward(weights, stored, grad_unit, position):
    embed_table, attention_weight, up_weight, down_weight, head_weight, small_params = weights
    positions, pieces, bias_up = split_vector(small_params)
    (
        norm_zero,
        input_zero,
        triple,
        allowed,
        prob_store,
        context,
        norm_one,
        input_one,
        inner,
        activated,
        norm_two,
        input_two,
        unit,
        scale_inverse,
    ) = stored
    count_rows = position.shape[0]
    grad_proj = (
        (grad_unit - unit * jnp.sum(grad_unit * unit, axis=-1, keepdims=True)) * scale_inverse
    ).astype(jnp.bfloat16)
    grad_head = contract_rows(input_two, grad_proj)
    grad_hidden_two = contract_cols(grad_proj, head_weight)
    grad_sum_two, grad_gain_two, grad_shift_two = norm_back(grad_hidden_two, norm_two, pieces[8])
    grad_sum_low = grad_sum_two.astype(jnp.bfloat16)
    grad_down = contract_rows(activated, grad_sum_low)
    grad_activated = contract_cols(grad_sum_low, down_weight)
    normal_cdf = 0.5 * (1.0 + lax.erf(inner / math.sqrt(2.0)))
    normal_pdf = jnp.exp(-0.5 * inner * inner) / math.sqrt(2.0 * math.pi)
    grad_inner = (grad_activated * (normal_cdf + inner * normal_pdf)).astype(jnp.bfloat16)
    grad_up = contract_rows(input_one, grad_inner)
    grad_bias_up = jnp.sum(grad_inner.astype(jnp.float32), axis=0)
    grad_hidden_one = grad_sum_two + contract_cols(grad_inner, up_weight)
    grad_sum_one, grad_gain_one, grad_shift_one = norm_back(grad_hidden_one, norm_one, pieces[5])
    grad_one_low = grad_sum_one.astype(jnp.bfloat16)
    grad_out_proj = contract_rows(context, grad_one_low)
    grad_context = (
        contract_cols(grad_one_low, attention_weight[:, 3 * D :])
        .astype(jnp.bfloat16)
        .reshape(count_rows, HEADS, HD)
    )
    probs = jnp.exp(score_block(triple[:, 0], triple[:, 1], allowed) - prob_store)
    grad_value = jnp.einsum(
        "hrc,rhd->chd", probs.astype(jnp.bfloat16), grad_context, preferred_element_type=jnp.float32
    )
    grad_probs = jnp.einsum(
        "rhd,chd->hrc", grad_context, triple[:, 2], preferred_element_type=jnp.float32
    )
    grad_scores = (
        probs * (grad_probs - jnp.sum(grad_probs * probs, axis=-1, keepdims=True))
    ).astype(jnp.bfloat16)
    grad_query = jnp.einsum(
        "hrc,chd->rhd", grad_scores, triple[:, 1], preferred_element_type=jnp.float32
    ) * HD ** (-0.5)
    grad_key = jnp.einsum(
        "hrc,rhd->chd", grad_scores, triple[:, 0], preferred_element_type=jnp.float32
    ) * HD ** (-0.5)
    grad_mixed = (
        jnp.stack([grad_query, grad_key, grad_value], axis=1)
        .reshape(count_rows, 3 * D)
        .astype(jnp.bfloat16)
    )
    grad_qkv = contract_rows(input_zero, grad_mixed)
    grad_mixed_sum = jnp.sum(grad_mixed.astype(jnp.float32), axis=0)
    grad_hidden_zero = grad_sum_one + contract_cols(grad_mixed, attention_weight[:, : 3 * D])
    grad_embedded, grad_gain_zero, grad_shift_zero = norm_back(
        grad_hidden_zero, norm_zero, pieces[0]
    )
    grad_positions = jnp.zeros((PMAX, D), jnp.float32).at[position].add(grad_embedded)
    grad_attention = jnp.concatenate([grad_qkv, grad_out_proj], axis=1)
    grad_small = jnp.concatenate(
        [
            grad_positions.reshape(-1),
            grad_gain_zero,
            grad_shift_zero,
            grad_mixed_sum[:D],
            grad_mixed_sum[2 * D :],
            jnp.sum(grad_sum_one, axis=0),
            grad_gain_one,
            grad_shift_one,
            jnp.sum(grad_sum_two, axis=0),
            grad_gain_two,
            grad_shift_two,
            grad_bias_up,
        ]
    )
    return (grad_embedded, grad_attention, grad_up, grad_down, grad_head, grad_small)


def adam_update(weight, moment, second, gradient, rate, count_steps):
    moment_new = BETA_ONE * moment + (1.0 - BETA_ONE) * gradient
    second_new = BETA_TWO * second + (1.0 - BETA_TWO) * gradient * gradient
    corrected = moment_new / (1.0 - BETA_ONE**count_steps)
    scaled = second_new / (1.0 - BETA_TWO**count_steps)
    weight_new = weight - rate * (corrected / (jnp.sqrt(scaled) + ADAM_EPS) + WEIGHT_DECAY * weight)
    return (weight_new, second_new)


def on_device(
    query_ids,
    passage_ids,
    passage_lengths,
    positives,
    negatives,
    pair_mask,
    assignments,
    step_count,
    embed_table,
    embed_table_moment,
    embed_table_second,
    attention_weight,
    attention_weight_moment,
    attention_weight_second,
    up_weight,
    up_weight_moment,
    up_weight_second,
    down_weight,
    down_weight_moment,
    down_weight_second,
    head_weight,
    head_weight_moment,
    head_weight_second,
    small_params,
    small_params_moment,
    small_params_second,
):
    mask_float = pair_mask.astype(jnp.float32)
    weights = (
        lax.all_gather(embed_table.astype(jnp.bfloat16), ("grp", "psg"), axis=0, tiled=True),
        lax.all_gather(attention_weight.astype(jnp.bfloat16), ("grp", "psg"), axis=1, tiled=True),
        lax.all_gather(up_weight.astype(jnp.bfloat16), ("grp", "psg"), axis=1, tiled=True),
        lax.all_gather(down_weight.astype(jnp.bfloat16), ("grp", "psg"), axis=0, tiled=True),
        lax.all_gather(head_weight.astype(jnp.bfloat16), ("grp", "psg"), axis=0, tiled=True),
        lax.all_gather(small_params.astype(jnp.bfloat16), ("grp", "psg"), axis=0, tiled=True),
    )
    groups = lax.axis_size("psg")
    member = lax.axis_index("psg")
    group_pass = groups * PPD
    query_tokens = query_ids.reshape(-1)
    query_position = jnp.tile(jnp.arange(SEG, dtype=jnp.int32), QDEV)
    query_segment = jnp.repeat(jnp.arange(QDEV, dtype=jnp.int32), SEG)
    passage_segment, passage_position = passage_layout(passage_lengths)
    passage_segment = passage_segment[0]
    passage_position = passage_position[0]
    passage_tokens = passage_ids[0]
    query_unit, query_stored = encode_forward(weights, query_tokens, query_position, query_segment)
    passage_unit, passage_stored = encode_forward(
        weights, passage_tokens, passage_position, passage_segment
    )
    group_query = lax.all_gather(query_unit, "psg", axis=0, tiled=True)
    onehot_local = (passage_segment[:, None] == jnp.arange(PPD, dtype=jnp.int32)).astype(
        jnp.float32
    )
    weighted = jnp.exp(contract_cols(group_query, passage_unit) / TEMPER)
    totals = jnp.dot(weighted, onehot_local, precision=HIGHEST)
    local_scores = jnp.sum((TEMPER * jnp.log(totals)).reshape(groups * QDEV, SEG, PPD), axis=1)
    all_scores = lax.all_gather(local_scores, "psg", axis=1, tiled=True)
    own_scores = lax.dynamic_slice_in_dim(all_scores, member * QDEV, QDEV, 0)
    columns = jnp.arange(group_pass, dtype=jnp.int32)
    pick_positive = (positives[:, None] == columns[None, :]).astype(jnp.float32)
    pick_negative = (negatives[:, :, None] == columns[None, None, :]).astype(jnp.float32)
    pos_score = jnp.sum(own_scores * pick_positive, axis=1)
    neg_score = jnp.sum(pick_negative * own_scores[:, None, :], axis=2)
    margins = MARGIN - pos_score[:, None] + neg_score
    numerator_local = jnp.sum(mask_float * jax.nn.softplus(margins))
    numerator_total, pair_count = lax.psum((numerator_local, jnp.sum(mask_float)), ("grp", "psg"))
    pair_floor = jnp.maximum(pair_count, 1.0)
    factor = mask_float * jax.nn.sigmoid(margins) / pair_floor
    grad_own = (
        jnp.sum(factor[:, :, None] * pick_negative, axis=1)
        - jnp.sum(factor, axis=1)[:, None] * pick_positive
    )
    grad_local = lax.all_to_all(grad_own, "psg", split_axis=1, concat_axis=0, tiled=True)
    grad_tokens = jnp.broadcast_to(grad_local[:, None, :], (groups * QDEV, SEG, PPD)).reshape(
        groups * QDEV * SEG, PPD
    )
    grad_weighted = contract_cols(TEMPER * grad_tokens / totals, onehot_local)
    grad_sims = (grad_weighted * weighted / TEMPER).astype(jnp.bfloat16)
    grad_query_unit = lax.psum_scatter(
        matmul(grad_sims, passage_unit).astype(jnp.bfloat16), "psg", scatter_dimension=0, tiled=True
    ).astype(jnp.float32)
    grad_passage_unit = contract_rows(grad_sims, group_query)
    query_grads = encode_backward(weights, query_stored, grad_query_unit, query_position)
    passage_grads = encode_backward(weights, passage_stored, grad_passage_unit, passage_position)
    every_token = jnp.concatenate([query_tokens, passage_tokens])
    every_grad = jnp.concatenate([query_grads[0], passage_grads[0]], axis=0)
    grad_table = jnp.zeros((weights[0].shape[0], D), jnp.float32).at[every_token].add(every_grad)
    picks = (assignments[0][:, None] == jnp.arange(NCENT, dtype=jnp.int32)[None, :]).astype(
        jnp.bfloat16
    )
    centroid_part = contract_rows(picks, passage_unit)
    count_part = jnp.sum(picks.astype(jnp.float32), axis=0)
    reduced = (
        lax.psum_scatter(grad_table, ("grp", "psg"), scatter_dimension=0, tiled=True),
        lax.psum_scatter(
            query_grads[1] + passage_grads[1], ("grp", "psg"), scatter_dimension=1, tiled=True
        ),
        lax.psum_scatter(
            query_grads[2] + passage_grads[2], ("grp", "psg"), scatter_dimension=1, tiled=True
        ),
        lax.psum_scatter(
            query_grads[3] + passage_grads[3], ("grp", "psg"), scatter_dimension=0, tiled=True
        ),
        lax.psum_scatter(
            query_grads[4] + passage_grads[4], ("grp", "psg"), scatter_dimension=0, tiled=True
        ),
        lax.psum_scatter(
            query_grads[5] + passage_grads[5], ("grp", "psg"), scatter_dimension=0, tiled=True
        ),
        lax.psum_scatter(centroid_part, ("grp", "psg"), scatter_dimension=0, tiled=True),
        lax.psum_scatter(count_part, ("grp", "psg"), scatter_dimension=0, tiled=True),
    )
    loss = numerator_total / pair_floor
    count_steps = step_count[0].astype(jnp.float32)
    table_new, table_second_new = adam_update(
        embed_table, embed_table_moment, embed_table_second, reduced[0], RATE_TABLE, count_steps
    )
    attn_new, attn_second_new = adam_update(
        attention_weight,
        attention_weight_moment,
        attention_weight_second,
        reduced[1],
        RATE_MATRIX,
        count_steps,
    )
    up_new, up_second_new = adam_update(
        up_weight, up_weight_moment, up_weight_second, reduced[2], RATE_MATRIX, count_steps
    )
    down_new, down_second_new = adam_update(
        down_weight, down_weight_moment, down_weight_second, reduced[3], RATE_MATRIX, count_steps
    )
    head_new, head_second_new = adam_update(
        head_weight, head_weight_moment, head_weight_second, reduced[4], RATE_MATRIX, count_steps
    )
    small_new, small_second_new = adam_update(
        small_params, small_params_moment, small_params_second, reduced[5], RATE_TABLE, count_steps
    )
    return (
        loss,
        reduced[6],
        reduced[7],
        table_new,
        reduced[0],
        table_second_new,
        attn_new,
        reduced[1],
        attn_second_new,
        up_new,
        reduced[2],
        up_second_new,
        down_new,
        reduced[3],
        down_second_new,
        head_new,
        reduced[4],
        head_second_new,
        small_new,
        reduced[5],
        small_second_new,
    )


def solution(mesh):
    in_specs = (
        P(("grp", "psg"), None),
        P(("grp", "psg"), None),
        P(("grp", "psg"), None),
        P(("grp", "psg")),
        P(("grp", "psg"), None),
        P(("grp", "psg"), None),
        P(("grp", "psg"), None),
        P(),
        P(("grp", "psg"), None),
        P(("grp", "psg"), None),
        P(("grp", "psg"), None),
        P(None, ("grp", "psg")),
        P(None, ("grp", "psg")),
        P(None, ("grp", "psg")),
        P(None, ("grp", "psg")),
        P(None, ("grp", "psg")),
        P(None, ("grp", "psg")),
        P(("grp", "psg"), None),
        P(("grp", "psg"), None),
        P(("grp", "psg"), None),
        P(("grp", "psg"), None),
        P(("grp", "psg"), None),
        P(("grp", "psg"), None),
        P(("grp", "psg")),
        P(("grp", "psg")),
        P(("grp", "psg")),
    )
    out_specs = (
        P(),
        P(("grp", "psg"), None),
        P(("grp", "psg")),
        P(("grp", "psg"), None),
        P(("grp", "psg"), None),
        P(("grp", "psg"), None),
        P(None, ("grp", "psg")),
        P(None, ("grp", "psg")),
        P(None, ("grp", "psg")),
        P(None, ("grp", "psg")),
        P(None, ("grp", "psg")),
        P(None, ("grp", "psg")),
        P(("grp", "psg"), None),
        P(("grp", "psg"), None),
        P(("grp", "psg"), None),
        P(("grp", "psg"), None),
        P(("grp", "psg"), None),
        P(("grp", "psg"), None),
        P(("grp", "psg")),
        P(("grp", "psg")),
        P(("grp", "psg")),
    )
    return jax.shard_map(
        on_device, mesh=mesh, in_specs=in_specs, out_specs=out_specs, check_vma=False
    )
```

profile of v0, /device:TPU:0, one launch (start us, length us, event | category | flops | bytes accessed | tf_op | source)
XLA Modules:
  0.0 2629.0 jit_solution(18174384974968669929)
XLA Ops:
  17.1 46.4 %all_gather.29 = bf16[768,128]{1,0:T(8,128)(2,1)} all-gather(bf16[24,128]{1,0:T(8,128)(2,1)S(1)} %convert_element_type.271), channel_id=1, replica_groups=mesh['grp'=8,'psg'=4] {'grp','psg'}, dimensions={0}, use_global_device_ids=true | all-gather | bytes 202752 | tf_op jit(solution)/shard_map/all_gather | solution.py:292
  64.4 73.8 %all-reduce.8.cloned.1.call-done = bf16[59904]{0:T(1024)(128)(2,1)} async-done(((bf16[59904]{0:T(1024)(128)(2,1)}), bf16[59904]{0:T(1024)(128)(2,1)}) %all-reduce.8.cloned.1.call-update) | async-done | bytes 119824
  150.8 251.4 %all-gather.5.cloned.1.call-done = bf16[30720,768]{1,0:T(8,128)(2,1)} async-done(((bf16[960,768]{1,0:T(8,128)(2,1)}), bf16[30720,768]{1,0:T(8,128)(2,1)}) %all-gather.5.cloned.1.call-update) | async-done | bytes 47185936 | tf_op jit(solution)/shard_map/all_gather | solution.py:288
  402.2 19.0 gather_fusion.2
  427.6 40.0 %all-gather.7.cloned.1.call-done = bf16[768,3072]{0,1:T(8,128)(2,1)} async-done(((bf16[768,96]{0,1:T(8,128)(2,1)}), bf16[768,3072]{0,1:T(8,128)(2,1)}) %all-gather.7.cloned.1.call-update) | async-done | bytes 4718608 | tf_op jit(solution)/shard_map/all_gather | solution.py:289
  499.3 34.0 %all-gather.9.cloned.1.call-done = bf16[768,3072]{0,1:T(8,128)(2,1)} async-done(((bf16[768,96]{0,1:T(8,128)(2,1)}), bf16[768,3072]{0,1:T(8,128)(2,1)}) %all-gather.9.cloned.1.call-update) | async-done | bytes 4718608 | tf_op jit(solution)/shard_map/all_gather | solution.py:290
  544.6 54.5 %all-gather.11.cloned.1.call-done = bf16[3072,768]{1,0:T(8,128)(2,1)} async-done(((bf16[96,768]{1,0:T(8,128)(2,1)}), bf16[3072,768]{1,0:T(8,128)(2,1)}) %all-gather.11.cloned.1.call-update) | async-done | bytes 4718608 | tf_op jit(solution)/shard_map/all_gather | solution.py:291
  612.2 21.6 fusion
  633.8 21.0 exponential_reduce_fusion
  654.9 19.4 convolution_convert_fusion.1
  678.7 35.7 %fusion.4 = (bf16[1024,3072]{1,0:T(8,128)(2,1)}, f32[1024,3072]{1,0:T(8,128)}) fusion(f32[3072]{0:T(1024)S(1)} %copy-done.142, bf16[768,3072]{0,1:T(8,128)(2,1)S(1)} %bitcast.188, f32[1024,768]{0,1:T(8,128)S(1)} %get-tuple-element.210, f32[768]{0:T(1024)S(1)} %get-tuple-element.188, f32[768]{0:T(1024)S(1)} %get-tuple-element.184, ...), kind=kOutput, calls=%fused_computation.18 | convolution fusion | flops 5043388416 | bytes 26765312 | tf_op jit(solution)/shard_map/dot_general | solution.py:32
  744.2 40.0 %all-reduce.4 = (f32[]{:T(128)}, f32[]{:T(128)}, f32[1024]{0:T(1024)}) all-reduce(f32[]{:T(128)} %get-tuple-element.150, f32[]{:T(128)} %get-tuple-element.149, f32[1024]{0:T(1024)} %convert_reduce_fusion.2), channel_id=1, replica_groups=mesh['grp'=8,'psg'=4] {'grp','psg'}, use_global_device_ids=true, to_apply=%region_25.26 | all-reduce | flops 1026 | bytes 8208 | tf_op jit(solution)/shard_map/psum | solution.py:325
  857.7 20.8 convolution_bitcast_fusion
  878.5 34.3 %multiply_reduce_fusion = (f32[12,1024]{1,0:T(8,128)S(1)}, f32[12,1024,1024]{1,2,0:T(8,128)}) fusion(f32[12,1024,1024]{1,2,0:T(8,128)} %get-tuple-element.208, f32[12,1024]{1,0:T(8,128)S(1)} %copy-done.67, pred[1024,1024]{0,1:T(8,128)(4,1)S(1)} %copy-done.1, bf16[1024,12,64]{0,2,1:T(8,128)(2,1)S(1)} %bitcast.173, bf16[1024,3,12,64]{0,3,2,1:T(8,128)(2,1)} %bitcast.157), kind=kOutput, calls=%fused_computation.8 | convolution fusion | flops 1673515008 | bytes 104955904 | tf_op jit(solution)/shard_map/rhd,chd->hrc/dot_general | solution.py:205
  912.8 41.1 %multiply_convert_fusion = bf16[12,1024,1024]{1,2,0:T(8,128)(2,1)} fusion(f32[12,1024,1024]{1,2,0:T(8,128)} %get-tuple-element.223, f32[12,1024,1024]{1,2,0:T(8,128)} %get-tuple-element.208, f32[12,1024]{1,0:T(8,128)S(1)} %get-tuple-element.222, f32[12,1024]{1,0:T(8,128)S(1)} %copy-done.67, pred[1024,1024]{0,1:T(8,128)(4,1)S(1)} %copy-done.1), kind=kLoop, calls=%fused_computation.7 | loop fusion | flops 75497472 | bytes 126976000 | tf_op jit(solution)/shard_map/convert_element_type | solution.py:210
  953.9 13.9 multiply_bitcast_fusion
  967.8 14.3 multiply_bitcast_fusion.1
  1113.1 29.3 %broadcast_in_dim.39 = f32[30720,768]{1,0:T(8,128)} broadcast(f32[]{:T(128)} %constant.59.clone.1), dimensions={} | broadcast | bytes 94371840 | tf_op jit(solution)/shard_map/broadcast_in_dim | solution.py:346
  1142.4 167.4 %scatter_fusion = f32[30720,768]{1,0:T(8,128)} fusion(f32[30720,768]{1,0:T(8,128)} %broadcast_in_dim.39, s32[1280]{0:T(1024)S(1)} %fusion.108, f32[1280,768]{1,0:T(8,128)} %copy.239), kind=kCustom, calls=%fused_computation.4 | custom fusion | flops 983040 | bytes 11801600 | tf_op jit(solution)/shard_map/scatter-add | solution.py:346
  1317.6 96.5 %reduce-scatter.24.cloned.1.call-done = f32[96,768]{1,0:T(8,128)} async-done(((f32[3072,768]{1,0:T(8,128)}), f32[96,768]{1,0:T(8,128)}) %reduce-scatter.24.cloned.1.call-update) | async-done | bytes 294928
  1416.3 139.7 %reduce-scatter.20.cloned.1.call-done = f32[96,768]{1,0:T(8,128)} async-done(((f32[3072,768]{1,0:T(8,128)}), f32[96,768]{1,0:T(8,128)}) %reduce-scatter.20.cloned.1.call-update) | async-done | bytes 294928 | tf_op jit(solution)/shard_map/reduce_scatter | solution.py:360
  1558.2 138.9 %reduce-scatter.22.cloned.1.call-done = f32[96,768]{1,0:T(8,128)} async-done(((f32[3072,768]{1,0:T(8,128)}), f32[96,768]{1,0:T(8,128)}) %reduce-scatter.22.cloned.1.call-update) | async-done | bytes 294928
  1699.4 785.8 %reduce-scatter.18.cloned.1.call-done = f32[960,768]{1,0:T(8,128)} async-done(((f32[30720,768]{1,0:T(8,128)}), f32[960,768]{1,0:T(8,128)}) %reduce-scatter.18.cloned.1.call-update) | async-done | bytes 2949136 | tf_op jit(solution)/shard_map/reduce_scatter | solution.py:353
  2491.5 129.7 %reduce-scatter.14.cloned.1.call-done = f32[32,128]{1,0:T(8,128)} async-done(((f32[1024,128]{1,0:T(8,128)}), f32[32,128]{1,0:T(8,128)}) %reduce-scatter.14.cloned.1.call-update) | async-done | bytes 16400 | tf_op jit(solution)/shard_map/reduce_scatter | solution.py:369
  (584 shorter events, 340.6 us)
Async XLA Ops:
  7.2 131.0 %all-reduce.8.cloned.1.call-start = ((), (), s32[]{:S(2)}) async-start(), calls=%async_computation.16 | async-start | bytes 241664
  9.1 393.2 %all-gather.5.cloned.1.call-start = ((), (), s32[]{:S(2)}) async-start(), calls=%async_computation.8 | async-start | bytes 48660480 | tf_op jit(solution)/shard_map/all_gather | solution.py:288
  12.3 455.2 %all-gather.7.cloned.1.call-start = ((), (), s32[]{:S(2)}) async-start(), calls=%async_computation.9 | async-start | bytes 4866048 | tf_op jit(solution)/shard_map/all_gather | solution.py:289
  13.1 520.2 %all-gather.9.cloned.1.call-start = ((), (), s32[]{:S(2)}) async-start(), calls=%async_computation.10 | async-start | bytes 4866048 | tf_op jit(solution)/shard_map/all_gather | solution.py:290
  13.9 585.1 %all-gather.11.cloned.1.call-start = ((), (), s32[]{:S(2)}) async-start(), calls=%async_computation.11 | async-start | bytes 4866048 | tf_op jit(solution)/shard_map/all_gather | solution.py:291
  14.6 999.6 %reduce-scatter.16.cloned.1.call-start = ((), (), s32[]{:S(2)}) async-start(), calls=%async_computation.13 | async-start | bytes 327680 | tf_op jit(solution)/shard_map/reduce_scatter | solution.py:338
  63.7 430.1 %copy-start.68 = (pred[256,256]{0,1:T(8,128)(4,1)}, pred[256,256]{0,1:T(8,128)(4,1)S(1)}, u32[]{:S(2)}) copy-start(pred[256,256]{0,1:T(8,128)(4,1)S(1)} %broadcast_compare_fusion.1) | copy-start | bytes 196612
  64.4 590.4 %copy-start = (pred[1024,1024]{0,1:T(8,128)(4,1)}, pred[1024,1024]{0,1:T(8,128)(4,1)S(1)}, u32[]{:S(2)}) copy-start(pred[1024,1024]{0,1:T(8,128)(4,1)S(1)} %broadcast_compare_fusion) | copy-start | bytes 3145732
  140.4 355.6 %copy-start.24 = (bf16[256,768]{1,0:T(8,128)(2,1)}, bf16[256,768]{1,0:T(8,128)(2,1)S(1)}, u32[]{:S(2)}) copy-start(bf16[256,768]{1,0:T(8,128)(2,1)S(1)} %gather_fusion.1) | copy-start | bytes 1179652
  147.3 527.0 %copy-start.8 = (bf16[1024,768]{0,1:T(8,128)(2,1)}, bf16[1024,768]{0,1:T(8,128)(2,1)S(1)}, u32[]{:S(2)}) copy-start(bf16[1024,768]{0,1:T(8,128)(2,1)S(1)} %copy.220) | copy-start | bytes 4718596
  148.7 454.9 %copy-start.102 = (f32[768]{0:T(1024)}, f32[768]{0:T(1024)S(1)}, u32[]{:S(2)}) copy-start(f32[768]{0:T(1024)S(1)} %get-tuple-element.186) | copy-start | bytes 9220
  148.7 525.6 %copy-start.87 = (f32[768]{0:T(1024)}, f32[768]{0:T(1024)S(1)}, u32[]{:S(2)}) copy-start(f32[768]{0:T(1024)S(1)} %get-tuple-element.192) | copy-start | bytes 9220
  148.7 565.8 %copy-start.89 = (f32[768]{0:T(1024)}, f32[768]{0:T(1024)S(1)}, u32[]{:S(2)}) copy-start(f32[768]{0:T(1024)S(1)} %get-tuple-element.188) | copy-start | bytes 9220
  149.5 454.2 %copy-start.80 = (f32[768]{0:T(1024)}, f32[768]{0:T(1024)S(1)}, u32[]{:S(2)}) copy-start(f32[768]{0:T(1024)S(1)} %get-tuple-element.183) | copy-start | bytes 9220
  149.5 524.9 %copy-start.78 = (f32[768]{0:T(1024)}, f32[768]{0:T(1024)S(1)}, u32[]{:S(2)}) copy-start(f32[768]{0:T(1024)S(1)} %get-tuple-element.185) | copy-start | bytes 9220
  982.1 332.7 %all-reduce.10.cloned.1.call-start = ((), (), s32[]{:S(2)}) async-start(), calls=%async_computation.19 | async-start | bytes 483328
  1049.3 267.0 %reduce-scatter.26.cloned.1.call-start = ((), (), s32[]{:S(2)}) async-start(), calls=%async_computation.20 | async-start | bytes 405504
  1050.5 363.7 %reduce-scatter.24.cloned.1.call-start = ((), (), s32[]{:S(2)}) async-start(), calls=%async_computation.18 | async-start | bytes 9732096
  1059.9 496.1 %reduce-scatter.20.cloned.1.call-start = ((), (), s32[]{:S(2)}) async-start(), calls=%async_computation.15 | async-start | bytes 9732096 | tf_op jit(solution)/shard_map/reduce_scatter | solution.py:360
  1073.7 623.4 %reduce-scatter.22.cloned.1.call-start = ((), (), s32[]{:S(2)}) async-start(), calls=%async_computation.17 | async-start | bytes 9732096
  1101.1 1384.1 %reduce-scatter.18.cloned.1.call-start = ((), (), s32[]{:S(2)}) async-start(), calls=%async_computation.14 | async-start | bytes 97320960 | tf_op jit(solution)/shard_map/reduce_scatter | solution.py:353
  1309.9 246.2 %copy-start.64 = (f32[96,768]{1,0:T(8,128)S(1)}, f32[96,768]{1,0:T(8,128)}, u32[]{:S(2)}) copy-start(f32[96,768]{1,0:T(8,128)} %param.43) | copy-start | bytes 884740
  1309.9 1311.2 %reduce-scatter.14.cloned.1.call-start = ((), (), s32[]{:S(2)}) async-start(), calls=%async_computation.12 | async-start | bytes 540672 | tf_op jit(solution)/shard_map/reduce_scatter | solution.py:369
  1313.3 1171.9 %copy-start.23 = (f32[960,768]{1,0:T(8,128)S(1)}, f32[960,768]{1,0:T(8,128)}, u32[]{:S(2)}) copy-start(f32[960,768]{1,0:T(8,128)} %param.34) | copy-start | bytes 8847364
  (159 other events, 2182.7 us)
Sparse Core Ops, SparseCore 0:
  14.2 123.9 all-reduce.7
  141.7 260.4 all-gather.4
  405.7 61.7 all-gather.6
  470.8 62.3 all-gather.8
  536.6 62.3 all-gather.10
  982.2 18.4 reduce-scatter.15
  1049.4 122.2 all-reduce.9
  1178.0 94.9 reduce-scatter.25
  1279.5 134.5 reduce-scatter.23
  1421.5 134.5 reduce-scatter.19
  1562.5 134.5 reduce-scatter.21
  1705.1 780.0 reduce-scatter.17
  2488.0 133.0 reduce-scatter.13
where the time goes:
time: 2650 us; the launch traced here: 2630 us
  waiting for transfers between devices  1740 us (66%)
  matrix products  326 us (12%)
  other arithmetic  309 us (12%)
  local copies, waits for them, and re-layouts  123 us (5%)
  blocking collectives  106 us (4%)
    reduce_scatter x1, waiting for transfers between devices, on_device(): lax.psum_scatter(grad_table, ('grp', 'psg'), scatter_dimension=0, tiled=T...  786 us
    unnamed x18, waiting for transfers between devices  309 us
    all_gather x1, waiting for transfers between devices, on_device(): lax.all_gather(embed_table.astype(jnp.bfloat16), ('grp', 'psg'), axis=0,...  251 us
    scatter-add x1, other arithmetic, on_device(): jnp.zeros((weights[0].shape[0], D), jnp.float32).at[every_token]  167 us
    reduce_scatter x1, waiting for transfers between devices, on_device(): lax.psum_scatter(query_grads[3] + passage_grads[3], ('grp', 'psg'), scatt...  140 us
    reduce_scatter x1, waiting for transfers between devices, on_device(): lax.psum_scatter(centroid_part, ('grp', 'psg'), scatter_dimension=0, tile...  130 us
    dot_general x11, matrix products, matmul(): return jnp.dot(lhs_mat, rhs_mat, preferred_element_type=jnp.float32)  78.1 us
    dot_general x12, matrix products, contract_cols(): lax.dot_general(lhs_mat, rhs_mat, (((1,), (1,)), ((), ())), preferred_ele...  61 us
  transfers between devices with their start and end apart: 13, of which 10 were waited for; matrix products, arithmetic and copies ran while one was open for 15% of the time, Pallas kernels for 0%

commit v1 on v0

v1 whole, which is shorter than its diff:
```python
import math

import jax
import jax.numpy as jnp
from jax import lax
from jax.experimental import pallas as pl
from jax.experimental.pallas import tpu as pltpu
from jax.sharding import PartitionSpec as P

D = 768
HEADS = 12
HD = 64
SEG = 32
PMAX = 64
ROW = 1024
PPD = 32
QDEV = 8
NCENT = 1024
DC = 128
BLK = 128
WIN = 256
ALL = ("grp", "psg")
BF = jnp.bfloat16
F32 = jnp.float32
MARK = 1e30


TEMPER = 0.2
MARGIN = 1.0
NORM_EPS = 1e-06
BETA_ONE = 0.9
BETA_TWO = 0.999
ADAM_EPS = 1e-08
WEIGHT_DECAY = 0.01
RATE_MATRIX = 0.01
RATE_TABLE = 0.1


def matmul(lhs_mat, rhs_mat):
    return jnp.dot(lhs_mat, rhs_mat, preferred_element_type=jnp.float32)


def contract_rows(lhs_mat, rhs_mat):
    return lax.dot_general(
        lhs_mat, rhs_mat, (((0,), (0,)), ((), ())), preferred_element_type=jnp.float32
    )


def contract_cols(lhs_mat, rhs_mat):
    return lax.dot_general(
        lhs_mat, rhs_mat, (((1,), (1,)), ((), ())), preferred_element_type=jnp.float32
    )


def layer_norm(values, scale_gain, shift_bias):
    average = jnp.mean(values, axis=-1, keepdims=True)
    centered = values - average
    inverse = lax.rsqrt(jnp.mean(centered * centered, axis=-1, keepdims=True) + NORM_EPS)
    normed = centered * inverse
    return (normed * (1.0 + scale_gain) + shift_bias, (normed, inverse))


def norm_back(upstream, stored, scale_gain):
    normed, inverse = stored
    scaled = upstream * (1.0 + scale_gain)
    back = inverse * (
        scaled
        - jnp.mean(scaled, axis=-1, keepdims=True)
        - normed * jnp.mean(scaled * normed, axis=-1, keepdims=True)
    )
    return (back, jnp.sum(upstream * normed, axis=0), jnp.sum(upstream, axis=0))


def starts_of(lengths):
    order = jnp.arange(PPD, dtype=jnp.int32)
    before = (order[:, None] > order[None, :]).astype(jnp.int32)
    return jnp.sum(before * lengths[..., None, :], axis=-1)


def layout_of(lengths):
    starts = starts_of(lengths)
    place = jnp.arange(ROW, dtype=jnp.int32)
    above = (place[:, None] >= starts[..., None, :]).astype(jnp.int32)
    segment = jnp.sum(above, axis=-1) - 1
    begin = jnp.max(above * starts[..., None, :], axis=-1)
    return segment, place - begin


def one_hot(index, depth):
    return (index[..., None] == jnp.arange(depth, dtype=jnp.int32)).astype(BF)


def split_two(values):
    high = lax.reduce_precision(values, 8, 7)
    return high.astype(BF), (values - high).astype(BF)


def split_three(values):
    high = lax.reduce_precision(values, 8, 7)
    middle = lax.reduce_precision(values - high, 8, 7)
    return high.astype(BF), middle.astype(BF), (values - high - middle).astype(BF)


def window_start(block, count):
    return min(max(block * BLK - (WIN - BLK) // 2, 0), count - WIN)


def attn_forward_kernel(count, segc_ref, segw_ref, z_ref, o_ref, lse_ref):
    block = pl.program_id(0)
    row = pl.multiple_of(block * BLK, BLK)
    first = pl.multiple_of(jnp.clip(row - (WIN - BLK) // 2, 0, count - WIN), 64)
    allowed = segc_ref[...] == segw_ref[0]
    lane = lax.broadcasted_iota(jnp.int32, (BLK, 2 * HD), 1)
    lane_head = lax.broadcasted_iota(jnp.int32, (BLK, 128), 1)
    kept = jnp.zeros((BLK, 128), F32)
    for pair in range(HEADS // 2):
        at = pair * 2 * HD
        query = z_ref[pl.ds(row, BLK), at : at + 2 * HD] * BF(HD ** (-0.5))
        key = z_ref[pl.ds(first, WIN), D + at : D + at + 2 * HD]
        value = z_ref[pl.ds(first, WIN), 2 * D + at : 2 * D + at + 2 * HD]
        parts = []
        for half in range(2):
            mine = (lane >= half * HD) & (lane < (half + 1) * HD)
            scores = contract_cols(jnp.where(mine, query, BF(0)), key)
            scores = jnp.where(allowed, scores, -1000000000.0)
            top = jnp.max(scores, axis=-1, keepdims=True)
            weight = jnp.exp(scores - top)
            total = jnp.sum(weight, axis=-1, keepdims=True)
            probs = (weight * (1.0 / total)).astype(BF)
            parts.append(matmul(probs, value))
            kept = jnp.where(lane_head == 2 * pair + half, top + jnp.log(total), kept)
        o_ref[:, at : at + 2 * HD] = jnp.where(lane < HD, parts[0], parts[1]).astype(BF)
    lse_ref[...] = kept


def attn_backward_kernel(
    count, blocks, segc_ref, segw_ref, z_ref, do_ref, lse_ref, dz_ref, dk_ref, dv_ref
):
    block = pl.program_id(0)
    row = pl.multiple_of(block * BLK, BLK)
    first = pl.multiple_of(jnp.clip(row - (WIN - BLK) // 2, 0, count - WIN), 64)

    @pl.when(block == 0)
    def _():
        dk_ref[...] = jnp.zeros_like(dk_ref)
        dv_ref[...] = jnp.zeros_like(dv_ref)

    allowed = segc_ref[...] == segw_ref[0]
    lane = lax.broadcasted_iota(jnp.int32, (BLK, 2 * HD), 1)
    kept = lse_ref[...]
    for pair in range(HEADS // 2):
        at = pair * 2 * HD
        query = z_ref[pl.ds(row, BLK), at : at + 2 * HD] * BF(HD ** (-0.5))
        key = z_ref[pl.ds(first, WIN), D + at : D + at + 2 * HD]
        value = z_ref[pl.ds(first, WIN), 2 * D + at : 2 * D + at + 2 * HD]
        upstream = do_ref[:, at : at + 2 * HD]
        grad_query = []
        grad_key = jnp.zeros((WIN, 2 * HD), F32)
        grad_value = jnp.zeros((WIN, 2 * HD), F32)
        for half in range(2):
            mine = (lane >= half * HD) & (lane < (half + 1) * HD)
            query_own = jnp.where(mine, query, BF(0))
            up_own = jnp.where(mine, upstream, BF(0))
            scores = jnp.where(allowed, contract_cols(query_own, key), -1000000000.0)
            probs = jnp.exp(scores - kept[:, 2 * pair + half : 2 * pair + half + 1])
            grad_probs = contract_cols(up_own, value)
            grad_value = grad_value + contract_rows(probs.astype(BF), up_own)
            inner = jnp.sum(grad_probs * probs, axis=-1, keepdims=True)
            grad_scores = (probs * (grad_probs - inner)).astype(BF)
            grad_query.append(matmul(grad_scores, key))
            grad_key = grad_key + contract_rows(grad_scores, query_own)
        own = jnp.where(lane < HD, grad_query[0], grad_query[1]) * HD ** (-0.5)
        dz_ref[pl.ds(row, BLK), at : at + 2 * HD] = own.astype(BF)
        dk_ref[pl.ds(first, WIN), at : at + 2 * HD] += grad_key
        dv_ref[pl.ds(first, WIN), at : at + 2 * HD] += grad_value

    @pl.when(block == blocks - 1)
    def _():
        dz_ref[:, D : 2 * D] = dk_ref[...].astype(BF)
        dz_ref[:, 2 * D :] = dv_ref[...].astype(BF)


def attention_specs(count):
    return [
        pl.BlockSpec((BLK, 1), lambda i: (i, 0)),
        pl.BlockSpec((1, 1, WIN), lambda i: (i, 0, 0)),
        pl.BlockSpec((count, 3 * D), lambda i: (0, 0)),
    ]


def attention_forward(segment_column, segment_windows, mixed):
    count = mixed.shape[0]
    blocks = count // BLK
    return pl.pallas_call(
        lambda *refs: attn_forward_kernel(count, *refs),
        grid=(blocks,),
        in_specs=attention_specs(count),
        out_specs=[
            pl.BlockSpec((BLK, D), lambda i: (i, 0)),
            pl.BlockSpec((BLK, 128), lambda i: (i, 0)),
        ],
        out_shape=[
            jax.ShapeDtypeStruct((count, D), BF),
            jax.ShapeDtypeStruct((count, 128), F32),
        ],
        compiler_params=pltpu.CompilerParams(vmem_limit_bytes=40 * 2**20),
        cost_estimate=pl.CostEstimate(
            flops=4 * count * WIN * 128 * HEADS, bytes_accessed=12000000, transcendentals=0
        ),
    )(segment_column, segment_windows, mixed)


def attention_backward(segment_column, segment_windows, mixed, upstream, kept):
    count = mixed.shape[0]
    blocks = count // BLK
    return pl.pallas_call(
        lambda *refs: attn_backward_kernel(count, blocks, *refs),
        grid=(blocks,),
        in_specs=attention_specs(count)
        + [
            pl.BlockSpec((BLK, D), lambda i: (i, 0)),
            pl.BlockSpec((BLK, 128), lambda i: (i, 0)),
        ],
        out_specs=pl.BlockSpec((count, 3 * D), lambda i: (0, 0)),
        out_shape=jax.ShapeDtypeStruct((count, 3 * D), BF),
        scratch_shapes=[pltpu.VMEM((count, D), F32), pltpu.VMEM((count, D), F32)],
        compiler_params=pltpu.CompilerParams(vmem_limit_bytes=56 * 2**20),
        cost_estimate=pl.CostEstimate(
            flops=10 * count * WIN * 128 * HEADS, bytes_accessed=18000000, transcendentals=0
        ),
    )(segment_column, segment_windows, mixed, upstream, kept)


def swap_half(parts, axis_name, bit, axis):
    size = lax.axis_size(axis_name)
    mine = (lax.axis_index(axis_name) >> bit) & 1
    pairs = [(i, i ^ (1 << bit)) for i in range(size)]
    sent = lax.dynamic_index_in_dim(parts, 1 - mine, axis, keepdims=False).astype(BF)
    held = lax.dynamic_index_in_dim(parts, mine, axis, keepdims=False)
    return held + lax.ppermute(sent, axis_name, pairs).astype(F32)


def reduce_rows(gradient, group_first):
    group_bits = lax.axis_size("grp").bit_length() - 1
    member_bits = lax.axis_size("psg").bit_length() - 1
    rows = gradient.shape[0] // (1 << (group_bits + member_bits))
    shape = (2,) * (group_bits + member_bits) + (rows, gradient.shape[1])
    parts = gradient.reshape(shape)
    names = [("grp", b) for b in reversed(range(group_bits))] + [
        ("psg", b) for b in reversed(range(member_bits))
    ]
    order = [("psg", 0)]
    if group_first:
        order += [("grp", 0)] + [("psg", b) for b in range(1, member_bits)]
        order += [("grp", b) for b in range(1, group_bits)]
    else:
        order += [("psg", b) for b in range(1, member_bits)]
        order += [("grp", b) for b in range(group_bits)]
    for step in order:
        at = names.index(step)
        parts = swap_half(parts, step[0], step[1], at)
        names.pop(at)
    return parts


def adam_update(weight, moment, second, gradient, rate, count_steps):
    moment_new = BETA_ONE * moment + (1.0 - BETA_ONE) * gradient
    second_new = BETA_TWO * second + (1.0 - BETA_TWO) * gradient * gradient
    corrected = moment_new / (1.0 - BETA_ONE**count_steps)
    scaled = second_new / (1.0 - BETA_TWO**count_steps)
    weight_new = weight - rate * (corrected / (jnp.sqrt(scaled) + ADAM_EPS) + WEIGHT_DECAY * weight)
    return (weight_new, second_new)


def on_device(
    query_ids,
    passage_ids,
    passage_lengths,
    positives,
    negatives,
    pair_mask,
    assignments,
    step_count,
    embed_table,
    embed_table_moment,
    embed_table_second,
    attention_weight,
    attention_weight_moment,
    attention_weight_second,
    up_weight,
    up_weight_moment,
    up_weight_second,
    down_weight,
    down_weight_moment,
    down_weight_second,
    head_weight,
    head_weight_moment,
    head_weight_second,
    small_params,
    small_params_moment,
    small_params_second,
):
    devices = lax.axis_size("grp") * lax.axis_size("psg")
    members = lax.axis_size("psg")
    member = lax.axis_index("psg")
    group = lax.axis_index("grp")
    shard_rows = embed_table.shape[0]
    queries = query_ids.shape[0]
    negative_count = negatives.shape[1]
    query_rows = queries * SEG
    count = ROW + query_rows
    capacity = 16 * ((count // devices + 8 + 15) // 16)
    small_size = small_params.shape[0]
    head_rows = head_weight.shape[0]
    mask_float = pair_mask.astype(F32)

    tokens = jnp.concatenate([passage_ids.reshape(-1), query_ids.reshape(-1)])
    passage_segment, passage_position = layout_of(passage_lengths[0])
    query_place = jnp.arange(query_rows, dtype=jnp.int32)
    segment = jnp.concatenate([passage_segment, PPD + query_place // SEG])
    position = jnp.concatenate([passage_position, query_place % SEG])
    segment_column = segment[:, None]
    segment_windows = jnp.stack(
        [
            segment[window_start(i, count) : window_start(i, count) + WIN][None]
            for i in range(count // BLK)
        ]
    )

    attn_rows = lax.all_gather(attention_weight.T.astype(BF), ALL, axis=0, tiled=True)
    up_rows = lax.all_gather(up_weight.T.astype(BF), ALL, axis=0, tiled=True)
    down_rows = lax.all_gather(down_weight.astype(BF), ALL, axis=0, tiled=True)

    owner = tokens // shard_rows
    local_row = tokens - owner * shard_rows
    owner_hot = one_hot(owner, devices)
    row_hot = one_hot(local_row, shard_rows)
    needed = jnp.minimum(contract_rows(owner_hot, row_hot), 1.0).astype(BF)
    spread = lambda v: jnp.broadcast_to(v.reshape(1, -1).astype(BF), (devices, v.size))
    payload = jnp.concatenate(
        [
            needed,
            spread(small_params),
            spread(head_weight),
            spread(passage_lengths),
            spread(jnp.sum(mask_float)),
        ],
        axis=1,
    )
    width = payload.shape[1]
    payload = jnp.pad(payload, ((0, 0), (0, -width % 128)))
    arrived = lax.all_to_all(payload, ALL, split_axis=0, concat_axis=0, tiled=True)
    cut = [0, shard_rows, small_size, head_rows * DC, PPD, 1]
    for i in range(1, len(cut)):
        cut[i] += cut[i - 1]
    asked, small_all, head_all, lengths_all, pairs_all = (
        arrived[:, cut[i] : cut[i + 1]] for i in range(5)
    )
    small_all = small_all.reshape(-1)
    head_full = head_all.reshape(D, DC)
    pair_floor = jnp.maximum(jnp.sum(pairs_all.astype(F32)), 1.0)
    place_row = jnp.arange(shard_rows, dtype=jnp.int32)
    earlier = (place_row[:, None] < place_row[None, :]).astype(BF)
    asked_rank = matmul(asked, earlier)
    slots = jnp.arange(capacity, dtype=jnp.int32).astype(F32)
    picked = (
        ((asked_rank[:, None, :] == slots[None, :, None]) & (asked[:, None, :] > 0))
        .astype(BF)
        .reshape(devices * capacity, shard_rows)
    )
    packed = matmul(picked, embed_table.astype(BF)).astype(BF).reshape(devices, capacity, D)
    too_many = jnp.max(jnp.sum(asked.astype(F32), axis=1)) > capacity
    last_slot = (jnp.arange(capacity) == capacity - 1)[None, :, None]
    packed = jnp.where(too_many & last_slot, BF(MARK), packed)
    packed = lax.all_to_all(packed, ALL, split_axis=0, concat_axis=0, tiled=True)
    overflow = jnp.max(packed[:, capacity - 1, :].astype(F32)) > 0.5 * MARK
    packed = packed.reshape(devices * capacity, D)
    needed_rank = jnp.minimum(matmul(needed, earlier), 255.0)
    token_rank = jnp.sum(matmul(owner_hot, needed_rank.astype(BF)) * row_hot.astype(F32), axis=1)
    slot = owner * capacity + jnp.minimum(token_rank.astype(jnp.int32), capacity - 1)
    slot_hot = one_hot(slot, devices * capacity)
    looked_up = lax.cond(
        overflow,
        lambda: lax.all_gather(embed_table.astype(BF), ALL, axis=0, tiled=True)[tokens].astype(F32),
        lambda: matmul(slot_hot, packed),
    )

    positions = small_all[: PMAX * D].reshape(PMAX, D)
    remainder = small_all[PMAX * D :].astype(F32)
    pieces = [remainder[i * D : (i + 1) * D] for i in range(10)]
    bias_up = remainder[10 * D :]
    position_hot = one_hot(position, PMAX)
    embedded = looked_up + matmul(position_hot, positions)
    hidden_zero, norm_zero = layer_norm(embedded, pieces[0], pieces[1])
    input_zero = hidden_zero.astype(BF)
    bias_mixed = jnp.concatenate([pieces[2], jnp.zeros((D,), F32), pieces[3]])
    mixed = (contract_cols(input_zero, attn_rows[: 3 * D]) + bias_mixed).astype(BF)
    context, kept = attention_forward(segment_column, segment_windows, mixed)
    hidden_one, norm_one = layer_norm(
        hidden_zero + contract_cols(context, attn_rows[3 * D :]) + pieces[4], pieces[5], pieces[6]
    )
    input_one = hidden_one.astype(BF)
    inner = contract_cols(input_one, up_rows) + bias_up
    activated = jax.nn.gelu(inner, approximate=False).astype(BF)
    hidden_two, norm_two = layer_norm(
        hidden_one + matmul(activated, down_rows) + pieces[7], pieces[8], pieces[9]
    )
    input_two = hidden_two.astype(BF)
    projected = matmul(input_two, head_full)
    scale_inverse = lax.rsqrt(jnp.sum(projected * projected, axis=-1, keepdims=True) + NORM_EPS)
    unit = projected * scale_inverse
    unit_low = unit.astype(BF)

    units = lax.all_gather(unit_low, "psg", axis=0)
    group_passage = units[:, :ROW]
    group_query = units[:, ROW:].reshape(members * query_rows, DC)
    own_query = unit_low[ROW:]
    own_passage = unit_low[:ROW]
    group_lengths = lax.dynamic_slice_in_dim(lengths_all, group * members, members, 0)
    group_segment, _ = layout_of(group_lengths.astype(jnp.int32))
    group_hot = one_hot(group_segment, PPD)
    passage_hot = one_hot(passage_segment, PPD)

    weighted_own = jnp.exp(
        jnp.einsum("qd,mtd->mqt", own_query, group_passage, preferred_element_type=F32) / TEMPER
    )
    sum_own = lambda part: jnp.einsum(
        "mqt,mtp->mqp", part, group_hot, preferred_element_type=F32
    )
    high, low = split_two(weighted_own)
    totals_own = sum_own(high) + sum_own(low)
    weighted = jnp.exp(contract_cols(group_query, own_passage) / TEMPER)
    high, low = split_two(weighted)
    totals = matmul(high, passage_hot) + matmul(low, passage_hot)
    own_scores = jnp.sum(
        (TEMPER * jnp.log(totals_own)).reshape(members, queries, SEG, PPD), axis=2
    )
    own_scores = own_scores.transpose(1, 0, 2).reshape(queries, members * PPD)
    columns = jnp.arange(members * PPD, dtype=jnp.int32)
    pick_positive = (positives[:, None] == columns[None, :]).astype(F32)
    pick_negative = (negatives[:, :, None] == columns[None, None, :]).astype(F32)
    pos_score = jnp.sum(own_scores * pick_positive, axis=1)
    neg_score = jnp.sum(pick_negative * own_scores[:, None, :], axis=2)
    margins = MARGIN - pos_score[:, None] + neg_score
    numerator = jnp.sum(mask_float * jax.nn.softplus(margins))
    factor = mask_float * jax.nn.sigmoid(margins) / pair_floor
    grad_own = (
        jnp.sum(factor[:, :, None] * pick_negative, axis=1)
        - jnp.sum(factor, axis=1)[:, None] * pick_positive
    )
    grad_group = lax.all_gather(grad_own, "psg", axis=0, tiled=True)
    grad_local = lax.dynamic_slice_in_dim(grad_group, member * PPD, PPD, 1)

    grad_own_split = grad_own.reshape(queries, 1, members, PPD).transpose(2, 0, 1, 3)
    ratio_own = (
        (TEMPER * grad_own_split) / totals_own.reshape(members, queries, SEG, PPD)
    ).reshape(members, query_rows, PPD)
    spread_own = jnp.einsum(
        "mqp,mtp->mqt", ratio_own.astype(BF), group_hot, preferred_element_type=F32
    )
    sims_own = (spread_own * weighted_own / TEMPER).astype(BF)
    grad_unit_query = jnp.einsum(
        "mqt,mtd->qd", sims_own, group_passage, preferred_element_type=F32
    )
    ratio = (
        (TEMPER * grad_local[:, None, :]) / totals.reshape(members * queries, SEG, PPD)
    ).reshape(members * query_rows, PPD)
    sims = (contract_cols(ratio.astype(BF), passage_hot) * weighted / TEMPER).astype(BF)
    grad_unit_passage = contract_rows(sims, group_query)
    grad_unit = jnp.concatenate([grad_unit_passage, grad_unit_query])

    grad_proj = (
        (grad_unit - unit * jnp.sum(grad_unit * unit, axis=-1, keepdims=True)) * scale_inverse
    ).astype(BF)
    grad_head = contract_rows(input_two, grad_proj)
    picks = one_hot(assignments[0], NCENT)
    centroid_part = contract_rows(picks, own_passage)
    count_part = jnp.sum(picks.astype(F32), axis=0)
    count_high, count_low = split_two(count_part)
    early = jnp.concatenate(
        [
            centroid_part.astype(BF).reshape(devices, -1),
            grad_head.astype(BF).reshape(devices, -1),
            count_high.reshape(devices, -1),
            count_low.reshape(devices, -1),
        ]
        + [spread(v) for v in split_three(numerator)],
        axis=1,
    )
    early_width = early.shape[1]
    early = jnp.pad(early, ((0, 0), (0, -early_width % 128)))
    early = lax.all_to_all(early, ALL, split_axis=0, concat_axis=0, tiled=True)
    early = jnp.sum(early.astype(F32), axis=0)
    cent_rows = NCENT // devices
    at = cent_rows * DC
    centroid_sums = early[:at].reshape(cent_rows, DC)
    head_reduced = early[at : at + head_rows * DC].reshape(head_rows, DC)
    at += head_rows * DC
    centroid_counts = early[at : at + cent_rows] + early[at + cent_rows : at + 2 * cent_rows]
    at += 2 * cent_rows
    loss = (early[at] + early[at + 1] + early[at + 2]) / pair_floor

    grad_hidden_two = contract_cols(grad_proj, head_full)
    grad_sum_two, grad_gain_two, grad_shift_two = norm_back(grad_hidden_two, norm_two, pieces[8])
    grad_two_low = grad_sum_two.astype(BF)
    down_reduced = reduce_rows(contract_rows(activated, grad_two_low), False)
    grad_activated = contract_cols(grad_two_low, down_rows)
    normal_cdf = 0.5 * (1.0 + lax.erf(inner / math.sqrt(2.0)))
    normal_pdf = jnp.exp(-0.5 * inner * inner) / math.sqrt(2.0 * math.pi)
    grad_inner = (grad_activated * (normal_cdf + inner * normal_pdf)).astype(BF)
    up_reduced = reduce_rows(contract_rows(grad_inner, input_one), True)
    grad_bias_up = jnp.sum(grad_inner.astype(F32), axis=0)
    grad_hidden_one = grad_sum_two + matmul(grad_inner, up_rows)
    grad_sum_one, grad_gain_one, grad_shift_one = norm_back(grad_hidden_one, norm_one, pieces[5])
    grad_one_low = grad_sum_one.astype(BF)
    grad_out_rows = contract_rows(grad_one_low, context)
    grad_context = matmul(grad_one_low, attn_rows[3 * D :]).astype(BF)
    grad_mixed = attention_backward(segment_column, segment_windows, mixed, grad_context, kept)
    grad_mixed_sum = jnp.sum(grad_mixed.astype(F32), axis=0)
    grad_hidden_zero = grad_sum_one + matmul(grad_mixed, attn_rows[: 3 * D])
    grad_embedded, grad_gain_zero, grad_shift_zero = norm_back(
        grad_hidden_zero, norm_zero, pieces[0]
    )
    grad_qkv_rows = contract_rows(grad_mixed, input_zero)
    attn_reduced = reduce_rows(jnp.concatenate([grad_qkv_rows, grad_out_rows], axis=0), False)

    grad_low = grad_embedded.astype(BF)
    grad_positions = contract_rows(position_hot, grad_low)
    grad_slots = contract_rows(slot_hot, grad_low).astype(BF).reshape(devices, capacity, D)
    grad_slots = lax.all_to_all(grad_slots, ALL, split_axis=0, concat_axis=0, tiled=True)

    def whole_table():
        table = jnp.zeros((shard_rows * devices, D), F32).at[tokens].add(grad_embedded)
        return lax.psum_scatter(table, ALL, scatter_dimension=0, tiled=True)

    table_reduced = lax.cond(
        overflow,
        whole_table,
        lambda: contract_rows(picked, grad_slots.reshape(devices * capacity, D)),
    )
    grad_small = jnp.concatenate(
        [
            grad_positions.reshape(-1),
            grad_gain_zero,
            grad_shift_zero,
            grad_mixed_sum[:D],
            grad_mixed_sum[2 * D :],
            jnp.sum(grad_sum_one, axis=0),
            grad_gain_one,
            grad_shift_one,
            jnp.sum(grad_sum_two, axis=0),
            grad_gain_two,
            grad_shift_two,
            grad_bias_up,
        ]
    ).reshape(devices, small_size)
    grad_small = jnp.pad(grad_small, ((0, 0), (0, -small_size % 128)))
    grad_small = lax.all_to_all(grad_small, ALL, split_axis=0, concat_axis=0, tiled=True)
    small_reduced = jnp.sum(grad_small, axis=0)[:small_size]

    count_steps = step_count[0].astype(F32)
    attn_reduced = attn_reduced.T
    up_reduced = up_reduced.T
    table_new, table_second_new = adam_update(
        embed_table, embed_table_moment, embed_table_second, table_reduced, RATE_TABLE, count_steps
    )
    attn_new, attn_second_new = adam_update(
        attention_weight,
        attention_weight_moment,
        attention_weight_second,
        attn_reduced,
        RATE_MATRIX,
        count_steps,
    )
    up_new, up_second_new = adam_update(
        up_weight, up_weight_moment, up_weight_second, up_reduced, RATE_MATRIX, count_steps
    )
    down_new, down_second_new = adam_update(
        down_weight, down_weight_moment, down_weight_second, down_reduced, RATE_MATRIX, count_steps
    )
    head_new, head_second_new = adam_update(
        head_weight, head_weight_moment, head_weight_second, head_reduced, RATE_MATRIX, count_steps
    )
    small_new, small_second_new = adam_update(
        small_params, small_params_moment, small_params_second, small_reduced, RATE_TABLE, count_steps
    )
    return (
        loss,
        centroid_sums,
        centroid_counts,
        table_new,
        table_reduced,
        table_second_new,
        attn_new,
        attn_reduced,
        attn_second_new,
        up_new,
        up_reduced,
        up_second_new,
        down_new,
        down_reduced,
        down_second_new,
        head_new,
        head_reduced,
        head_second_new,
        small_new,
        small_reduced,
        small_second_new,
    )


def solution(mesh):
    in_specs = (
        P(("grp", "psg"), None),
        P(("grp", "psg"), None),
        P(("grp", "psg"), None),
        P(("grp", "psg")),
        P(("grp", "psg"), None),
        P(("grp", "psg"), None),
        P(("grp", "psg"), None),
        P(),
        P(("grp", "psg"), None),
        P(("grp", "psg"), None),
        P(("grp", "psg"), None),
        P(None, ("grp", "psg")),
        P(None, ("grp", "psg")),
        P(None, ("grp", "psg")),
        P(None, ("grp", "psg")),
        P(None, ("grp", "psg")),
        P(None, ("grp", "psg")),
        P(("grp", "psg"), None),
        P(("grp", "psg"), None),
        P(("grp", "psg"), None),
        P(("grp", "psg"), None),
        P(("grp", "psg"), None),
        P(("grp", "psg"), None),
        P(("grp", "psg")),
        P(("grp", "psg")),
        P(("grp", "psg")),
    )
    out_specs = (
        P(),
        P(("grp", "psg"), None),
        P(("grp", "psg")),
        P(("grp", "psg"), None),
        P(("grp", "psg"), None),
        P(("grp", "psg"), None),
        P(None, ("grp", "psg")),
        P(None, ("grp", "psg")),
        P(None, ("grp", "psg")),
        P(None, ("grp", "psg")),
        P(None, ("grp", "psg")),
        P(None, ("grp", "psg")),
        P(("grp", "psg"), None),
        P(("grp", "psg"), None),
        P(("grp", "psg"), None),
        P(("grp", "psg"), None),
        P(("grp", "psg"), None),
        P(("grp", "psg"), None),
        P(("grp", "psg")),
        P(("grp", "psg")),
        P(("grp", "psg")),
    )
    return jax.shard_map(
        on_device, mesh=mesh, in_specs=in_specs, out_specs=out_specs, check_vma=False
    )
```

time: 2650 us -> 753 us (0.28)
  waiting for transfers between devices: 1740 us -> 228 us
  other arithmetic: 309 us -> 85.8 us
  matrix products: 326 us -> 216 us
  blocking collectives: 106 us -> 5.34 us
  Pallas kernels: 0 us -> 50.3 us
  starting transfers between devices: 0.92 us -> 47.8 us
  local copies, waits for them, and re-layouts: 123 us -> 80.2 us
    reduce_scatter x4 -> x0, waiting for transfers between devices: 1060 us -> none  [the longest x1 786 us: on_device(): lax.psum_scatter(grad_table, ('grp', 'psg'), scatter_dimension=0, tiled=T...]
    unnamed x18 -> x4, waiting for transfers between devices: 309 us -> 0.57 us
    all_gather x4, waiting for transfers between devices: 380 us -> 101 us  [the longest x1 49.5 us: on_device(): lax.all_gather(attention_weight.T.astype(BF), ALL, axis=0, tiled=True)]
    scatter-add x3 -> x0, other arithmetic: 179 us -> none  [the longest x1 167 us: on_device(): jnp.zeros((weights[0].shape[0], D), jnp.float32).at[every_token]]
    dot_general x13 -> x4, matrix products: 135 us -> 8.26 us  [the longest x1 4.07 us: on_device(): jnp.einsum('mqt,mtd->qd', sims_own, group_passage, preferred_element_type...]
    all_to_all x0 -> x5, waiting for transfers between devices: none -> 68.6 us  [the longest x1 48.9 us: on_device(): lax.all_to_all(packed, ALL, split_axis=0, concat_axis=0, tiled=True)]
    ppermute x0 -> x15, waiting for transfers between devices: none -> 57.7 us  [swap_half(): return held + lax.ppermute(sent, axis_name, pairs).astype(F32)]
    all_gather x3 -> x1, blocking collectives: 57.9 us -> 5.34 us  [on_device(): grad_group = lax.all_gather(grad_own, 'psg', axis=0, tiled=True)]
  transfers between devices with their start and end apart: 13 -> 24, of which waited for: 10 -> 12; matrix products, arithmetic and copies ran while one was open for 15% -> 23% of each run, Pallas kernels for 0% -> 2%
where the time goes in v1:
time: 753 us; the launch traced here: 742 us
  waiting for transfers between devices  228 us (30%)
  matrix products  216 us (29%)
  other arithmetic  85.8 us (11%)
  local copies, waits for them, and re-layouts  80.2 us (11%)
  Pallas kernels  50.3 us (7%)
  starting transfers between devices  47.8 us (6%)
  between operations  28.7 us (4%)
    dot_general x6, matrix products, contract_cols(): lax.dot_general(lhs_mat, rhs_mat, (((1,), (1,)), ((), ())), preferred_ele...  91 us
    dot_general x12, matrix products, matmul(): return jnp.dot(lhs_mat, rhs_mat, preferred_element_type=jnp.float32)  58.9 us
    ppermute x15, waiting for transfers between devices, swap_half(): return held + lax.ppermute(sent, axis_name, pairs).astype(F32)  57.7 us
    dot_general x11, matrix products, contract_rows(): lax.dot_general(lhs_mat, rhs_mat, (((0,), (0,)), ((), ())), preferred_ele...  57.4 us
    all_gather x1, waiting for transfers between devices, on_device(): lax.all_gather(attention_weight.T.astype(BF), ALL, axis=0, tiled=True)  49.5 us
    all_to_all x1, waiting for transfers between devices, on_device(): lax.all_to_all(packed, ALL, split_axis=0, concat_axis=0, tiled=True)  48.9 us
    all_gather x1, waiting for transfers between devices, on_device(): up_rows = lax.all_gather(up_weight.T.astype(BF), ALL, axis=0, tiled=True)  36.9 us
    pallas_call x1, Pallas kernels, attention_backward(): pl.pallas_call(lambda *refs: attn_backward_kernel(count, blocks, *refs),...  36.3 us
  transfers between devices with their start and end apart: 24, of which 12 were waited for; matrix products, arithmetic and copies ran while one was open for 23% of the time, Pallas kernels for 2%

profile of v1, /device:TPU:0, one launch (start us, length us, event | category | flops | bytes accessed | tf_op | source)
XLA Modules:
  0.0 741.6 jit_solution(2629913627773756560)
XLA Ops:
  17.7 7.3 all-to-all-start
  25.1 13.1 %all-to-all-done = bf16[32,2,3008]{2,1,0:T(2,128)(2,1)S(1)} async-done(((bf16[32,2,3008]{2,1,0:T(2,128)(2,1)}), bf16[32,2,3008]{2,1,0:T(2,128)(2,1)S(1)}, u32[]{:S(2)}, u32[]{:S(2)}) %all-to-all-start) | async-done | bytes 385056 | tf_op jit(solution)/shard_map/all_to_all | solution.py:352
  59.4 48.9 %all-to-all-done.1 = bf16[32,48,768]{2,1,0:T(8,128)(2,1)} async-done(((bf16[32,48,768]{2,1,0:T(8,128)(2,1)}), bf16[32,48,768]{2,1,0:T(8,128)(2,1)}, u32[]{:S(2)}, u32[]{:S(2)}) %all-to-all-start.1) | async-done | bytes 2359328 | tf_op jit(solution)/shard_map/all_to_all | solution.py:375
  110.7 8.2 %conditional.2 = (f32[1280,768]{1,0:T(8,128)}) conditional(s32[]{:T(128)} %convert_element_type.381, (bf16[32,48,768]{2,1,0:T(8,128)(2,1)}, bf16[1280,1536]{1,0:T(8,128)(2,1)}) %tuple.20, (f32[960,768]{1,0:T(8,128)S(1)}, s32[1280]{0:T(1024)S(1)}) %tuple.105), branch_computations={%region_5.6_spmd, %region_6.7_spmd} | conditional | flops 3019898880 | bytes 160264224 | solution.py:382
  110.8 8.0 %fusion.164 = f32[1280,768]{1,0:T(8,128)} fusion(bf16[1280,1536]{1,0:T(8,128)(2,1)} %get-tuple-element.20, bf16[1536,768]{1,0:T(8,128)(2,1)} %bitcast), kind=kOutput, calls=%fused_computation.366 | convolution fusion | flops 3019898880 | bytes 10223616 | tf_op jit(solution)/shard_map/cond/branch_0_fun/dot_general | solution.py:40
  137.2 49.5 %all-gather.9.cloned.1.call-done = bf16[3072,768]{1,0:T(8,128)(2,1)} async-done(((bf16[96,768]{1,0:T(8,128)(2,1)}), bf16[3072,768]{1,0:T(8,128)(2,1)}) %all-gather.9.cloned.1.call-update) | async-done | bytes 4718608 | tf_op jit(solution)/shard_map/all_gather | solution.py:330
  186.7 8.5 %fusion.16.refs_2_ = bf16[1280,2304]{1,0:T(8,128)(2,1)S(1)} fusion(f32[2304]{0:T(1024)S(1)} %pad_maximum_fusion.2, bf16[3072,768]{1,0:T(8,128)(2,1)} %all-gather.9.cloned.1.call-done, f32[1280,768]{0,1:T(8,128)} %copy-done.9, f32[768]{0:T(1024)S(1)} %get-tuple-element.112, f32[768]{0:T(1024)S(1)} %get-tuple-element.113, f32[1280]{0:T(1024)S(1)} %add_rsqrt_fusion.3, ...), kind=kOutput, calls=%fused_computation.34 | convolution fusion | flops 4540661760 | bytes 13394944 | tf_op jit(solution)/shard_map/dot_general | solution.py:50
  195.2 14.0 %shard_map.409 = (bf16[1280,768]{1,0:T(8,128)(2,1)S(1)}, f32[1280,128]{1,0:T(8,128)S(1)}) custom-call(s32[1280,1]{1,0:T(8,128)S(1)} %broadcast_in_dim.49.refs_0_, s32[10,1,256]{2,1,0:T(1,128)S(1)} %constant_dynamic-update-slice_fusion.refs_1_, bf16[1280,2304]{1,0:T(8,128)(2,1)S(1)} %fusion.16.refs_2_), custom_call_target="tpu_custom_call" | custom-call | flops 2013265920 | bytes 12000000 | tf_op jit(solution)/shard_map/pallas_call | solution.py:194
  215.7 36.9 %all-gather.11.cloned.1.call-done = bf16[3072,768]{1,0:T(8,128)(2,1)} async-done(((bf16[96,768]{1,0:T(8,128)(2,1)}), bf16[3072,768]{1,0:T(8,128)(2,1)}) %all-gather.11.cloned.1.call-update) | async-done | bytes 4718608 | tf_op jit(solution)/shard_map/all_gather | solution.py:331
  252.5 60.1 %fusion.2 = (bf16[1280,3072]{1,0:T(8,128)(2,1)}, f32[1280,3072]{1,0:T(8,128)}) fusion(f32[3072]{0:T(1024)S(1)} %slice.224, bf16[3072,768]{1,0:T(8,128)(2,1)} %all-gather.11.cloned.1.call-done, f32[1280,768]{0,1:T(8,128)} %copy-done.15, f32[768]{0:T(1024)S(1)} %get-tuple-element.107, f32[768]{0:T(1024)S(1)} %get-tuple-element.108, ...), kind=kOutput, calls=%fused_computation.9 | convolution fusion | flops 6304235520 | bytes 32272384 | tf_op jit(solution)/shard_map/dot_general | solution.py:50
  318.4 11.8 %fusion.162 = (f32[1280]{0:T(1024)S(1)}, f32[1280,768]{0,1:T(8,128)S(1)}) fusion(f32[768]{0:T(1024)S(1)} %get-tuple-element.106, bf16[1280,3072]{1,0:T(8,128)(2,1)} %get-tuple-element.137, bf16[3072,768]{1,0:T(8,128)(2,1)} %all-gather.13.cloned.1.call-done, f32[768]{0:T(1024)S(1)} %get-tuple-element.107, f32[768]{0:T(1024)S(1)} %get-tuple-element.108, ...), kind=kOutput, calls=%fused_computation.364 | convolution fusion | flops 6046678016 | bytes 20471808 | tf_op jit(solution)/shard_map/dot_general | solution.py:40
  341.3 8.5 %all-gather.15.cloned.1.call-done = bf16[5120,128]{0,1:T(8,128)(2,1)} async-done(((bf16[1280,128]{0,1:T(8,128)(2,1)}), bf16[5120,128]{0,1:T(8,128)(2,1)}) %all-gather.15.cloned.1.call-update) | async-done | bytes 1310736 | tf_op jit(solution)/shard_map/all_gather | solution.py:414
  407.8 11.1 %fusion.79 = f32[3072,768]{1,0:T(8,128)} fusion(bf16[1280,3072]{1,0:T(8,128)(2,1)} %get-tuple-element.137, f32[1280,768]{0,1:T(8,128)S(1)} %get-tuple-element.83), kind=kOutput, calls=%fused_computation.152 | convolution fusion | flops 6040780800 | bytes 21233664 | tf_op jit(solution)/shard_map/dot_general | solution.py:44
  418.9 14.3 %convert_reduce_fusion = (f32[3072]{0:T(1024)S(1)}, bf16[1280,3072]{1,0:T(8,128)(2,1)S(1)}) fusion(f32[1280,3072]{1,0:T(8,128)} %get-tuple-element.138, f32[3072]{0:T(1024)S(1)} %copy-done.79, bf16[3072,768]{1,0:T(8,128)(2,1)S(1)} %bitcast.239, f32[1280,768]{0,1:T(8,128)S(1)} %get-tuple-element.83), kind=kOutput, calls=%fused_computation.16 | convolution fusion | flops 6091895808 | bytes 32268288 | tf_op jit(solution)/shard_map/dot_general | solution.py:50
  436.3 9.7 %fusion.140 = f32[3072,768]{1,0:T(8,128)} fusion(bf16[1280,3072]{1,0:T(8,128)(2,1)S(1)} %get-tuple-element.150, f32[1280,768]{0,1:T(8,128)S(1)} %copy-done.16, f32[768]{0:T(1024)S(1)} %copy-done.90, f32[768]{0:T(1024)S(1)} %copy-done.71, f32[1280]{0:T(1024)S(1)} %add_rsqrt_fusion.2, f32[1280]{0:T(1024)S(1)} %broadcast_multiply_fusion.7), kind=kOutput, calls=%fused_computation.354 | convolution fusion | flops 6044712960 | bytes 21250048 | tf_op jit(solution)/shard_map/dot_general | solution.py:44
  446.0 13.5 %multiply_reduce_fusion.2 = (f32[768]{0:T(1024)S(1)}, f32[1280]{0:T(1024)S(1)}, f32[1280]{0:T(1024)S(1)}, f32[768]{0:T(1024)S(1)}, f32[1280,768]{0,1:T(8,128)}) fusion(f32[1280,768]{0,1:T(8,128)S(1)} %copy-done.16, f32[1280]{0:T(1024)S(1)} %add_rsqrt_fusion.2, f32[1280]{0:T(1024)S(1)} %broadcast_multiply_fusion.7, f32[768]{0:T(1024)S(1)} %copy-done.71, ...), kind=kOutput, calls=%fused_computation.68 | convolution fusion | flops 6049624064 | bytes 24409088 | tf_op jit(solution)/shard_map/dot_general | solution.py:40
  468.1 36.3 %shard_map.410 = bf16[1280,2304]{1,0:T(8,128)(2,1)} custom-call(s32[1280,1]{1,0:T(8,128)} %copy-done, s32[10,1,256]{2,1,0:T(1,128)} %copy-done.1, bf16[1280,2304]{1,0:T(8,128)(2,1)} %copy-done.2, bf16[1280,768]{1,0:T(8,128)(2,1)} %convolution_convert_fusion.1.refs_3_, f32[1280,128]{1,0:T(8,128)} %copy-done.5), custom_call_target="tpu_custom_call" | custom-call | flops 5033164800 | bytes 18000000 | tf_op jit(solution)/shard_map/pallas_call | solution.py:216
  508.2 10.3 %fusion.144 = f32[2304,768]{1,0:T(8,128)} fusion(bf16[1280,2304]{1,0:T(8,128)(2,1)} %shard_map.410, f32[1280,768]{0,1:T(8,128)S(1)} %copy-done.11, f32[768]{0:T(1024)S(1)} %copy-done.88, f32[768]{0:T(1024)S(1)} %copy-done.73, f32[1280]{0:T(1024)S(1)} %copy-done.67, f32[1280]{0:T(1024)S(1)} %copy-done.54), kind=kOutput, calls=%fused_computation.356 | convolution fusion | flops 4534763520 | bytes 16924672 | tf_op jit(solution)/shard_map/dot_general | solution.py:44
  521.7 10.8 %multiply_reduce_fusion.3 = (f32[768]{0:T(1024)S(1)}, f32[1280]{0:T(1024)S(1)}, f32[1280]{0:T(1024)S(1)}, f32[768]{0:T(1024)S(1)}, f32[1280,768]{0,1:T(8,128)}) fusion(f32[1280,768]{0,1:T(8,128)S(1)} %copy-done.11, f32[1280]{0:T(1024)S(1)} %copy-done.67, f32[1280]{0:T(1024)S(1)} %copy-done.54, f32[768]{0:T(1024)S(1)} %copy-done.73, ...), kind=kOutput, calls=%fused_computation.69 | convolution fusion | flops 4539674624 | bytes 21263360 | tf_op jit(solution)/shard_map/dot_general | solution.py:40
  558.8 7.1 pad_maximum_fusion
  578.6 7.1 convolution_convert_fusion
  626.4 24.8 %collective-permute-done.11 = bf16[2,2,2,96,768]{4,3,0,1,2:T(8,128)(2,1)} collective-permute-done((bf16[2,2,2,96,768]{4,3,0,1,2:T(8,128)(2,1)}, bf16[2,2,2,96,768]{4,3,0,1,2:T(8,128)(2,1)}, u32[]{:S(2)}, u32[]{:S(2)}) %collective-permute-start.11) | collective-permute-done | bytes 1179680 | tf_op jit(solution)/shard_map/ppermute | solution.py:240
  658.0 18.5 %collective-permute-done.1 = bf16[2,2,2,96,768]{4,3,0,1,2:T(8,128)(2,1)} collective-permute-done((bf16[2,2,2,96,768]{4,3,0,1,2:T(8,128)(2,1)}, bf16[2,2,2,96,768]{4,3,0,1,2:T(8,128)(2,1)}, u32[]{:S(2)}, u32[]{:S(2)}) %collective-permute-start.1) | collective-permute-done | bytes 1179680 | tf_op jit(solution)/shard_map/ppermute | solution.py:240
  681.7 7.3 collective-permute-done.7
  (464 shorter events, 282.1 us)
Async XLA Ops:
  17.7 20.5 %all-to-all-start = ((bf16[32,2,3008]{2,1,0:T(2,128)(2,1)}), bf16[32,2,3008]{2,1,0:T(2,128)(2,1)S(1)}, u32[]{:S(2)}, u32[]{:S(2)}) async-start(bf16[32,2,3008]{2,1,0:T(2,128)(2,1)} %reshape.561), calls=%async_computation.1 | async-start | bytes 786432 | tf_op jit(solution)/shard_map/all_to_all | solution.py:352
  50.1 58.1 %all-to-all-start.1 = ((bf16[32,48,768]{2,1,0:T(8,128)(2,1)}), bf16[32,48,768]{2,1,0:T(8,128)(2,1)}, u32[]{:S(2)}, u32[]{:S(2)}) async-start(bf16[32,48,768]{2,1,0:T(8,128)(2,1)} %broadcast_select_fusion), calls=%async_computation.2 | async-start | bytes 4718592 | tf_op jit(solution)/shard_map/all_to_all | solution.py:375
  119.0 67.7 %all-gather.9.cloned.1.call-start = ((), (), s32[]{:S(2)}) async-start(), calls=%async_computation.8 | async-start | bytes 4866048 | tf_op jit(solution)/shard_map/all_gather | solution.py:330
  119.6 133.0 %all-gather.11.cloned.1.call-start = ((), (), s32[]{:S(2)}) async-start(), calls=%async_computation.9 | async-start | bytes 4866048 | tf_op jit(solution)/shard_map/all_gather | solution.py:331
  121.3 197.1 %all-gather.13.cloned.1.call-start = ((), (), s32[]{:S(2)}) async-start(), calls=%async_computation.10 | async-start | bytes 4866048 | tf_op jit(solution)/shard_map/all_gather | solution.py:332
  123.0 226.8 %all-gather.15.cloned.1.call-start = ((), (), s32[]{:S(2)}) async-start(), calls=%async_computation.11 | async-start | bytes 1638400 | tf_op jit(solution)/shard_map/all_gather | solution.py:414
  545.4 27.4 %all-to-all-start.4 = ((f32[32,1,1920]{2,1,0:T(1,128)}), f32[32,1,1920]{2,1,0:T(1,128)S(1)}, u32[]{:S(2)}, u32[]{:S(2)}) async-start(f32[32,1,1920]{2,1,0:T(1,128)} %all_to_all.33), calls=%async_computation.5 | async-start | bytes 491520 | tf_op jit(solution)/shard_map/all_to_all | solution.py:558
  554.3 47.1 %collective-permute-start.10 = (bf16[2,2,2,2,96,768]{5,4,0,1,2,3:T(8,128)(2,1)}, bf16[2,2,2,2,96,768]{5,4,0,1,2,3:T(8,128)(2,1)}, u32[]{:S(2)}, u32[]{:S(2)}) collective-permute-start(bf16[2,2,2,2,96,768]{5,4,0,1,2,3:T(8,128)(2,1)} %fusion.38), channel_id=1, source_target_pairs={{0,1},{1,0},{2,3},{3,2},{4,5},{5,4},{6,7},{7,6},{8,9},{9,8},{10,11... | collective-permute-start | bytes 7077896 | tf_op jit(solution)/shard_map/ppermute | solution.py:240
  558.6 51.9 %collective-permute-start.5 = (bf16[2,2,2,2,96,768]{5,4,0,1,3,2:T(8,128)(2,1)}, bf16[2,2,2,2,96,768]{5,4,0,1,3,2:T(8,128)(2,1)}, u32[]{:S(2)}, u32[]{:S(2)}) collective-permute-start(bf16[2,2,2,2,96,768]{5,4,0,1,3,2:T(8,128)(2,1)} %fusion.37), channel_id=1, source_target_pairs={{0,1},{1,0},{2,3},{3,2},{4,5},{5,4},{6,7},{7,6},{8,9},{9,8},{10,11... | collective-permute-start | bytes 7077896 | tf_op jit(solution)/shard_map/ppermute | solution.py:240
  570.1 46.7 %collective-permute-start = (bf16[2,2,2,2,96,768]{5,4,0,1,2,3:T(8,128)(2,1)}, bf16[2,2,2,2,96,768]{5,4,0,1,2,3:T(8,128)(2,1)}, u32[]{:S(2)}, u32[]{:S(2)}) collective-permute-start(bf16[2,2,2,2,96,768]{5,4,0,1,2,3:T(8,128)(2,1)} %fusion.36), channel_id=1, source_target_pairs={{0,1},{1,0},{2,3},{3,2},{4,5},{5,4},{6,7},{7,6},{8,9},{9,8},{10,11... | collective-permute-start | bytes 7077896 | tf_op jit(solution)/shard_map/ppermute | solution.py:240
  572.8 20.4 %all-to-all-start.2 = ((bf16[32,2,3648]{2,1,0:T(2,128)(2,1)}), bf16[32,2,3648]{2,1,0:T(2,128)(2,1)S(1)}, u32[]{:S(2)}, u32[]{:S(2)}) async-start(bf16[32,2,3648]{2,1,0:T(2,128)(2,1)} %reshape.563), calls=%async_computation.3 | async-start | bytes 950272 | tf_op jit(solution)/shard_map/all_to_all | solution.py:492
  594.0 118.5 %all-to-all-start.3 = ((bf16[32,48,768]{2,1,0:T(8,128)(2,1)}), bf16[32,48,768]{2,1,0:T(8,128)(2,1)S(1)}, u32[]{:S(2)}, u32[]{:S(2)}) async-start(bf16[32,48,768]{2,1,0:T(8,128)(2,1)} %bitcast.215), calls=%async_computation.4 | async-start | bytes 4718592 | tf_op jit(solution)/shard_map/all_to_all | solution.py:530
  608.7 42.5 %collective-permute-start.11 = (bf16[2,2,2,96,768]{4,3,0,1,2:T(8,128)(2,1)}, bf16[2,2,2,96,768]{4,3,0,1,2:T(8,128)(2,1)}, u32[]{:S(2)}, u32[]{:S(2)}) collective-permute-start(bf16[2,2,2,96,768]{4,3,0,1,2:T(8,128)(2,1)} %fusion.54), channel_id=1, source_target_pairs={{0,2},{1,3},{2,0},{3,1},{4,6},{5,7},{6,4},{7,5},{8,10},{9,11},{10,... | collective-permute-start | bytes 3538952 | tf_op jit(solution)/shard_map/ppermute | solution.py:240
  615.3 40.2 %collective-permute-start.6 = (bf16[2,2,2,96,768]{4,3,0,1,2:T(8,128)(2,1)}, bf16[2,2,2,96,768]{4,3,0,1,2:T(8,128)(2,1)}, u32[]{:S(2)}, u32[]{:S(2)}) collective-permute-start(bf16[2,2,2,96,768]{4,3,0,1,2:T(8,128)(2,1)} %fusion.53), channel_id=1, source_target_pairs={{0,4},{4,0},{8,12},{12,8},{16,20},{20,16},{24,28},{28,24},{1,5},{5... | collective-permute-start | bytes 3538952 | tf_op jit(solution)/shard_map/ppermute | solution.py:240
  622.6 53.9 %collective-permute-start.1 = (bf16[2,2,2,96,768]{4,3,0,1,2:T(8,128)(2,1)}, bf16[2,2,2,96,768]{4,3,0,1,2:T(8,128)(2,1)}, u32[]{:S(2)}, u32[]{:S(2)}) collective-permute-start(bf16[2,2,2,96,768]{4,3,0,1,2:T(8,128)(2,1)} %fusion.52), channel_id=1, source_target_pairs={{0,2},{1,3},{2,0},{3,1},{4,6},{5,7},{6,4},{7,5},{8,10},{9,11},{10,... | collective-permute-start | bytes 3538952 | tf_op jit(solution)/shard_map/ppermute | solution.py:240
  653.6 26.5 %collective-permute-start.12 = (bf16[2,2,96,768]{3,2,0,1:T(8,128)(2,1)S(1)}, bf16[2,2,96,768]{3,2,0,1:T(8,128)(2,1)S(1)}, u32[]{:S(2)}, u32[]{:S(2)}) collective-permute-start(bf16[2,2,96,768]{3,2,0,1:T(8,128)(2,1)S(1)} %fusion.86), channel_id=1, source_target_pairs={{0,4},{4,0},{8,12},{12,8},{16,20},{20,16},{24,28},{28,24},{1,5},{5... | collective-permute-start | bytes 1769480 | tf_op jit(solution)/shard_map/ppermute | solution.py:240
  657.9 31.1 %collective-permute-start.7 = (bf16[2,2,96,768]{3,2,0,1:T(8,128)(2,1)S(1)}, bf16[2,2,96,768]{3,2,0,1:T(8,128)(2,1)S(1)}, u32[]{:S(2)}, u32[]{:S(2)}) collective-permute-start(bf16[2,2,96,768]{3,2,0,1:T(8,128)(2,1)S(1)} %fusion.85), channel_id=1, source_target_pairs={{0,2},{1,3},{2,0},{3,1},{4,6},{5,7},{6,4},{7,5},{8,10},{9,11},{10,... | collective-permute-start | bytes 1769480 | tf_op jit(solution)/shard_map/ppermute | solution.py:240
  678.2 15.4 %collective-permute-start.2 = (bf16[2,2,96,768]{3,2,0,1:T(8,128)(2,1)S(1)}, bf16[2,2,96,768]{3,2,0,1:T(8,128)(2,1)S(1)}, u32[]{:S(2)}, u32[]{:S(2)}) collective-permute-start(bf16[2,2,96,768]{3,2,0,1:T(8,128)(2,1)S(1)} %fusion.84), channel_id=1, source_target_pairs={{0,4},{4,0},{8,12},{12,8},{16,20},{20,16},{24,28},{28,24},{1,5},{5... | collective-permute-start | bytes 1769480 | tf_op jit(solution)/shard_map/ppermute | solution.py:240
  680.3 14.6 %collective-permute-start.13 = (bf16[2,96,768]{2,1,0:T(8,128)(2,1)S(1)}, bf16[2,96,768]{2,1,0:T(8,128)(2,1)S(1)}, u32[]{:S(2)}, u32[]{:S(2)}) collective-permute-start(bf16[2,96,768]{2,1,0:T(8,128)(2,1)S(1)} %fusion.98), channel_id=1, source_target_pairs={{0,8},{4,12},{8,0},{12,4},{16,24},{20,28},{24,16},{28,20},{1,9},{5... | collective-permute-start | bytes 884744 | tf_op jit(solution)/shard_map/ppermute | solution.py:240
  689.2 10.6 %collective-permute-start.8 = (bf16[2,96,768]{2,1,0:T(8,128)(2,1)S(1)}, bf16[2,96,768]{2,1,0:T(8,128)(2,1)S(1)}, u32[]{:S(2)}, u32[]{:S(2)}) collective-permute-start(bf16[2,96,768]{2,1,0:T(8,128)(2,1)S(1)} %fusion.97), channel_id=1, source_target_pairs={{0,8},{4,12},{8,0},{12,4},{16,24},{20,28},{24,16},{28,20},{1,9},{5... | collective-permute-start | bytes 884744 | tf_op jit(solution)/shard_map/ppermute | solution.py:240
  693.8 16.0 %collective-permute-start.3 = (bf16[2,96,768]{2,1,0:T(8,128)(2,1)S(1)}, bf16[2,96,768]{2,1,0:T(8,128)(2,1)S(1)}, u32[]{:S(2)}, u32[]{:S(2)}) collective-permute-start(bf16[2,96,768]{2,1,0:T(8,128)(2,1)S(1)} %fusion.96), channel_id=1, source_target_pairs={{0,8},{4,12},{8,0},{12,4},{16,24},{20,28},{24,16},{28,20},{1,9},{5... | collective-permute-start | bytes 884744 | tf_op jit(solution)/shard_map/ppermute | solution.py:240
  695.7 31.9 %collective-permute-start.14 = (bf16[96,768]{1,0:T(8,128)(2,1)}, bf16[96,768]{1,0:T(8,128)(2,1)S(1)}, u32[]{:S(2)}, u32[]{:S(2)}) collective-permute-start(bf16[96,768]{1,0:T(8,128)(2,1)} %fusion.114), channel_id=1, source_target_pairs={{0,16},{4,20},{8,24},{12,28},{16,0},{20,4},{24,8},{28,12},{1,17},{... | collective-permute-start | bytes 442376 | tf_op jit(solution)/shard_map/ppermute | solution.py:240
  700.6 28.0 %collective-permute-start.9 = (bf16[96,768]{1,0:T(8,128)(2,1)}, bf16[96,768]{1,0:T(8,128)(2,1)}, u32[]{:S(2)}, u32[]{:S(2)}) collective-permute-start(bf16[96,768]{1,0:T(8,128)(2,1)} %fusion.113), channel_id=1, source_target_pairs={{0,16},{4,20},{8,24},{12,28},{16,0},{20,4},{24,8},{28,12},{1,17},{... | collective-permute-start | bytes 442376 | tf_op jit(solution)/shard_map/ppermute | solution.py:240
  710.7 19.8 %collective-permute-start.4 = (bf16[96,768]{1,0:T(8,128)(2,1)}, bf16[96,768]{1,0:T(8,128)(2,1)}, u32[]{:S(2)}, u32[]{:S(2)}) collective-permute-start(bf16[96,768]{1,0:T(8,128)(2,1)} %fusion.112), channel_id=1, source_target_pairs={{0,16},{4,20},{8,24},{12,28},{16,0},{20,4},{24,8},{28,12},{1,17},{... | collective-permute-start | bytes 442376 | tf_op jit(solution)/shard_map/ppermute | solution.py:240
  (104 other events, 2028.4 us)
Sparse Core Ops, SparseCore 1:
  123.4 63.3 all-gather.8
  190.5 62.0 all-gather.10
  256.3 62.0 all-gather.12
  333.5 16.3 all-gather.14

commit v2 on v1

--- a/solution.py
+++ b/solution.py
@@ -231,36 +231,249 @@
     )(segment_column, segment_windows, mixed, upstream, kept)
 
 
-def swap_half(parts, axis_name, bit, axis):
-    size = lax.axis_size(axis_name)
+def bits_of(axis_name):
+    return [(axis_name, b) for b in range(lax.axis_size(axis_name).bit_length() - 1)]
+
+
+def cut_chunks(gradient):
+    names = bits_of("grp")[::-1] + bits_of("psg")[::-1]
+    rows = gradient.shape[0] >> len(names)
+    return gradient.reshape((2,) * len(names) + (rows, gradient.shape[1])), names
+
+
+def halve_start(state, step):
+    parts, names = state
+    axis_name, bit = step
+    at = names.index(step)
     mine = (lax.axis_index(axis_name) >> bit) & 1
-    pairs = [(i, i ^ (1 << bit)) for i in range(size)]
-    sent = lax.dynamic_index_in_dim(parts, 1 - mine, axis, keepdims=False).astype(BF)
-    held = lax.dynamic_index_in_dim(parts, mine, axis, keepdims=False)
-    return held + lax.ppermute(sent, axis_name, pairs).astype(F32)
-
-
-def reduce_rows(gradient, group_first):
-    group_bits = lax.axis_size("grp").bit_length() - 1
-    member_bits = lax.axis_size("psg").bit_length() - 1
-    rows = gradient.shape[0] // (1 << (group_bits + member_bits))
-    shape = (2,) * (group_bits + member_bits) + (rows, gradient.shape[1])
-    parts = gradient.reshape(shape)
-    names = [("grp", b) for b in reversed(range(group_bits))] + [
-        ("psg", b) for b in reversed(range(member_bits))
+    pairs = [(i, i ^ (1 << bit)) for i in range(lax.axis_size(axis_name))]
+    sent = lax.dynamic_index_in_dim(parts, 1 - mine, at, keepdims=False).astype(BF)
+    held = lax.dynamic_index_in_dim(parts, mine, at, keepdims=False)
+    return held, lax.ppermute(sent, axis_name, pairs), names[:at] + names[at + 1 :]
+
+
+def halve_end(flying):
+    held, received, names = flying
+    return held + received.astype(F32), names
+
+
+def gate(value, *flying):
+    value, received = lax.optimization_barrier((value, tuple(f[1] for f in flying)))
+    return value, *((f[0], r, f[2]) for f, r in zip(flying, received))
+
+
+def place_of():
+    return lax.axis_index("grp") * lax.axis_size("psg") + lax.axis_index("psg")
+
+
+def mesh_place(place):
+    members = lax.axis_size("psg")
+    return (place // members, place % members)
+
+
+def flipped(place, mask):
+    result, bit = place, 0
+    while mask >> bit:
+        if (mask >> bit) & 1:
+            result = result + (1 - 2 * ((place // (1 << bit)) % 2)) * (1 << bit)
+        bit += 1
+    return result
+
+
+def greet_all(devices, me):
+    barrier = pltpu.get_barrier_semaphore()
+
+    @pl.loop(1, devices)
+    def _(i):
+        pl.semaphore_signal(
+            barrier,
+            inc=1,
+            device_id=mesh_place((me + i) % devices),
+            device_id_type=pl.DeviceIdType.MESH,
+        )
+
+    pl.semaphore_wait(barrier, devices - 1)
+
+
+def gather_plan(order, group):
+    held, steps = [0], []
+    for bit in order:
+        fresh = [(1 << bit) | m for m in held]
+        steps.append([fresh[i : i + group] for i in range(0, len(fresh), group)])
+        held = held + fresh
+    return steps
+
+
+def pack_rows(asked, table, rank_ref, packed_ref):
+    devices, capacity, _ = packed_ref.shape
+    width = table.shape[0]
+    asked = jnp.concatenate([asked[:, j, :] for j in range(width // 128)], axis=1)
+    above = lax.broadcasted_iota(jnp.int32, (width, width), 0)
+    earlier = (above < lax.broadcasted_iota(jnp.int32, (width, width), 1)).astype(F32).astype(BF)
+    rank_ref[...] = jnp.where(asked > 0.5, matmul(asked.astype(BF), earlier), -1.0)
+    most = jnp.max(jnp.sum(asked, axis=1, keepdims=True), axis=0, keepdims=True)
+    together = 8
+
+    @pl.loop(0, devices // together)
+    def _(i):
+        rank = rank_ref[pl.ds(pl.multiple_of(i * together, together), together), :]
+        slot = lax.broadcasted_iota(jnp.int32, (together, capacity, width), 1).astype(F32)
+        picked = jnp.where(rank[:, None, :] == slot, 1.0, 0.0)
+        picked = picked.reshape(together * capacity, width).astype(BF)
+        rows = matmul(picked, table[...]).reshape(together, capacity, D)
+        place = lax.broadcasted_iota(jnp.int32, (together, capacity, D), 1)
+        rows = jnp.where((place == capacity - 1) & (most > capacity)[:, :, None], MARK, rows)
+        packed_ref[pl.ds(i * together, together)] = rows.astype(BF)
+
+
+def gather_kernel(devices, pieces, *refs):
+    matrices = 3
+    sources, (needed, notes, table) = refs[:matrices], refs[matrices : matrices + 3]
+    outs, (notes_out, rows_out, rank) = refs[6:9], refs[9:12]
+    asked, packed, arrive, beside, leave, local, notes_sem, ask_sem, rows_sem = refs[12:]
+    me = place_of()
+    group = max(devices // 8, 1)
+    greet_all(devices, me)
+
+    def push(source, target_ref, target, send, recv):
+        pltpu.make_async_remote_copy(
+            src_ref=source,
+            dst_ref=target_ref,
+            send_sem=send,
+            recv_sem=recv,
+            device_id=mesh_place(target),
+            device_id_type=pl.DeviceIdType.MESH,
+        ).start()
+
+    def settle(some, semaphore):
+        pltpu.make_async_copy(some, some, semaphore).wait()
+
+    @pl.loop(1, devices)
+    def _(i):
+        target = (me + i) % devices
+        push(needed.at[target], asked.at[me], target, ask_sem.at[0], ask_sem.at[1])
+
+    def start(piece, mask, target, semaphore):
+        which, first, rows, _ = pieces[piece]
+        there = outs[which].at[flipped(me, mask), pl.ds(first, rows)]
+        here = sources[which].at[pl.ds(first, rows)] if mask == 0 else there
+        push(here, there, flipped(me, target), leave.at[piece], semaphore)
+
+    def wait(piece, blocks, semaphore):
+        which, first, rows, _ = pieces[piece]
+        settle(outs[which].at[pl.ds(0, blocks), pl.ds(first, rows)], semaphore)
+
+    plans, numbers = [], []
+    for piece in range(len(pieces)):
+        plan = gather_plan(pieces[piece][3], group)
+        number, count = {}, 0
+        for groups in plan:
+            for masks in groups:
+                for mask in masks:
+                    number[mask] = count
+                count += 1
+        plans.append(plan)
+        numbers.append(number)
+
+    def send_on(piece, mask, after):
+        order = pieces[piece][3]
+        for step in range(after + 1, len(order)):
+            target = 1 << order[step]
+            start(piece, mask, target, arrive.at[piece, numbers[piece][mask | target]])
+        start(piece, mask, 1, beside.at[piece])
+
+    def pass_on(piece, step):
+        for masks in plans[piece][step]:
+            wait(piece, len(masks), arrive.at[piece, numbers[piece][masks[0]]])
+            for mask in masks:
+                send_on(piece, mask, step)
+
+    for piece in range(len(pieces)):
+        send_on(piece, 0, -1)
+
+    @pl.loop(1, devices)
+    def _(i):
+        target = (me + i) % devices
+        push(notes, notes_out.at[me], target, notes_sem.at[0], notes_sem.at[1])
+
+    own = [
+        pltpu.make_async_copy(source, out.at[me], local.at[i])
+        for i, (source, out) in enumerate(zip(sources, outs))
     ]
-    order = [("psg", 0)]
-    if group_first:
-        order += [("grp", 0)] + [("psg", b) for b in range(1, member_bits)]
-        order += [("grp", b) for b in range(1, group_bits)]
-    else:
-        order += [("psg", b) for b in range(1, member_bits)]
-        order += [("grp", b) for b in range(group_bits)]
-    for step in order:
-        at = names.index(step)
-        parts = swap_half(parts, step[0], step[1], at)
-        names.pop(at)
-    return parts
+    own.append(pltpu.make_async_copy(notes, notes_out.at[me], local.at[matrices]))
+    own_asked = pltpu.make_async_copy(needed.at[me], asked.at[me], local.at[matrices + 1])
+    for copy in own:
+        copy.start()
+    own_asked.start()
+    for piece in range(len(pieces)):
+        pass_on(piece, 0)
+    own_asked.wait()
+    for i in range(2):
+        settle(asked.at[pl.ds(0, devices - 1)], ask_sem.at[i])
+    pack_rows(asked[...], table, rank, packed)
+
+    masks = sorted(range(1, devices), key=lambda m: -bin(m).count("1"))
+    steps = len(pieces[0][3])
+    each = -(-(devices - 1) // (len(pieces) * (steps - 1)))
+    kept_rows = pltpu.make_async_copy(packed.at[me], rows_out.at[me], local.at[matrices + 2])
+    kept_rows.start()
+    for step in range(1, steps):
+        for piece in range(len(pieces)):
+            pass_on(piece, step)
+            now, masks = masks[:each], masks[each:]
+            for mask in now:
+                target = flipped(me, mask)
+                push(packed.at[target], rows_out.at[me], target, rows_sem.at[0], rows_sem.at[1])
+    for piece in range(len(pieces)):
+        wait(piece, devices // 2, beside.at[piece])
+        wait(piece, devices - 1, leave.at[piece])
+    for copy in own:
+        copy.wait()
+    kept_rows.wait()
+    for i in range(2):
+        settle(notes_out.at[pl.ds(0, devices - 1)], notes_sem.at[i])
+        settle(rows_out.at[pl.ds(0, devices - 1)], rows_sem.at[i])
+
+
+def gather_all(sources, needed, notes, table, capacity):
+    devices = needed.shape[0]
+    rows = sources[0].shape[0]
+    bits = devices.bit_length() - 1
+    high = list(range(3, bits))[::-1]
+    one, other = (*high, 2, 1), (*high, 1, 2)
+    cut = rows // 32 * 16
+    pieces = [(0, 0, rows, one), (2, 0, rows, other), (1, cut, rows - cut, one)]
+    if cut:
+        pieces.append((1, 0, cut, other))
+    count = max(sum(map(len, gather_plan(p[3], max(devices // 8, 1)))) for p in pieces)
+    anywhere = pl.BlockSpec(memory_space=pl.ANY)
+    inside = pl.BlockSpec(memory_space=pltpu.VMEM)
+    dma = pltpu.SemaphoreType.DMA
+    *gathered, noted, arrived, rank = pl.pallas_call(
+        lambda *refs: gather_kernel(devices, pieces, *refs),
+        in_specs=[anywhere] * 3 + [inside] * 3,
+        out_specs=[anywhere] * 5 + [inside],
+        out_shape=[jax.ShapeDtypeStruct((devices, *s.shape), s.dtype) for s in (*sources, notes)]
+        + [
+            jax.ShapeDtypeStruct((devices, capacity, D), BF),
+            jax.ShapeDtypeStruct((devices, table.shape[0]), F32),
+        ],
+        scratch_shapes=[
+            pltpu.VMEM(needed.shape, F32),
+            pltpu.VMEM((devices, capacity, D), BF),
+            dma((len(pieces), count)),
+            dma((len(pieces),)),
+            dma((len(pieces),)),
+            dma((6,)),
+            dma((2,)),
+            dma((2,)),
+            dma((2,)),
+        ],
+        compiler_params=pltpu.CompilerParams(
+            collective_id=0, has_side_effects=True, vmem_limit_bytes=48 * 2**20
+        ),
+    )(*sources, needed, notes, table)
+    return gathered, noted, arrived, rank
 
 
 def adam_update(weight, moment, second, gradient, rate, count_steps):
@@ -327,55 +540,48 @@
         ]
     )
 
-    attn_rows = lax.all_gather(attention_weight.T.astype(BF), ALL, axis=0, tiled=True)
-    up_rows = lax.all_gather(up_weight.T.astype(BF), ALL, axis=0, tiled=True)
-    down_rows = lax.all_gather(down_weight.astype(BF), ALL, axis=0, tiled=True)
+    def shard_of(rows):
+        return jnp.pad(rows.astype(BF), ((0, -rows.shape[0] % 16), (0, 0)))
+
+    matrix_rows = down_weight.shape[0]
+    shards = [shard_of(attention_weight.T), shard_of(up_weight.T), shard_of(down_weight)]
 
     owner = tokens // shard_rows
     local_row = tokens - owner * shard_rows
     owner_hot = one_hot(owner, devices)
     row_hot = one_hot(local_row, shard_rows)
-    needed = jnp.minimum(contract_rows(owner_hot, row_hot), 1.0).astype(BF)
-    spread = lambda v: jnp.broadcast_to(v.reshape(1, -1).astype(BF), (devices, v.size))
-    payload = jnp.concatenate(
+    needed = jnp.minimum(contract_rows(owner_hot, row_hot), 1.0)
+    width = -(-shard_rows // 1024) * 1024
+    table = jnp.pad(embed_table.astype(BF), ((0, width - shard_rows), (0, 0)))
+    notes = jnp.concatenate(
         [
-            needed,
-            spread(small_params),
-            spread(head_weight),
-            spread(passage_lengths),
-            spread(jnp.sum(mask_float)),
-        ],
-        axis=1,
-    )
-    width = payload.shape[1]
-    payload = jnp.pad(payload, ((0, 0), (0, -width % 128)))
-    arrived = lax.all_to_all(payload, ALL, split_axis=0, concat_axis=0, tiled=True)
-    cut = [0, shard_rows, small_size, head_rows * DC, PPD, 1]
+            v.reshape(-1).astype(BF)
+            for v in (small_params, head_weight, passage_lengths, jnp.sum(mask_float))
+        ]
+    )
+    notes = jnp.pad(notes, (0, -notes.size % 2048)).reshape(-1, 128)
+    gathered, noted, packed, asked_rank = gather_all(
+        shards,
+        jnp.pad(needed, ((0, 0), (0, width - shard_rows))).reshape(devices, width // 128, 128),
+        notes,
+        table,
+        capacity,
+    )
+    asked_rank = asked_rank[:, :shard_rows]
+    attn_rows, up_rows, down_rows = (g[:, :matrix_rows].reshape(-1, D) for g in gathered)
+    noted = noted.reshape(devices, -1)
+    cut = [0, small_size, head_rows * DC, PPD, 1]
     for i in range(1, len(cut)):
         cut[i] += cut[i - 1]
-    asked, small_all, head_all, lengths_all, pairs_all = (
-        arrived[:, cut[i] : cut[i + 1]] for i in range(5)
-    )
+    small_all, head_all, lengths_all, pairs_all = (noted[:, cut[i] : cut[i + 1]] for i in range(4))
     small_all = small_all.reshape(-1)
     head_full = head_all.reshape(D, DC)
     pair_floor = jnp.maximum(jnp.sum(pairs_all.astype(F32)), 1.0)
     place_row = jnp.arange(shard_rows, dtype=jnp.int32)
     earlier = (place_row[:, None] < place_row[None, :]).astype(BF)
-    asked_rank = matmul(asked, earlier)
-    slots = jnp.arange(capacity, dtype=jnp.int32).astype(F32)
-    picked = (
-        ((asked_rank[:, None, :] == slots[None, :, None]) & (asked[:, None, :] > 0))
-        .astype(BF)
-        .reshape(devices * capacity, shard_rows)
-    )
-    packed = matmul(picked, embed_table.astype(BF)).astype(BF).reshape(devices, capacity, D)
-    too_many = jnp.max(jnp.sum(asked.astype(F32), axis=1)) > capacity
-    last_slot = (jnp.arange(capacity) == capacity - 1)[None, :, None]
-    packed = jnp.where(too_many & last_slot, BF(MARK), packed)
-    packed = lax.all_to_all(packed, ALL, split_axis=0, concat_axis=0, tiled=True)
     overflow = jnp.max(packed[:, capacity - 1, :].astype(F32)) > 0.5 * MARK
     packed = packed.reshape(devices * capacity, D)
-    needed_rank = jnp.minimum(matmul(needed, earlier), 255.0)
+    needed_rank = jnp.minimum(matmul(needed.astype(BF), earlier), 255.0)
     token_rank = jnp.sum(matmul(owner_hot, needed_rank.astype(BF)) * row_hot.astype(F32), axis=1)
     slot = owner * capacity + jnp.minimum(token_rank.astype(jnp.int32), capacity - 1)
     slot_hot = one_hot(slot, devices * capacity)
@@ -401,7 +607,7 @@
     )
     input_one = hidden_one.astype(BF)
     inner = contract_cols(input_one, up_rows) + bias_up
-    activated = jax.nn.gelu(inner, approximate=False).astype(BF)
+    activated = (0.5 * inner * (1.0 + lax.erf(inner / math.sqrt(2.0)))).astype(BF)
     hidden_two, norm_two = layer_norm(
         hidden_one + matmul(activated, down_rows) + pieces[7], pieces[8], pieces[9]
     )
@@ -484,7 +690,7 @@
             count_high.reshape(devices, -1),
             count_low.reshape(devices, -1),
         ]
-        + [spread(v) for v in split_three(numerator)],
+        + [jnp.broadcast_to(v, (devices, 1)) for v in split_three(numerator)],
         axis=1,
     )
     early_width = early.shape[1]
@@ -503,41 +709,48 @@
     grad_hidden_two = contract_cols(grad_proj, head_full)
     grad_sum_two, grad_gain_two, grad_shift_two = norm_back(grad_hidden_two, norm_two, pieces[8])
     grad_two_low = grad_sum_two.astype(BF)
-    down_reduced = reduce_rows(contract_rows(activated, grad_two_low), False)
+    member_bits, group_bits = bits_of("psg"), bits_of("grp")
+    member_first = member_bits + group_bits
+    group_first = member_bits[:1] + group_bits[:1] + member_bits[1:] + group_bits[1:]
+    down = halve_start(cut_chunks(contract_rows(activated, grad_two_low)), member_first[0])
     grad_activated = contract_cols(grad_two_low, down_rows)
     normal_cdf = 0.5 * (1.0 + lax.erf(inner / math.sqrt(2.0)))
     normal_pdf = jnp.exp(-0.5 * inner * inner) / math.sqrt(2.0 * math.pi)
     grad_inner = (grad_activated * (normal_cdf + inner * normal_pdf)).astype(BF)
-    up_reduced = reduce_rows(contract_rows(grad_inner, input_one), True)
+    grad_inner, down = gate(grad_inner, down)
+    down = halve_start(halve_end(down), member_first[1])
+    up = halve_start(cut_chunks(contract_rows(grad_inner, input_one)), group_first[0])
     grad_bias_up = jnp.sum(grad_inner.astype(F32), axis=0)
     grad_hidden_one = grad_sum_two + matmul(grad_inner, up_rows)
+    grad_hidden_one, up = gate(grad_hidden_one, up)
+    up = halve_start(halve_end(up), group_first[1])
     grad_sum_one, grad_gain_one, grad_shift_one = norm_back(grad_hidden_one, norm_one, pieces[5])
     grad_one_low = grad_sum_one.astype(BF)
     grad_out_rows = contract_rows(grad_one_low, context)
     grad_context = matmul(grad_one_low, attn_rows[3 * D :]).astype(BF)
+    grad_context, down = gate(grad_context, down)
+    down = halve_start(halve_end(down), member_first[2])
     grad_mixed = attention_backward(segment_column, segment_windows, mixed, grad_context, kept)
+    grad_mixed, down, up = gate(grad_mixed, down, up)
+    down = halve_start(halve_end(down), member_first[3])
+    up = halve_start(halve_end(up), group_first[2])
+    grad_qkv_rows = contract_rows(grad_mixed, input_zero)
+    attn = halve_start(
+        cut_chunks(jnp.concatenate([grad_qkv_rows, grad_out_rows], axis=0)), member_first[0]
+    )
     grad_mixed_sum = jnp.sum(grad_mixed.astype(F32), axis=0)
     grad_hidden_zero = grad_sum_one + matmul(grad_mixed, attn_rows[: 3 * D])
+    grad_hidden_zero, down, up, attn = gate(grad_hidden_zero, down, up, attn)
+    down = halve_start(halve_end(down), member_first[4])
+    up = halve_start(halve_end(up), group_first[3])
+    attn = halve_start(halve_end(attn), member_first[1])
     grad_embedded, grad_gain_zero, grad_shift_zero = norm_back(
         grad_hidden_zero, norm_zero, pieces[0]
     )
-    grad_qkv_rows = contract_rows(grad_mixed, input_zero)
-    attn_reduced = reduce_rows(jnp.concatenate([grad_qkv_rows, grad_out_rows], axis=0), False)
 
     grad_low = grad_embedded.astype(BF)
     grad_positions = contract_rows(position_hot, grad_low)
     grad_slots = contract_rows(slot_hot, grad_low).astype(BF).reshape(devices, capacity, D)
-    grad_slots = lax.all_to_all(grad_slots, ALL, split_axis=0, concat_axis=0, tiled=True)
-
-    def whole_table():
-        table = jnp.zeros((shard_rows * devices, D), F32).at[tokens].add(grad_embedded)
-        return lax.psum_scatter(table, ALL, scatter_dimension=0, tiled=True)
-
-    table_reduced = lax.cond(
-        overflow,
-        whole_table,
-        lambda: contract_rows(picked, grad_slots.reshape(devices * capacity, D)),
-    )
     grad_small = jnp.concatenate(
         [
             grad_positions.reshape(-1),
@@ -554,9 +767,40 @@
             grad_bias_up,
         ]
     ).reshape(devices, small_size)
-    grad_small = jnp.pad(grad_small, ((0, 0), (0, -small_size % 128)))
-    grad_small = lax.all_to_all(grad_small, ALL, split_axis=0, concat_axis=0, tiled=True)
-    small_reduced = jnp.sum(grad_small, axis=0)[:small_size]
+    grad_small = jnp.pad(grad_small.astype(BF), ((0, 0), (0, -small_size % D)))
+    grad_slots = jnp.concatenate([grad_slots, grad_small.reshape(devices, -1, D)], axis=1)
+    grad_slots, down, up = gate(grad_slots, down, up)
+    grad_slots = lax.all_to_all(grad_slots, ALL, split_axis=0, concat_axis=0, tiled=True)
+    small_reduced = jnp.sum(grad_slots[:, capacity:].astype(F32), axis=0).reshape(-1)[:small_size]
+    grad_slots = grad_slots[:, :capacity]
+    down = halve_end(down)
+    up = halve_end(halve_start(halve_end(up), group_first[4]))
+    attn = halve_end(attn)
+    for step in member_first[2:]:
+        attn = halve_end(halve_start(attn, step))
+    for step in member_first[5:]:
+        down = halve_end(halve_start(down, step))
+    for step in group_first[5:]:
+        up = halve_end(halve_start(up, step))
+    down_reduced, up_reduced, attn_reduced = down[0], up[0], attn[0]
+
+    def whole_table():
+        table = jnp.zeros((shard_rows * devices, D), F32).at[tokens].add(grad_embedded)
+        return lax.psum_scatter(table, ALL, scatter_dimension=0, tiled=True)
+
+    def own_rows():
+        slots = jnp.arange(capacity, dtype=jnp.int32).astype(F32)
+        picked = (asked_rank[:, None, :] == slots[None, :, None]).astype(BF)
+        return contract_rows(
+            picked.reshape(devices * capacity, shard_rows),
+            grad_slots.reshape(devices * capacity, D),
+        )
+
+    table_reduced = lax.cond(
+        overflow,
+        whole_table,
+        own_rows,
+    )
 
     count_steps = step_count[0].astype(F32)
     attn_reduced = attn_reduced.T

time: 753 us -> 653 us (0.87)
  waiting for transfers between devices: 228 us -> 91.3 us
  Pallas kernels: 50.3 us -> 158 us
  matrix products: 216 us -> 157 us
  starting transfers between devices: 47.8 us -> 24.6 us
  other arithmetic: 85.8 us -> 96.5 us
    pallas_call x0 -> x1, Pallas kernels: none -> 108 us  [gather_all(): pl.pallas_call(lambda *refs: gather_kernel(devices, pieces, *refs), in_sp...]
    all_gather x3 -> x0, waiting for transfers between devices: 92.1 us -> none  [the longest x1 49.5 us: on_device(): lax.all_gather(attention_weight.T.astype(BF), ALL, axis=0, tiled=True)]
    all_to_all x3 -> x0, waiting for transfers between devices: 62 us -> none  [the longest x1 48.9 us: on_device(): lax.all_to_all(packed, ALL, split_axis=0, concat_axis=0, tiled=True)]
    dot_general x6, matrix products: 91 us -> 40.4 us  [contract_cols(): lax.dot_general(lhs_mat, rhs_mat, (((1,), (1,)), ((), ())), preferred_ele...]
    ppermute x15, waiting for transfers between devices: 57.7 us -> 79.8 us  [halve_start(): lax.ppermute(sent, axis_name, pairs)]
    all_to_all x3 -> x0, starting transfers between devices: 15.5 us -> none  [the longest x1 7.3 us: on_device(): lax.all_to_all(payload, ALL, split_axis=0, concat_axis=0, tiled=True)]
    convert_element_type x15 -> x16, local copies, waits for them, and re-layouts: 18.5 us -> 9.36 us  [the longest x15 9.16 us: halve_start(): lax.dynamic_index_in_dim(parts, 1 - mine, at, keepdims=False).astype(BF)]
    ppermute x15, starting transfers between devices: 23.4 us -> 15.4 us  [halve_start(): lax.ppermute(sent, axis_name, pairs)]
  transfers between devices with their start and end apart: 24 -> 18, of which waited for: 12 -> 7; matrix products, arithmetic and copies ran while one was open for 23% -> 19% of each run, Pallas kernels for 2% -> 6%
where the time goes in v2:
time: 653 us; the launch traced here: 642 us
  Pallas kernels  158 us (24%)
  matrix products  157 us (24%)
  other arithmetic  96.5 us (15%)
  waiting for transfers between devices  91.3 us (14%)
  local copies, waits for them, and re-layouts  81 us (12%)
  between operations  27.9 us (4%)
  starting transfers between devices  24.6 us (4%)
    pallas_call x1, Pallas kernels, gather_all(): pl.pallas_call(lambda *refs: gather_kernel(devices, pieces, *refs), in_sp...  108 us
    ppermute x15, waiting for transfers between devices, halve_start(): lax.ppermute(sent, axis_name, pairs)  79.8 us
    dot_general x11, matrix products, contract_rows(): lax.dot_general(lhs_mat, rhs_mat, (((0,), (0,)), ((), ())), preferred_ele...  54.1 us
    dot_general x10, matrix products, matmul(): return jnp.dot(lhs_mat, rhs_mat, preferred_element_type=jnp.float32)  53.7 us
    dot_general x6, matrix products, contract_cols(): lax.dot_general(lhs_mat, rhs_mat, (((1,), (1,)), ((), ())), preferred_ele...  40.4 us
    pallas_call x1, Pallas kernels, attention_backward(): pl.pallas_call(lambda *refs: attn_backward_kernel(count, blocks, *refs),...  36.4 us
    unnamed x285, local copies, waits for them, and re-layouts  32.9 us
    add x12, other arithmetic, halve_end(): return (held + received.astype(F32), names)  20.5 us
  transfers between devices with their start and end apart: 18, of which 7 were waited for; matrix products, arithmetic and copies ran while one was open for 19% of the time, Pallas kernels for 6%

profile of v2, /device:TPU:0, one launch (start us, length us, event | category | flops | bytes accessed | tf_op | source)
XLA Modules:
  0.0 642.1 jit_solution(2776537593155732045)
XLA Ops:
  26.1 107.7 %shard_map.409 = (bf16[32,96,768]{2,1,0:T(8,128)(2,1)}, bf16[32,96,768]{2,1,0:T(8,128)(2,1)}, bf16[32,96,768]{2,1,0:T(8,128)(2,1)}, bf16[32,48,128]{2,1,0:T(8,12...) custom-call(bf16[96,768]{1,0:T(8,128)(2,1)S(1)} %get-tuple-element.196.refs_0_, ...), custom_call_target="tpu_custom_call" | custom-call | tf_op jit(solution)/shard_map/pallas_call | solution.py:452
  147.7 8.2 %conditional.2 = (f32[1280,768]{1,0:T(8,128)}) conditional(s32[]{:T(128)} %convert_element_type.379, (bf16[32,48,768]{2,1,0:T(8,128)(2,1)}, bf16[1280,1536]{1,0:T(8,128)(2,1)}) %tuple.26, (f32[960,768]{1,0:T(8,128)}, s32[1280]{0:T(1024)S(1)}) %tuple.27), branch_computations={%region_3.4_spmd, %region_4.5_spmd} | conditional | flops 3019898880 | bytes 160264224 | solution.py:588
  147.7 8.0 %fusion.156 = f32[1280,768]{1,0:T(8,128)} fusion(bf16[1280,1536]{1,0:T(8,128)(2,1)} %get-tuple-element.25, bf16[1536,768]{1,0:T(8,128)(2,1)} %bitcast.223), kind=kOutput, calls=%fused_computation.331 | convolution fusion | flops 3019898880 | bytes 10223616 | tf_op jit(solution)/shard_map/cond/branch_0_fun/dot_general | solution.py:40
  168.1 5.8 fusion.16.refs_2_
  174.0 14.0 %shard_map.410 = (bf16[1280,768]{1,0:T(8,128)(2,1)S(1)}, f32[1280,128]{1,0:T(8,128)S(1)}) custom-call(s32[1280,1]{1,0:T(8,128)S(1)} %broadcast_in_dim.20.refs_0_, s32[10,1,256]{2,1,0:T(1,128)S(1)} %constant_dynamic-update-slice_fusion.refs_1_, bf16[1280,2304]{1,0:T(8,128)(2,1)S(1)} %fusion.16.refs_2_), custom_call_target="tpu_custom_call" | custom-call | flops 2013265920 | bytes 12000000 | tf_op jit(solution)/shard_map/pallas_call | solution.py:194
  191.7 12.5 %multiply_convert_fusion = (bf16[1280,3072]{1,0:T(8,128)(2,1)}, f32[1280,3072]{1,0:T(8,128)}) fusion(f32[3072]{0:T(1024)S(1)} %slice.238, bf16[3072,768]{1,0:T(8,128)(2,1)S(1)} %bitcast.236, f32[1280,768]{0,1:T(8,128)S(1)} %get-tuple-element.182, f32[768]{0:T(1024)S(1)} %get-tuple-element.151, f32[768]{0:T(1024)S(1)} %get-tuple-element.152, ...), kind=kOutput, calls=%fused_computation.19 | convolution fusion | flops 6068305920 | bytes 32272384 | tf_op jit(solution)/shard_map/dot_general | solution.py:50
  204.3 11.5 %fusion.154 = (f32[1280]{0:T(1024)S(1)}, f32[1280,768]{0,1:T(8,128)S(1)}) fusion(f32[768]{0:T(1024)S(1)} %get-tuple-element.150, bf16[1280,3072]{1,0:T(8,128)(2,1)} %get-tuple-element.183, bf16[3072,768]{1,0:T(8,128)(2,1)} %bitcast.237, f32[768]{0:T(1024)S(1)} %get-tuple-element.151, f32[768]{0:T(1024)S(1)} %get-tuple-element.152, ...), kind=kOutput, calls=%fused_computation.329 | convolution fusion | flops 6046678016 | bytes 20471808 | tf_op jit(solution)/shard_map/dot_general | solution.py:40
  226.1 11.5 %all-gather.6.cloned.1.call-done = bf16[5120,128]{0,1:T(8,128)(2,1)} async-done(((bf16[1280,128]{0,1:T(8,128)(2,1)}), bf16[5120,128]{0,1:T(8,128)(2,1)}) %all-gather.6.cloned.1.call-update) | async-done | bytes 1310736 | tf_op jit(solution)/shard_map/all_gather | solution.py:620
  305.0 10.4 %fusion.70 = f32[3072,768]{1,0:T(8,128)S(1)} fusion(bf16[1280,3072]{1,0:T(8,128)(2,1)} %get-tuple-element.183, f32[1280,768]{0,1:T(8,128)S(1)} %get-tuple-element.143), kind=kOutput, calls=%fused_computation.130 | convolution fusion | flops 6040780800 | bytes 21233664 | tf_op jit(solution)/shard_map/dot_general | solution.py:44
  319.9 16.1 %fusion.15 = bf16[1280,3072]{1,0:T(8,128)(2,1)S(1)} fusion(bf16[3072,768]{1,0:T(8,128)(2,1)} %bitcast.238, f32[1280,3072]{1,0:T(8,128)} %get-tuple-element.184, f32[3072]{0:T(1024)S(1)} %copy-done.93, f32[1280,768]{0,1:T(8,128)} %copy-done.27), kind=kOutput, calls=%fused_computation.18 | convolution fusion | flops 6084034560 | bytes 32256000 | tf_op jit(solution)/shard_map/dot_general | solution.py:50
  336.2 7.1 %fusion.132 = f32[3072,768]{1,0:T(8,128)S(1)} fusion(bf16[1280,3072]{1,0:T(8,128)(2,1)S(1)} %fusion.15, f32[1280,768]{0,1:T(8,128)S(1)} %copy-done.12, f32[768]{0:T(1024)S(1)} %copy-done.114, f32[768]{0:T(1024)S(1)} %copy-done.77, f32[1280]{0:T(1024)S(1)} %copy-done.63, f32[1280]{0:T(1024)S(1)} %copy-done.54), kind=kOutput, calls=%fused_computation.319 | convolution fusion | flops 6044712960 | bytes 21250048 | tf_op jit(solution)/shard_map/dot_general | solution.py:44
  352.2 11.3 %convolution_add_fusion.2 = f32[1280,768]{0,1:T(8,128)S(1)} fusion(f32[1280,768]{0,1:T(8,128)} %copy-done.27, bf16[1280,3072]{1,0:T(8,128)(2,1)} %copy-done.21, bf16[3072,768]{1,0:T(8,128)(2,1)} %bitcast.233), kind=kOutput, calls=%fused_computation.72 | convolution fusion | flops 6040780800 | bytes 20447232 | tf_op jit(solution)/shard_map/dot_general | solution.py:40
  385.3 36.4 %shard_map.411 = bf16[1280,2304]{1,0:T(8,128)(2,1)} custom-call(s32[1280,1]{1,0:T(8,128)} %copy-done, s32[10,1,256]{2,1,0:T(1,128)} %copy-done.1, bf16[1280,2304]{1,0:T(8,128)(2,1)} %copy-done.2, bf16[1280,768]{1,0:T(8,128)(2,1)} %convolution_convert_fusion.1.refs_3_, f32[1280,128]{1,0:T(8,128)} %copy-done.5), custom_call_target="tpu_custom_call" | custom-call | flops 5033164800 | bytes 18000000 | tf_op jit(solution)/shard_map/pallas_call | solution.py:216
  427.9 8.0 %fusion.136 = f32[2304,768]{1,0:T(8,128)} fusion(bf16[1280,2304]{1,0:T(8,128)(2,1)S(1)} %copy-done.22, f32[1280,768]{0,1:T(8,128)S(1)} %copy-done.9, f32[768]{0:T(1024)S(1)} %copy-done.112, f32[768]{0:T(1024)S(1)} %copy-done.74, f32[1280]{0:T(1024)S(1)} %copy-done.67, f32[1280]{0:T(1024)S(1)} %copy-done.59), kind=kOutput, calls=%fused_computation.321 | convolution fusion | flops 4534763520 | bytes 16924672 | tf_op jit(solution)/shard_map/dot_general | solution.py:44
  436.0 8.0 %pad_maximum_fusion = f32[3072,768]{1,0:T(8,128)} fusion(f32[768,768]{1,0:T(8,128)} %fusion.67, f32[2304,768]{1,0:T(8,128)} %fusion.136), kind=kLoop, calls=%fused_computation.23 | loop fusion | flops 2359296 | bytes 18874368 | tf_op jit(solution)/shard_map/concatenate | solution.py:739
  467.6 9.8 %convolution_add_fusion.3 = f32[1280,768]{0,1:T(8,128)} fusion(f32[1280,768]{0,1:T(8,128)S(1)} %copy-done.26, bf16[1280,2304]{1,0:T(8,128)(2,1)} %shard_map.411, bf16[2304,768]{1,0:T(8,128)(2,1)S(1)} %bitcast.210), kind=kOutput, calls=%fused_computation.73 | convolution fusion | flops 4530831360 | bytes 17301504 | tf_op jit(solution)/shard_map/dot_general | solution.py:40
  502.1 6.1 convolution_convert_fusion
  537.7 42.5 %collective-permute-done.10 = bf16[2,2,2,96,768]{4,3,0,1,2:T(8,128)(2,1)} collective-permute-done((bf16[2,2,2,96,768]{4,3,0,1,2:T(8,128)(2,1)}, bf16[2,2,2,96,768]{4,3,0,1,2:T(8,128)(2,1)}, u32[]{:S(2)}, u32[]{:S(2)}) %collective-permute-start.10) | collective-permute-done | bytes 1179680 | tf_op jit(solution)/shard_map/ppermute | solution.py:252
  585.0 13.1 %collective-permute-done.11 = bf16[2,2,96,768]{3,2,0,1:T(8,128)(2,1)S(1)} collective-permute-done((bf16[2,2,96,768]{3,2,0,1:T(8,128)(2,1)S(1)}, bf16[2,2,96,768]{3,2,0,1:T(8,128)(2,1)S(1)}, u32[]{:S(2)}, u32[]{:S(2)}) %collective-permute-start.11) | collective-permute-done | bytes 589856 | tf_op jit(solution)/shard_map/ppermute | solution.py:252
  602.2 7.4 %collective-permute-done.12 = bf16[2,96,768]{2,1,0:T(8,128)(2,1)S(1)} collective-permute-done((bf16[2,96,768]{2,1,0:T(8,128)(2,1)S(1)}, bf16[2,96,768]{2,1,0:T(8,128)(2,1)S(1)}, u32[]{:S(2)}, u32[]{:S(2)}) %collective-permute-start.12) | collective-permute-done | bytes 294944 | tf_op jit(solution)/shard_map/ppermute | solution.py:252
  611.5 6.3 collective-permute-done.13
  620.0 6.4 conditional.3
  620.0 6.4 fusion.5
  627.1 6.2 multiply_subtract_fusion
  (492 shorter events, 247.6 us)
Async XLA Ops:
  133.9 85.2 %copy-start.33 = (bf16[4,8,48,128]{3,1,2,0:T(8,128)(2,1)}, bf16[4,8,48,128]{3,1,2,0:T(8,128)(2,1)S(1)}, u32[]{:S(2)}) copy-start(bf16[4,8,48,128]{3,1,2,0:T(8,128)(2,1)S(1)} %copy.197) | copy-start | bytes 1179652
  135.3 55.3 %copy-start.92 = (f32[3072]{0:T(1024)}, f32[3072]{0:T(1024)S(1)}, u32[]{:S(2)}) copy-start(f32[3072]{0:T(1024)S(1)} %slice.238) | copy-start | bytes 36868
  135.4 52.6 %copy-start.73 = (f32[768]{0:T(1024)}, f32[768]{0:T(1024)S(1)}, u32[]{:S(2)}) copy-start(f32[768]{0:T(1024)S(1)} %get-tuple-element.157) | copy-start | bytes 9220
  135.4 52.6 %copy-start.111 = (f32[768]{0:T(1024)}, f32[768]{0:T(1024)S(1)}, u32[]{:S(2)}) copy-start(f32[768]{0:T(1024)S(1)} %get-tuple-element.156) | copy-start | bytes 9220
  135.4 68.9 %copy-start.76 = (f32[768]{0:T(1024)}, f32[768]{0:T(1024)S(1)}, u32[]{:S(2)}) copy-start(f32[768]{0:T(1024)S(1)} %get-tuple-element.152) | copy-start | bytes 9220
  135.4 68.9 %copy-start.113 = (f32[768]{0:T(1024)}, f32[768]{0:T(1024)S(1)}, u32[]{:S(2)}) copy-start(f32[768]{0:T(1024)S(1)} %get-tuple-element.151) | copy-start | bytes 9220
  155.9 81.6 %all-gather.6.cloned.1.call-start = ((), (), s32[]{:S(2)}) async-start(), calls=%async_computation.5 | async-start | bytes 1638400 | tf_op jit(solution)/shard_map/all_gather | solution.py:620
  319.4 16.7 %collective-permute-start = (bf16[2,2,2,2,96,768]{5,4,0,1,2,3:T(8,128)(2,1)S(1)}, bf16[2,2,2,2,96,768]{5,4,0,1,2,3:T(8,128)(2,1)}, u32[]{:S(2)}, u32[]{:S(2)}) collective-permute-start(bf16[2,2,2,2,96,768]{5,4,0,1,2,3:T(8,128)(2,1)S(1)} %fusion.32), channel_id=1, source_target_pairs={{0,1},{1,0},{2,3},{3,2},{4,5},{5,4},{6,7},{7,6},{8,9},{9,8},{10,11... | collective-permute-start | bytes 7077896 | tf_op jit(solution)/shard_map/ppermute | solution.py:252
  347.0 16.5 %collective-permute-start.1 = (bf16[2,2,2,2,96,768]{5,4,0,1,3,2:T(8,128)(2,1)S(1)}, bf16[2,2,2,2,96,768]{5,4,0,1,3,2:T(8,128)(2,1)}, u32[]{:S(2)}, u32[]{:S(2)}) collective-permute-start(bf16[2,2,2,2,96,768]{5,4,0,1,3,2:T(8,128)(2,1)S(1)} %fusion.33), channel_id=1, source_target_pairs={{0,1},{1,0},{2,3},{3,2},{4,5},{5,4},{6,7},{7,6},{8,9},{9,8},{10,11... | collective-permute-start | bytes 7077896 | tf_op jit(solution)/shard_map/ppermute | solution.py:252
  351.9 28.5 %collective-permute-start.2 = (bf16[2,2,2,96,768]{4,3,0,1,2:T(8,128)(2,1)}, bf16[2,2,2,96,768]{4,3,0,1,2:T(8,128)(2,1)}, u32[]{:S(2)}, u32[]{:S(2)}) collective-permute-start(bf16[2,2,2,96,768]{4,3,0,1,2:T(8,128)(2,1)} %fusion.47), channel_id=1, source_target_pairs={{0,2},{1,3},{2,0},{3,1},{4,6},{5,7},{6,4},{7,5},{8,10},{9,11},{10,... | collective-permute-start | bytes 3538952 | tf_op jit(solution)/shard_map/ppermute | solution.py:252
  381.5 46.4 %collective-permute-start.4 = (bf16[2,2,2,96,768]{4,3,0,1,2:T(8,128)(2,1)}, bf16[2,2,2,96,768]{4,3,0,1,2:T(8,128)(2,1)}, u32[]{:S(2)}, u32[]{:S(2)}) collective-permute-start(bf16[2,2,2,96,768]{4,3,0,1,2:T(8,128)(2,1)} %fusion.48), channel_id=1, source_target_pairs={{0,4},{4,0},{8,12},{12,8},{16,20},{20,16},{24,28},{28,24},{1,5},{5... | collective-permute-start | bytes 3538952 | tf_op jit(solution)/shard_map/ppermute | solution.py:252
  384.6 42.5 %collective-permute-start.3 = (bf16[2,2,96,768]{3,2,0,1:T(8,128)(2,1)S(1)}, bf16[2,2,96,768]{3,2,0,1:T(8,128)(2,1)S(1)}, u32[]{:S(2)}, u32[]{:S(2)}) collective-permute-start(bf16[2,2,96,768]{3,2,0,1:T(8,128)(2,1)S(1)} %fusion.75), channel_id=1, source_target_pairs={{0,4},{4,0},{8,12},{12,8},{16,20},{20,16},{24,28},{28,24},{1,5},{5... | collective-permute-start | bytes 1769480 | tf_op jit(solution)/shard_map/ppermute | solution.py:252
  448.0 35.6 %collective-permute-start.7 = (bf16[2,2,2,2,96,768]{5,4,0,1,2,3:T(8,128)(2,1)}, bf16[2,2,2,2,96,768]{5,4,0,1,2,3:T(8,128)(2,1)}, u32[]{:S(2)}, u32[]{:S(2)}) collective-permute-start(bf16[2,2,2,2,96,768]{5,4,0,1,2,3:T(8,128)(2,1)} %fusion.34), channel_id=1, source_target_pairs={{0,1},{1,0},{2,3},{3,2},{4,5},{5,4},{6,7},{7,6},{8,9},{9,8},{10,11... | collective-permute-start | bytes 7077896 | tf_op jit(solution)/shard_map/ppermute | solution.py:252
  450.7 66.8 %all-to-all-start = ((bf16[32,2,3648]{2,1,0:T(2,128)(2,1)}), bf16[32,2,3648]{2,1,0:T(2,128)(2,1)}, u32[]{:S(2)}, u32[]{:S(2)}) async-start(bf16[32,2,3648]{2,1,0:T(2,128)(2,1)} %reshape.547), calls=%async_computation.1 | async-start | bytes 950272 | tf_op jit(solution)/shard_map/all_to_all | solution.py:698
  461.8 21.0 %collective-permute-start.5 = (bf16[2,96,768]{2,1,0:T(8,128)(2,1)}, bf16[2,96,768]{2,1,0:T(8,128)(2,1)}, u32[]{:S(2)}, u32[]{:S(2)}) collective-permute-start(bf16[2,96,768]{2,1,0:T(8,128)(2,1)} %fusion.87), channel_id=1, source_target_pairs={{0,8},{4,12},{8,0},{12,4},{16,24},{20,28},{24,16},{28,20},{1,9},{5... | collective-permute-start | bytes 884744 | tf_op jit(solution)/shard_map/ppermute | solution.py:252
  465.9 16.9 %collective-permute-start.6 = (bf16[2,2,96,768]{3,2,0,1:T(8,128)(2,1)S(1)}, bf16[2,2,96,768]{3,2,0,1:T(8,128)(2,1)S(1)}, u32[]{:S(2)}, u32[]{:S(2)}) collective-permute-start(bf16[2,2,96,768]{3,2,0,1:T(8,128)(2,1)S(1)} %fusion.76), channel_id=1, source_target_pairs={{0,2},{1,3},{2,0},{3,1},{4,6},{5,7},{6,4},{7,5},{8,10},{9,11},{10,... | collective-permute-start | bytes 1769480 | tf_op jit(solution)/shard_map/ppermute | solution.py:252
  499.9 17.6 %collective-permute-start.9 = (bf16[2,96,768]{2,1,0:T(8,128)(2,1)S(1)}, bf16[2,96,768]{2,1,0:T(8,128)(2,1)}, u32[]{:S(2)}, u32[]{:S(2)}) collective-permute-start(bf16[2,96,768]{2,1,0:T(8,128)(2,1)S(1)} %fusion.88), channel_id=1, source_target_pairs={{0,8},{4,12},{8,0},{12,4},{16,24},{20,28},{24,16},{28,20},{1,9},{5... | collective-permute-start | bytes 884744 | tf_op jit(solution)/shard_map/ppermute | solution.py:252
  508.3 9.2 %collective-permute-start.8 = (bf16[96,768]{1,0:T(8,128)(2,1)S(1)}, bf16[96,768]{1,0:T(8,128)(2,1)S(1)}, u32[]{:S(2)}, u32[]{:S(2)}) collective-permute-start(bf16[96,768]{1,0:T(8,128)(2,1)S(1)} %fusion.103), channel_id=1, source_target_pairs={{0,16},{4,20},{8,24},{12,28},{16,0},{20,4},{24,8},{28,12},{1,17},{... | collective-permute-start | bytes 442376 | tf_op jit(solution)/shard_map/ppermute | solution.py:252
  517.5 101.3 %all-to-all-start.1 = ((bf16[32,51,768]{2,1,0:T(8,128)(2,1)}), bf16[32,51,768]{2,1,0:T(8,128)(2,1)}, u32[]{:S(2)}, u32[]{:S(2)}) async-start(bf16[32,51,768]{2,1,0:T(8,128)(2,1)} %pad_maximum_fusion.1), calls=%async_computation.2 | async-start | bytes 5505024 | tf_op jit(solution)/shard_map/all_to_all | solution.py:773
  528.8 51.4 %collective-permute-start.10 = (bf16[2,2,2,96,768]{4,3,0,1,2:T(8,128)(2,1)}, bf16[2,2,2,96,768]{4,3,0,1,2:T(8,128)(2,1)}, u32[]{:S(2)}, u32[]{:S(2)}) collective-permute-start(bf16[2,2,2,96,768]{4,3,0,1,2:T(8,128)(2,1)} %fusion.49), channel_id=1, source_target_pairs={{0,2},{1,3},{2,0},{3,1},{4,6},{5,7},{6,4},{7,5},{8,10},{9,11},{10,... | collective-permute-start | bytes 3538952 | tf_op jit(solution)/shard_map/ppermute | solution.py:252
  582.6 15.4 %collective-permute-start.11 = (bf16[2,2,96,768]{3,2,0,1:T(8,128)(2,1)S(1)}, bf16[2,2,96,768]{3,2,0,1:T(8,128)(2,1)S(1)}, u32[]{:S(2)}, u32[]{:S(2)}) collective-permute-start(bf16[2,2,96,768]{3,2,0,1:T(8,128)(2,1)S(1)} %fusion.77), channel_id=1, source_target_pairs={{0,4},{4,0},{8,12},{12,8},{16,20},{20,16},{24,28},{28,24},{1,5},{5... | collective-permute-start | bytes 1769480 | tf_op jit(solution)/shard_map/ppermute | solution.py:252
  598.3 11.4 %collective-permute-start.12 = (bf16[2,96,768]{2,1,0:T(8,128)(2,1)S(1)}, bf16[2,96,768]{2,1,0:T(8,128)(2,1)S(1)}, u32[]{:S(2)}, u32[]{:S(2)}) collective-permute-start(bf16[2,96,768]{2,1,0:T(8,128)(2,1)S(1)} %fusion.89), channel_id=1, source_target_pairs={{0,8},{4,12},{8,0},{12,4},{16,24},{20,28},{24,16},{28,20},{1,9},{5... | collective-permute-start | bytes 884744 | tf_op jit(solution)/shard_map/ppermute | solution.py:252
  598.4 12.1 %collective-permute-start.14 = (bf16[96,768]{1,0:T(8,128)(2,1)S(1)}, bf16[96,768]{1,0:T(8,128)(2,1)S(1)}, u32[]{:S(2)}, u32[]{:S(2)}) collective-permute-start(bf16[96,768]{1,0:T(8,128)(2,1)S(1)} %fusion.105), channel_id=1, source_target_pairs={{0,16},{4,20},{8,24},{12,28},{16,0},{20,4},{24,8},{28,12},{1,17},{... | collective-permute-start | bytes 442376 | tf_op jit(solution)/shard_map/ppermute | solution.py:252
  609.8 8.1 %collective-permute-start.13 = (bf16[96,768]{1,0:T(8,128)(2,1)S(1)}, bf16[96,768]{1,0:T(8,128)(2,1)S(1)}, u32[]{:S(2)}, u32[]{:S(2)}) collective-permute-start(bf16[96,768]{1,0:T(8,128)(2,1)S(1)} %fusion.104), channel_id=1, source_target_pairs={{0,16},{4,20},{8,24},{12,28},{16,0},{20,4},{24,8},{28,12},{1,17},{... | collective-permute-start | bytes 442376 | tf_op jit(solution)/shard_map/ppermute | solution.py:252
  (124 other events, 1211.0 us)
Sparse Core Ops, SparseCore 1:
  219.2 18.3 all-gather.5

commit v3 on v2

--- a/solution.py
+++ b/solution.py
@@ -229,37 +229,6 @@
             flops=10 * count * WIN * 128 * HEADS, bytes_accessed=18000000, transcendentals=0
         ),
     )(segment_column, segment_windows, mixed, upstream, kept)
-
-
-def bits_of(axis_name):
-    return [(axis_name, b) for b in range(lax.axis_size(axis_name).bit_length() - 1)]
-
-
-def cut_chunks(gradient):
-    names = bits_of("grp")[::-1] + bits_of("psg")[::-1]
-    rows = gradient.shape[0] >> len(names)
-    return gradient.reshape((2,) * len(names) + (rows, gradient.shape[1])), names
-
-
-def halve_start(state, step):
-    parts, names = state
-    axis_name, bit = step
-    at = names.index(step)
-    mine = (lax.axis_index(axis_name) >> bit) & 1
-    pairs = [(i, i ^ (1 << bit)) for i in range(lax.axis_size(axis_name))]
-    sent = lax.dynamic_index_in_dim(parts, 1 - mine, at, keepdims=False).astype(BF)
-    held = lax.dynamic_index_in_dim(parts, mine, at, keepdims=False)
-    return held, lax.ppermute(sent, axis_name, pairs), names[:at] + names[at + 1 :]
-
-
-def halve_end(flying):
-    held, received, names = flying
-    return held + received.astype(F32), names
-
-
-def gate(value, *flying):
-    value, received = lax.optimization_barrier((value, tuple(f[1] for f in flying)))
-    return value, *((f[0], r, f[2]) for f, r in zip(flying, received))
 
 
 def place_of():
@@ -474,6 +443,159 @@
         ),
     )(*sources, needed, notes, table)
     return gathered, noted, arrived, rank
+
+
+def reduce_plan(order, group):
+    held = [0]
+    for bit in reversed(order):
+        held = [m | (1 << bit) for m in held] + held
+    steps = []
+    for step in range(len(order) + 1):
+        if step:
+            held = [m for m in held if not (m >> order[step - 1]) & 1]
+        steps.append([held[i : i + group] for i in range(0, len(held), group)])
+    return steps
+
+
+def reduce_kernel(devices, pieces, spread, *refs):
+    count = len({p[0] for p in pieces})
+    sources, rows_in = refs[:count], refs[count]
+    outs, rows_out = refs[count + 1 : 2 * count + 1], refs[2 * count + 1]
+    held, landed = refs[2 * count + 2 : 3 * count + 2], refs[3 * count + 2 : 4 * count + 2]
+    arrive, leave, load, rows_sem, own_sem = refs[4 * count + 2 :]
+    me = place_of()
+    group = max(devices // 16, 1)
+    greet_all(devices, me)
+
+    def push(source, target_ref, target, send, recv):
+        pltpu.make_async_remote_copy(
+            src_ref=source,
+            dst_ref=target_ref,
+            send_sem=send,
+            recv_sem=recv,
+            device_id=mesh_place(target),
+            device_id_type=pl.DeviceIdType.MESH,
+        ).start()
+
+    def settle(some, semaphore):
+        pltpu.make_async_copy(some, some, semaphore).wait()
+
+    plans, slots, places, numbers = [], [], [], []
+    for piece in pieces:
+        plan = reduce_plan(piece[3], group)
+        slots.append({m: i for i, m in enumerate(sum(plan[0], []))})
+        place, number, at, count = {}, {}, 0, 0
+        for step, groups in enumerate(plan):
+            for masks in groups:
+                for mask in masks:
+                    place[step, mask], number[step, mask] = at, count
+                    at += 1
+                count += 1
+        plans.append(plan)
+        places.append(place)
+        numbers.append(number)
+
+    def rows_of(piece):
+        return pl.ds(pieces[piece][1], pieces[piece][2])
+
+    def send(piece, step, mask, bit, source):
+        which = pieces[piece][0]
+        kept = mask & ~(1 << bit)
+        push(
+            source,
+            landed[which].at[places[piece][step, kept], rows_of(piece)],
+            flipped(me, 1 << bit),
+            leave.at[piece],
+            arrive.at[piece, numbers[piece][step, kept]],
+        )
+
+    order = sorted(range(1, devices), key=lambda m: -bin(m).count("1"))
+
+    def send_rows(amount):
+        for _ in range(min(amount, len(order))):
+            target = flipped(me, order.pop(0))
+            push(rows_in.at[target], rows_out.at[me], target, rows_sem.at[0], rows_sem.at[1])
+
+    own_rows = pltpu.make_async_copy(rows_in.at[me], rows_out.at[me], own_sem)
+    own_rows.start()
+    send_rows(spread[0])
+    for masks in plans[0][0]:
+        for piece in range(len(pieces)):
+            which = pieces[piece][0]
+            for mask in plans[piece][0][plans[0][0].index(masks)]:
+                source = sources[which].at[flipped(me, mask | 1), rows_of(piece)]
+                send(piece, 0, mask | 1, 0, source)
+    for piece in range(len(pieces)):
+        which = pieces[piece][0]
+        for mask in slots[piece]:
+            pltpu.make_async_copy(
+                sources[which].at[flipped(me, mask), rows_of(piece)],
+                held[which].at[slots[piece][mask], rows_of(piece)],
+                load.at[piece],
+            ).start()
+    turn = 1
+    for step in range(len(pieces[0][3]) + 1):
+        for at in range(len(plans[0][step])):
+            for piece in range(len(pieces)):
+                which, _, _, bits = pieces[piece]
+                rows = rows_of(piece)
+                if step == 0 and at == 0:
+                    settle(held[which].at[pl.ds(0, devices // 2), rows], load.at[piece])
+                masks = plans[piece][step][at]
+                some = landed[which].at[pl.ds(0, len(masks)), rows]
+                settle(some, arrive.at[piece, numbers[piece][step, masks[0]]])
+                for mask in masks:
+                    slot = slots[piece][mask]
+                    total = held[which][slot, rows].astype(F32)
+                    total = total + landed[which][places[piece][step, mask], rows].astype(F32)
+                    if step == len(bits):
+                        outs[which][rows] = total
+                        continue
+                    held[which][slot, rows] = total.astype(held[which].dtype)
+                    if (mask >> bits[step]) & 1:
+                        send(piece, step + 1, mask, bits[step], held[which].at[slot, rows])
+            send_rows(spread[turn] if turn < len(spread) else 0)
+            turn += 1
+    send_rows(devices)
+    for piece in range(len(pieces)):
+        which = pieces[piece][0]
+        settle(landed[which].at[pl.ds(0, devices - 1), rows_of(piece)], leave.at[piece])
+    own_rows.wait()
+    for i in range(2):
+        settle(rows_out.at[pl.ds(0, devices - 1)], rows_sem.at[i])
+
+
+def reduce_all(sources, rows_in):
+    devices = rows_in.shape[0]
+    bits = devices.bit_length() - 1
+    high = list(range(3, bits))
+    one, other = (1, 2, *high), (2, 1, *high)
+    pieces = []
+    for i in (0, 2, 1, 3, 4):
+        rows = sources[i].shape[1]
+        cut = rows // 32 * 16 if i == 1 else 0
+        pieces.append((i, cut, rows - cut, one if i in (0, 1, 3) else other))
+        if cut:
+            pieces.append((i, 0, cut, other))
+    spread = [6] + [2] * devices
+    count = max(sum(map(len, reduce_plan(p[3], max(devices // 16, 1)))) for p in pieces)
+    anywhere = pl.BlockSpec(memory_space=pl.ANY)
+    inside = pl.BlockSpec(memory_space=pltpu.VMEM)
+    dma = pltpu.SemaphoreType.DMA
+    *reduced, arrived = pl.pallas_call(
+        lambda *refs: reduce_kernel(devices, pieces, spread, *refs),
+        in_specs=[anywhere] * (len(sources) + 1),
+        out_specs=[inside] * len(sources) + [anywhere],
+        out_shape=[jax.ShapeDtypeStruct(s.shape[1:], F32) for s in sources]
+        + [jax.ShapeDtypeStruct(rows_in.shape, rows_in.dtype)],
+        scratch_shapes=[pltpu.VMEM((devices // 2, *s.shape[1:]), s.dtype) for s in sources]
+        + [pltpu.VMEM((devices - 1, *s.shape[1:]), s.dtype) for s in sources]
+        + [dma((len(pieces), count)), dma((len(pieces),)), dma((len(pieces),)), dma((2,)), dma],
+        compiler_params=pltpu.CompilerParams(
+            collective_id=1, has_side_effects=True, vmem_limit_bytes=48 * 2**20
+        ),
+    )(*sources, rows_in)
+    return reduced, arrived
 
 
 def adam_update(weight, moment, second, gradient, rate, count_steps):
@@ -682,72 +804,29 @@
     picks = one_hot(assignments[0], NCENT)
     centroid_part = contract_rows(picks, own_passage)
     count_part = jnp.sum(picks.astype(F32), axis=0)
-    count_high, count_low = split_two(count_part)
-    early = jnp.concatenate(
-        [
-            centroid_part.astype(BF).reshape(devices, -1),
-            grad_head.astype(BF).reshape(devices, -1),
-            count_high.reshape(devices, -1),
-            count_low.reshape(devices, -1),
-        ]
-        + [jnp.broadcast_to(v, (devices, 1)) for v in split_three(numerator)],
-        axis=1,
-    )
-    early_width = early.shape[1]
-    early = jnp.pad(early, ((0, 0), (0, -early_width % 128)))
-    early = lax.all_to_all(early, ALL, split_axis=0, concat_axis=0, tiled=True)
-    early = jnp.sum(early.astype(F32), axis=0)
-    cent_rows = NCENT // devices
-    at = cent_rows * DC
-    centroid_sums = early[:at].reshape(cent_rows, DC)
-    head_reduced = early[at : at + head_rows * DC].reshape(head_rows, DC)
-    at += head_rows * DC
-    centroid_counts = early[at : at + cent_rows] + early[at + cent_rows : at + 2 * cent_rows]
-    at += 2 * cent_rows
-    loss = (early[at] + early[at + 1] + early[at + 2]) / pair_floor
 
     grad_hidden_two = contract_cols(grad_proj, head_full)
     grad_sum_two, grad_gain_two, grad_shift_two = norm_back(grad_hidden_two, norm_two, pieces[8])
     grad_two_low = grad_sum_two.astype(BF)
-    member_bits, group_bits = bits_of("psg"), bits_of("grp")
-    member_first = member_bits + group_bits
-    group_first = member_bits[:1] + group_bits[:1] + member_bits[1:] + group_bits[1:]
-    down = halve_start(cut_chunks(contract_rows(activated, grad_two_low)), member_first[0])
+    grad_down_rows = contract_rows(activated, grad_two_low)
     grad_activated = contract_cols(grad_two_low, down_rows)
     normal_cdf = 0.5 * (1.0 + lax.erf(inner / math.sqrt(2.0)))
     normal_pdf = jnp.exp(-0.5 * inner * inner) / math.sqrt(2.0 * math.pi)
     grad_inner = (grad_activated * (normal_cdf + inner * normal_pdf)).astype(BF)
-    grad_inner, down = gate(grad_inner, down)
-    down = halve_start(halve_end(down), member_first[1])
-    up = halve_start(cut_chunks(contract_rows(grad_inner, input_one)), group_first[0])
+    grad_up_rows = contract_rows(grad_inner, input_one)
     grad_bias_up = jnp.sum(grad_inner.astype(F32), axis=0)
     grad_hidden_one = grad_sum_two + matmul(grad_inner, up_rows)
-    grad_hidden_one, up = gate(grad_hidden_one, up)
-    up = halve_start(halve_end(up), group_first[1])
     grad_sum_one, grad_gain_one, grad_shift_one = norm_back(grad_hidden_one, norm_one, pieces[5])
     grad_one_low = grad_sum_one.astype(BF)
     grad_out_rows = contract_rows(grad_one_low, context)
     grad_context = matmul(grad_one_low, attn_rows[3 * D :]).astype(BF)
-    grad_context, down = gate(grad_context, down)
-    down = halve_start(halve_end(down), member_first[2])
     grad_mixed = attention_backward(segment_column, segment_windows, mixed, grad_context, kept)
-    grad_mixed, down, up = gate(grad_mixed, down, up)
-    down = halve_start(halve_end(down), member_first[3])
-    up = halve_start(halve_end(up), group_first[2])
     grad_qkv_rows = contract_rows(grad_mixed, input_zero)
-    attn = halve_start(
-        cut_chunks(jnp.concatenate([grad_qkv_rows, grad_out_rows], axis=0)), member_first[0]
-    )
     grad_mixed_sum = jnp.sum(grad_mixed.astype(F32), axis=0)
     grad_hidden_zero = grad_sum_one + matmul(grad_mixed, attn_rows[: 3 * D])
-    grad_hidden_zero, down, up, attn = gate(grad_hidden_zero, down, up, attn)
-    down = halve_start(halve_end(down), member_first[4])
-    up = halve_start(halve_end(up), group_first[3])
-    attn = halve_start(halve_end(attn), member_first[1])
     grad_embedded, grad_gain_zero, grad_shift_zero = norm_back(
         grad_hidden_zero, norm_zero, pieces[0]
     )
-
     grad_low = grad_embedded.astype(BF)
     grad_positions = contract_rows(position_hot, grad_low)
     grad_slots = contract_rows(slot_hot, grad_low).astype(BF).reshape(devices, capacity, D)
@@ -766,23 +845,37 @@
             grad_shift_two,
             grad_bias_up,
         ]
-    ).reshape(devices, small_size)
-    grad_small = jnp.pad(grad_small.astype(BF), ((0, 0), (0, -small_size % D)))
-    grad_slots = jnp.concatenate([grad_slots, grad_small.reshape(devices, -1, D)], axis=1)
-    grad_slots, down, up = gate(grad_slots, down, up)
-    grad_slots = lax.all_to_all(grad_slots, ALL, split_axis=0, concat_axis=0, tiled=True)
-    small_reduced = jnp.sum(grad_slots[:, capacity:].astype(F32), axis=0).reshape(-1)[:small_size]
-    grad_slots = grad_slots[:, :capacity]
-    down = halve_end(down)
-    up = halve_end(halve_start(halve_end(up), group_first[4]))
-    attn = halve_end(attn)
-    for step in member_first[2:]:
-        attn = halve_end(halve_start(attn, step))
-    for step in member_first[5:]:
-        down = halve_end(halve_start(down, step))
-    for step in group_first[5:]:
-        up = halve_end(halve_start(up, step))
-    down_reduced, up_reduced, attn_reduced = down[0], up[0], attn[0]
+    )
+
+    def chunks(rows):
+        rows = rows.astype(BF).reshape(devices, matrix_rows, D)
+        return jnp.pad(rows, ((0, 0), (0, -matrix_rows % 16), (0, 0)))
+
+    def side_by_side(parts, sublanes):
+        joined = jnp.concatenate([p.reshape(devices, -1) for p in parts], axis=1)
+        joined = jnp.pad(joined, ((0, 0), (0, -joined.shape[1] % (sublanes * 128))))
+        return joined.reshape(devices, -1, 128)
+
+    reduced, grad_slots = reduce_all(
+        [
+            chunks(jnp.concatenate([grad_qkv_rows.astype(BF), grad_out_rows.astype(BF)])),
+            chunks(grad_up_rows),
+            chunks(grad_down_rows),
+            side_by_side([centroid_part.astype(BF), grad_head.astype(BF)], 16),
+            side_by_side(
+                [grad_small, count_part, jnp.broadcast_to(numerator, (devices, 1))], 8
+            ),
+        ],
+        grad_slots,
+    )
+    attn_reduced, up_reduced, down_reduced = (r[:matrix_rows] for r in reduced[:3])
+    wide, fine = reduced[3].reshape(-1), reduced[4].reshape(-1)
+    centroid_rows = NCENT // devices
+    centroid_sums = wide[: centroid_rows * DC].reshape(centroid_rows, DC)
+    head_reduced = wide[centroid_rows * DC :][: head_rows * DC].reshape(head_rows, DC)
+    small_reduced = fine[:small_size]
+    centroid_counts = fine[small_size:][:centroid_rows]
+    loss = fine[small_size + centroid_rows] / pair_floor
 
     def whole_table():
         table = jnp.zeros((shard_rows * devices, D), F32).at[tokens].add(grad_embedded)

time: 653 us -> 579 us (0.89)
  Pallas kernels: 158 us -> 274 us
  waiting for transfers between devices: 91.3 us -> 10.2 us
  other arithmetic: 96.5 us -> 49.2 us
  local copies, waits for them, and re-layouts: 81 us -> 51 us
  starting transfers between devices: 24.6 us -> 0.04 us
  between operations: 27.9 us -> 21.2 us
    pallas_call x0 -> x1, Pallas kernels: none -> 116 us  [reduce_all(): pl.pallas_call(lambda *refs: reduce_kernel(devices, pieces, spread, *refs...]
    ppermute x15 -> x0, waiting for transfers between devices: 79.8 us -> none  [halve_start(): lax.ppermute(sent, axis_name, pairs)]
    add x13 -> x1, other arithmetic: 21 us -> 0.01 us  [on_device(): segment = jnp.concatenate([passage_segment, PPD + query_place // SEG])]
    unnamed x285 -> x245, local copies, waits for them, and re-layouts: 32.9 us -> 16.6 us
    ppermute x15 -> x0, starting transfers between devices: 15.4 us -> none  [halve_start(): lax.ppermute(sent, axis_name, pairs)]
    convert_element_type x16 -> x0, local copies, waits for them, and re-layouts: 9.36 us -> none  [the longest x15 9.16 us: halve_start(): lax.dynamic_index_in_dim(parts, 1 - mine, at, keepdims=False).astype(BF)]
    all_to_all x2 -> x0, starting transfers between devices: 9.1 us -> none  [the longest x1 4.77 us: on_device(): early = lax.all_to_all(early, ALL, split_axis=0, concat_axis=0, tiled=True)]
    reduce_sum x3 -> x1, other arithmetic: 12.5 us -> 4.59 us  [norm_back(): return (back, jnp.sum(upstream * normed, axis=0), jnp.sum(upstream, axis=0))]
  transfers between devices with their start and end apart: 18 -> 1, of which waited for: 7 -> 1; matrix products, arithmetic and copies ran while one was open for 19% -> 1% of each run, Pallas kernels for 6% -> 0%
where the time goes in v3:
time: 579 us; the launch traced here: 569 us
  Pallas kernels  274 us (47%)
  matrix products  157 us (27%)
  local copies, waits for them, and re-layouts  51 us (9%)
  other arithmetic  49.2 us (8%)
  between operations  21.2 us (4%)
  waiting for transfers between devices  10.2 us (2%)
    pallas_call x1, Pallas kernels, reduce_all(): pl.pallas_call(lambda *refs: reduce_kernel(devices, pieces, spread, *refs...  116 us
    pallas_call x1, Pallas kernels, gather_all(): pl.pallas_call(lambda *refs: gather_kernel(devices, pieces, *refs), in_sp...  108 us
    dot_general x10, matrix products, matmul(): return jnp.dot(lhs_mat, rhs_mat, preferred_element_type=jnp.float32)  54.2 us
    dot_general x11, matrix products, contract_rows(): lax.dot_general(lhs_mat, rhs_mat, (((0,), (0,)), ((), ())), preferred_ele...  53.5 us
    dot_general x6, matrix products, contract_cols(): lax.dot_general(lhs_mat, rhs_mat, (((1,), (1,)), ((), ())), preferred_ele...  41.6 us
    pallas_call x1, Pallas kernels, attention_backward(): pl.pallas_call(lambda *refs: attn_backward_kernel(count, blocks, *refs),...  36.6 us
    unnamed x245, local copies, waits for them, and re-layouts  16.6 us
    pallas_call x1, Pallas kernels, attention_forward(): pl.pallas_call(lambda *refs: attn_forward_kernel(count, *refs), grid=(blo...  13.8 us
  transfers between devices with their start and end apart: 1, of which 1 were waited for; matrix products, arithmetic and copies ran while one was open for 1% of the time, Pallas kernels for 0%

profile of v3, /device:TPU:0, one launch (start us, length us, event | category | flops | bytes accessed | tf_op | source)
XLA Modules:
  0.0 568.6 jit_solution(9164982015461781802)
XLA Ops:
  19.9 107.7 %shard_map.409 = (bf16[32,96,768]{2,1,0:T(8,128)(2,1)}, bf16[32,96,768]{2,1,0:T(8,128)(2,1)}, bf16[32,96,768]{2,1,0:T(8,128)(2,1)}, bf16[32,48,128]{2,1,0:T(8,12...) custom-call(bf16[96,768]{1,0:T(8,128)(2,1)S(1)} %get-tuple-element.167.refs_0_, ...), custom_call_target="tpu_custom_call" | custom-call | tf_op jit(solution)/shard_map/pallas_call | solution.py:421
  144.4 8.4 %conditional.2 = (f32[1280,768]{1,0:T(8,128)}) conditional(s32[]{:T(128)} %convert_element_type.229, (bf16[32,48,768]{2,1,0:T(8,128)(2,1)}, bf16[1280,1536]{1,0:T(8,128)(2,1)}) %tuple.20, (f32[960,768]{1,0:T(8,128)S(1)}, s32[1280]{0:T(1024)S(1)}) %tuple.94), branch_computations={%region_5.6_spmd, %region_6.7_spmd} | conditional | flops 3019898880 | bytes 160264224 | solution.py:710
  144.4 8.0 %fusion.132 = f32[1280,768]{1,0:T(8,128)} fusion(bf16[1280,1536]{1,0:T(8,128)(2,1)} %get-tuple-element.24, bf16[1536,768]{1,0:T(8,128)(2,1)} %bitcast.159), kind=kOutput, calls=%fused_computation.284 | convolution fusion | flops 3019898880 | bytes 10223616 | tf_op jit(solution)/shard_map/cond/branch_0_fun/dot_general | solution.py:40
  152.9 5.5 copy.99
  165.1 5.8 %fusion.13.refs_2_ = bf16[1280,2304]{1,0:T(8,128)(2,1)S(1)} fusion(bf16[2304,768]{1,0:T(8,128)(2,1)S(1)} %bitcast.147, f32[2304]{0:T(1024)S(1)} %pad_maximum_fusion.2, f32[1280,768]{0,1:T(8,128)S(1)} %get-tuple-element.147, f32[768]{0:T(1024)S(1)} %get-tuple-element.130, f32[768]{0:T(1024)S(1)} %get-tuple-element.131, f32[1280]{0:T(1024)S(1)} %add_rsqrt_fusion.3, ...), kind=kOutput, calls=%fused_computation.23 | convolution fusion | flops 4540661760 | bytes 13394944 | tf_op jit(solution)/shard_map/dot_general | solution.py:50
  170.9 13.8 %shard_map.410 = (bf16[1280,768]{1,0:T(8,128)(2,1)S(1)}, f32[1280,128]{1,0:T(8,128)S(1)}) custom-call(s32[1280,1]{1,0:T(8,128)S(1)} %broadcast_in_dim.13.refs_0_, s32[10,1,256]{2,1,0:T(1,128)S(1)} %constant_dynamic-update-slice_fusion.refs_1_, bf16[1280,2304]{1,0:T(8,128)(2,1)S(1)} %fusion.13.refs_2_), custom_call_target="tpu_custom_call" | custom-call | flops 2013265920 | bytes 12000000 | tf_op jit(solution)/shard_map/pallas_call | solution.py:194
  188.5 12.7 %multiply_convert_fusion = (bf16[1280,3072]{1,0:T(8,128)(2,1)}, f32[1280,3072]{1,0:T(8,128)}) fusion(f32[3072]{0:T(1024)S(1)} %slice.201, bf16[3072,768]{1,0:T(8,128)(2,1)S(1)} %bitcast.172, f32[1280,768]{0,1:T(8,128)S(1)} %get-tuple-element.149, f32[768]{0:T(1024)S(1)} %get-tuple-element.125, f32[768]{0:T(1024)S(1)} %get-tuple-element.126, ...), kind=kOutput, calls=%fused_computation.19 | convolution fusion | flops 6068305920 | bytes 32272384 | tf_op jit(solution)/shard_map/dot_general | solution.py:50
  201.2 11.4 %fusion.130 = (f32[1280]{0:T(1024)S(1)}, f32[1280,768]{0,1:T(8,128)S(1)}) fusion(f32[768]{0:T(1024)S(1)} %get-tuple-element.124, bf16[1280,3072]{1,0:T(8,128)(2,1)} %get-tuple-element.150, bf16[3072,768]{1,0:T(8,128)(2,1)} %bitcast.173, f32[768]{0:T(1024)S(1)} %get-tuple-element.125, f32[768]{0:T(1024)S(1)} %get-tuple-element.126, ...), kind=kOutput, calls=%fused_computation.282 | convolution fusion | flops 6046678016 | bytes 20471808 | tf_op jit(solution)/shard_map/dot_general | solution.py:40
  229.3 10.1 %all-gather.6.cloned.1.call-done = bf16[5120,128]{0,1:T(8,128)(2,1)} async-done(((bf16[1280,128]{0,1:T(8,128)(2,1)}), bf16[5120,128]{0,1:T(8,128)(2,1)}) %all-gather.6.cloned.1.call-update) | async-done | bytes 1310736 | tf_op jit(solution)/shard_map/all_gather | solution.py:742
  250.4 5.2 all_gather.14
  272.0 5.8 %copy.113 = f32[1280,768]{0,1:T(8,128)} copy(f32[1280,768]{1,0:T(8,128)} %get-tuple-element.161) | data formatting | bytes 7864320 | tf_op jit(solution)/shard_map/dot_general | solution.py:50
  277.8 4.6 multiply_reduce_fusion.1
  284.9 17.2 %convert_reduce_fusion = (f32[3072]{0:T(1024)S(1)}, bf16[1280,3072]{1,0:T(8,128)(2,1)}) fusion(f32[1280,3072]{1,0:T(8,128)} %get-tuple-element.151, f32[3072]{0:T(1024)S(1)} %copy-done.87, bf16[3072,768]{1,0:T(8,128)(2,1)S(1)} %bitcast.176, f32[1280,768]{0,1:T(8,128)S(1)} %get-tuple-element.117), kind=kOutput, calls=%fused_computation.18 | convolution fusion | flops 6091895808 | bytes 32268288 | tf_op jit(solution)/shard_map/dot_general | solution.py:50
  302.1 13.1 %multiply_reduce_fusion.2 = (f32[768]{0:T(1024)S(1)}, f32[1280]{0:T(1024)S(1)}, f32[1280]{0:T(1024)S(1)}, f32[768]{0:T(1024)S(1)}, f32[1280,768]{0,1:T(8,128)}) fusion(f32[1280,768]{0,1:T(8,128)S(1)} %copy-done.19, f32[1280]{0:T(1024)S(1)} %copy-done.68, f32[1280]{0:T(1024)S(1)} %copy-done.55, f32[768]{0:T(1024)S(1)} %copy-done.77, ...), kind=kOutput, calls=%fused_computation.52 | convolution fusion | flops 6049624064 | bytes 24409088 | tf_op jit(solution)/shard_map/dot_general | solution.py:40
  321.7 36.6 %shard_map.411 = bf16[1280,2304]{1,0:T(8,128)(2,1)} custom-call(s32[1280,1]{1,0:T(8,128)} %copy-done, s32[10,1,256]{2,1,0:T(1,128)} %copy-done.1, bf16[1280,2304]{1,0:T(8,128)(2,1)} %copy-done.2, bf16[1280,768]{1,0:T(8,128)(2,1)} %convolution_convert_fusion.4.refs_3_, f32[1280,128]{1,0:T(8,128)} %copy-done.5), custom_call_target="tpu_custom_call" | custom-call | flops 5033164800 | bytes 18000000 | tf_op jit(solution)/shard_map/pallas_call | solution.py:216
  358.3 11.5 %multiply_reduce_fusion.3 = (f32[768]{0:T(1024)S(1)}, f32[1280]{0:T(1024)S(1)}, f32[1280]{0:T(1024)S(1)}, f32[768]{0:T(1024)S(1)}, f32[1280,768]{0,1:T(8,128)}) fusion(f32[1280,768]{0,1:T(8,128)S(1)} %copy-done.10, f32[1280]{0:T(1024)S(1)} %copy-done.74, f32[1280]{0:T(1024)S(1)} %copy-done.59, f32[768]{0:T(1024)S(1)} %copy-done.79, ...), kind=kOutput, calls=%fused_computation.53 | convolution fusion | flops 4539674624 | bytes 21263360 | tf_op jit(solution)/shard_map/dot_general | solution.py:40
  379.4 12.2 %convolution_convert_fusion = bf16[3072,768]{1,0:T(8,128)(2,1)} fusion(bf16[1280,3072]{1,0:T(8,128)(2,1)} %get-tuple-element.150, f32[1280,768]{0,1:T(8,128)S(1)} %copy-done.25), kind=kOutput, calls=%fused_computation.30 | convolution fusion | flops 6043140096 | bytes 16515072 | tf_op jit(solution)/shard_map/dot_general | solution.py:44
  391.7 12.2 %convolution_convert_fusion.1 = bf16[3072,768]{1,0:T(8,128)(2,1)} fusion(bf16[1280,3072]{1,0:T(8,128)(2,1)} %get-tuple-element.163, f32[1280,768]{0,1:T(8,128)S(1)} %copy-done.20, f32[768]{0:T(1024)S(1)} %copy-done.99, f32[768]{0:T(1024)S(1)} %copy-done.77, f32[1280]{0:T(1024)S(1)} %copy-done.68, f32[1280]{0:T(1024)S(1)} %copy-done.55), kind=kOutput, calls=%fused_computation.31 | convolution fusion | flops 6047072256 | bytes 16531456 | tf_op jit(solution)/shard_map/dot_general | solution.py:44
  403.8 6.8 %convolution_convert_fusion.2 = bf16[2304,768]{1,0:T(8,128)(2,1)} fusion(bf16[1280,2304]{1,0:T(8,128)(2,1)S(1)} %copy-done.21, f32[1280,768]{0,1:T(8,128)S(1)} %copy-done.10, f32[768]{0:T(1024)S(1)} %copy-done.97, f32[768]{0:T(1024)S(1)} %copy-done.79, f32[1280]{0:T(1024)S(1)} %copy-done.74, f32[1280]{0:T(1024)S(1)} %copy-done.59), kind=kOutput, calls=%fused_computation.32 | convolution fusion | flops 4536532992 | bytes 13385728 | tf_op jit(solution)/shard_map/dot_general | solution.py:44
  415.8 4.9 pad_maximum_fusion
  420.7 116.3 %shard_map.412 = (f32[96,768]{1,0:T(8,128)S(1)}, f32[96,768]{1,0:T(8,128)S(1)}, f32[96,768]{1,0:T(8,128)S(1)}, f32[64,128]{1,0:T(8,128)S(1)}, f32[16,128]{1,0:T(8,128)S(1)}, /*index=5*/bf16[32,48,768]{2,1,0:T(8,128)(2,1)}) custom-call(bf16[32,96,768]{2,1,0:T(8,128)(2,1)} %bitcast.142, bf16[32,96,768]{2,1,0:T(8,128)(2,1)} %bitcast.145, ...), custom_call_target="tpu_custom_call" | custom-call | tf_op jit(solution)/shard_map/pallas_call | solution.py:585
  539.6 6.5 %conditional.3 = (f32[960,768]{1,0:T(8,128)}) conditional(s32[]{:T(128)} %convert_element_type.229, (f32[32,1024]{1,0:T(8,128)}, bf16[32,48,768]{2,1,0:T(8,128)(2,1)}) %tuple.22, (s32[1280]{0:T(1024)S(1)}, f32[1280,768]{0,1:T(8,128)}) %tuple.95), branch_computations={%region_42.43_spmd, %region_43.46_spmd} | conditional | flops 2266398720 | bytes 406010944 | solution.py:892
  539.6 6.4 %fusion.4 = f32[960,768]{1,0:T(8,128)} fusion(bf16[32,48,768]{2,1,0:T(8,128)(2,1)} %get-tuple-element.29, f32[32,960]{1,0:T(8,128)} %bitcast.177, f32[48]{0:T(128)S(1)} %iota_convert_fusion), kind=kOutput, calls=%fused_computation.6 | convolution fusion | flops 2266398720 | bytes 5431488 | tf_op jit(solution)/shard_map/cond/branch_0_fun/dot_general | solution.py:44
  551.4 6.2 %multiply_subtract_fusion = (f32[960,768]{1,0:T(8,128)}, f32[960,768]{1,0:T(8,128)}) fusion(f32[960,768]{1,0:T(8,128)S(1)} %copy-done.13, f32[960,768]{1,0:T(8,128)} %get-tuple-element.211, f32[960,768]{1,0:T(8,128)} %param.39, f32[]{:T(128)} %bitcast.37, f32[]{:T(128)} %bitcast.36, f32[960,768]{1,0:T(8,128)} %param.40), kind=kLoop, calls=%fused_computation.83 | loop fusion | flops 11059200 | bytes 17694728 | tf_op jit(solution)/shard_map/sub | solution.py:606
  (379 shorter events, 112.9 us)
Async XLA Ops:
  127.8 93.3 %copy-start.33 = (bf16[4,8,48,128]{3,1,2,0:T(8,128)(2,1)}, bf16[4,8,48,128]{3,1,2,0:T(8,128)(2,1)S(1)}, u32[]{:S(2)}) copy-start(bf16[4,8,48,128]{3,1,2,0:T(8,128)(2,1)S(1)} %copy.138) | copy-start | bytes 1179652
  138.4 46.3 %copy-start.78 = (f32[768]{0:T(1024)}, f32[768]{0:T(1024)S(1)}, u32[]{:S(2)}) copy-start(f32[768]{0:T(1024)S(1)} %get-tuple-element.131) | copy-start | bytes 9220
  138.4 46.3 %copy-start.96 = (f32[768]{0:T(1024)}, f32[768]{0:T(1024)S(1)}, u32[]{:S(2)}) copy-start(f32[768]{0:T(1024)S(1)} %get-tuple-element.130) | copy-start | bytes 9220
  138.4 62.7 %copy-start.76 = (f32[768]{0:T(1024)}, f32[768]{0:T(1024)S(1)}, u32[]{:S(2)}) copy-start(f32[768]{0:T(1024)S(1)} %get-tuple-element.126) | copy-start | bytes 9220
  138.4 62.7 %copy-start.98 = (f32[768]{0:T(1024)}, f32[768]{0:T(1024)S(1)}, u32[]{:S(2)}) copy-start(f32[768]{0:T(1024)S(1)} %get-tuple-element.125) | copy-start | bytes 9220
  138.4 49.0 %copy-start.86 = (f32[3072]{0:T(1024)}, f32[3072]{0:T(1024)S(1)}, u32[]{:S(2)}) copy-start(f32[3072]{0:T(1024)S(1)} %slice.201) | copy-start | bytes 36868
  152.8 86.6 %all-gather.6.cloned.1.call-start = ((), (), s32[]{:S(2)}) async-start(), calls=%async_computation.3 | async-start | bytes 1638400 | tf_op jit(solution)/shard_map/all_gather | solution.py:742
  161.5 23.3 %copy-start.9 = (f32[1280,768]{0,1:T(8,128)}, f32[1280,768]{0,1:T(8,128)S(1)}, u32[]{:S(2)}) copy-start(f32[1280,768]{0,1:T(8,128)S(1)} %get-tuple-element.147) | copy-start | bytes 11796484
  161.5 23.3 %copy-start.58 = (f32[1280]{0:T(1024)}, f32[1280]{0:T(1024)S(1)}, u32[]{:S(2)}) copy-start(f32[1280]{0:T(1024)S(1)} %broadcast_multiply_fusion.8) | copy-start | bytes 15364
  161.9 22.9 %copy-start.73 = (f32[1280]{0:T(1024)}, f32[1280]{0:T(1024)S(1)}, u32[]{:S(2)}) copy-start(f32[1280]{0:T(1024)S(1)} %add_rsqrt_fusion.3) | copy-start | bytes 15364
  170.9 16.0 %copy-start.2 = (bf16[1280,2304]{1,0:T(8,128)(2,1)}, bf16[1280,2304]{1,0:T(8,128)(2,1)S(1)}, u32[]{:S(2)}) copy-start(bf16[1280,2304]{1,0:T(8,128)(2,1)S(1)} %fusion.13.refs_2_) | copy-start | bytes 17694724
  186.9 14.2 %copy-start.18 = (f32[1280,768]{0,1:T(8,128)}, f32[1280,768]{0,1:T(8,128)S(1)}, u32[]{:S(2)}) copy-start(f32[1280,768]{0,1:T(8,128)S(1)} %get-tuple-element.149) | copy-start | bytes 11796484
  224.2 20.2 %copy-start.32 = (bf16[1280,128]{0,1:T(8,128)(2,1)S(1)}, bf16[1280,128]{0,1:T(8,128)(2,1)}, u32[]{:S(2)}) copy-start(bf16[1280,128]{0,1:T(8,128)(2,1)} %multiply_convert_fusion.3) | copy-start | bytes 983044
  284.6 17.4 %copy-start.24 = (f32[1280,768]{0,1:T(8,128)}, f32[1280,768]{0,1:T(8,128)S(1)}, u32[]{:S(2)}) copy-start(f32[1280,768]{0,1:T(8,128)S(1)} %get-tuple-element.117) | copy-start | bytes 11796484
  284.9 17.2 %copy-start.19 = (f32[1280,768]{0,1:T(8,128)S(1)}, f32[1280,768]{0,1:T(8,128)}, u32[]{:S(2)}) copy-start(f32[1280,768]{0,1:T(8,128)} %copy-done.18) | copy-start | bytes 11796484
  284.9 17.2 %copy-start.55 = (f32[1280]{0:T(1024)S(1)}, f32[1280]{0:T(1024)}, u32[]{:S(2)}) copy-start(f32[1280]{0:T(1024)} %copy-done.54) | copy-start | bytes 15364
  284.9 17.2 %copy-start.68 = (f32[1280]{0:T(1024)S(1)}, f32[1280]{0:T(1024)}, u32[]{:S(2)}) copy-start(f32[1280]{0:T(1024)} %copy-done.67) | copy-start | bytes 15364
  284.9 17.2 %copy-start.77 = (f32[768]{0:T(1024)S(1)}, f32[768]{0:T(1024)}, u32[]{:S(2)}) copy-start(f32[768]{0:T(1024)} %copy-done.76) | copy-start | bytes 9220
  318.7 39.6 %copy-start.26 = (f32[1280,768]{0,1:T(8,128)}, f32[1280,768]{0,1:T(8,128)S(1)}, u32[]{:S(2)}) copy-start(f32[1280,768]{0,1:T(8,128)S(1)} %get-tuple-element.119) | copy-start | bytes 11796484
  321.7 36.6 %copy-start.10 = (f32[1280,768]{0,1:T(8,128)S(1)}, f32[1280,768]{0,1:T(8,128)}, u32[]{:S(2)}) copy-start(f32[1280,768]{0,1:T(8,128)} %copy-done.9) | copy-start | bytes 11796484
  321.7 36.6 %copy-start.59 = (f32[1280]{0:T(1024)S(1)}, f32[1280]{0:T(1024)}, u32[]{:S(2)}) copy-start(f32[1280]{0:T(1024)} %copy-done.58) | copy-start | bytes 15364
  321.7 36.6 %copy-start.74 = (f32[1280]{0:T(1024)S(1)}, f32[1280]{0:T(1024)}, u32[]{:S(2)}) copy-start(f32[1280]{0:T(1024)} %copy-done.73) | copy-start | bytes 15364
  321.7 36.6 %copy-start.79 = (f32[768]{0:T(1024)S(1)}, f32[768]{0:T(1024)}, u32[]{:S(2)}) copy-start(f32[768]{0:T(1024)} %copy-done.78) | copy-start | bytes 9220
  420.7 118.7 %copy-start.57 = (s32[1280]{0:T(1024)S(1)}, s32[1280]{0:T(1024)}, u32[]{:S(2)}) copy-start(s32[1280]{0:T(1024)} %copy-done.56) | copy-start | bytes 15364
  (85 other events, 430.5 us)
Sparse Core Ops, SparseCore 1:
  221.1 18.3 all-gather.5

commit v4 on v3

--- a/solution.py
+++ b/solution.py
@@ -134,7 +134,7 @@
 
 
 def attn_backward_kernel(
-    count, blocks, segc_ref, segw_ref, z_ref, do_ref, lse_ref, dz_ref, dk_ref, dv_ref
+    count, blocks, segc_ref, segw_ref, z_ref, do_ref, lse_ref, one_ref, dz_ref, dk_ref, dv_ref
 ):
     block = pl.program_id(0)
     row = pl.multiple_of(block * BLK, BLK)
@@ -174,10 +174,12 @@
         dk_ref[pl.ds(first, WIN), at : at + 2 * HD] += grad_key
         dv_ref[pl.ds(first, WIN), at : at + 2 * HD] += grad_value
 
+    dz_ref[pl.ds(row, BLK), 3 * D :] = one_ref[...]
+
     @pl.when(block == blocks - 1)
     def _():
         dz_ref[:, D : 2 * D] = dk_ref[...].astype(BF)
-        dz_ref[:, 2 * D :] = dv_ref[...].astype(BF)
+        dz_ref[:, 2 * D : 3 * D] = dv_ref[...].astype(BF)
 
 
 def attention_specs(count):
@@ -210,7 +212,7 @@
     )(segment_column, segment_windows, mixed)
 
 
-def attention_backward(segment_column, segment_windows, mixed, upstream, kept):
+def attention_backward(segment_column, segment_windows, mixed, upstream, kept, beside):
     count = mixed.shape[0]
     blocks = count // BLK
     return pl.pallas_call(
@@ -220,15 +222,16 @@
         + [
             pl.BlockSpec((BLK, D), lambda i: (i, 0)),
             pl.BlockSpec((BLK, 128), lambda i: (i, 0)),
+            pl.BlockSpec((BLK, D), lambda i: (i, 0)),
         ],
-        out_specs=pl.BlockSpec((count, 3 * D), lambda i: (0, 0)),
-        out_shape=jax.ShapeDtypeStruct((count, 3 * D), BF),
+        out_specs=pl.BlockSpec((count, 4 * D), lambda i: (0, 0)),
+        out_shape=jax.ShapeDtypeStruct((count, 4 * D), BF),
         scratch_shapes=[pltpu.VMEM((count, D), F32), pltpu.VMEM((count, D), F32)],
         compiler_params=pltpu.CompilerParams(vmem_limit_bytes=56 * 2**20),
         cost_estimate=pl.CostEstimate(
             flops=10 * count * WIN * 128 * HEADS, bytes_accessed=18000000, transcendentals=0
         ),
-    )(segment_column, segment_windows, mixed, upstream, kept)
+    )(segment_column, segment_windows, mixed, upstream, kept, beside)
 
 
 def place_of():
@@ -273,33 +276,35 @@
     return steps
 
 
-def pack_rows(asked, table, rank_ref, packed_ref):
-    devices, capacity, _ = packed_ref.shape
-    width = table.shape[0]
+def earlier_rows(width):
+    above = lax.broadcasted_iota(jnp.int32, (width, width), 0)
+    return (above < lax.broadcasted_iota(jnp.int32, (width, width), 1)).astype(F32).astype(BF)
+
+
+def rank_rows(asked, earlier, rank_ref):
+    width = earlier.shape[0]
     asked = jnp.concatenate([asked[:, j, :] for j in range(width // 128)], axis=1)
-    above = lax.broadcasted_iota(jnp.int32, (width, width), 0)
-    earlier = (above < lax.broadcasted_iota(jnp.int32, (width, width), 1)).astype(F32).astype(BF)
     rank_ref[...] = jnp.where(asked > 0.5, matmul(asked.astype(BF), earlier), -1.0)
-    most = jnp.max(jnp.sum(asked, axis=1, keepdims=True), axis=0, keepdims=True)
-    together = 8
-
-    @pl.loop(0, devices // together)
-    def _(i):
-        rank = rank_ref[pl.ds(pl.multiple_of(i * together, together), together), :]
-        slot = lax.broadcasted_iota(jnp.int32, (together, capacity, width), 1).astype(F32)
-        picked = jnp.where(rank[:, None, :] == slot, 1.0, 0.0)
-        picked = picked.reshape(together * capacity, width).astype(BF)
-        rows = matmul(picked, table[...]).reshape(together, capacity, D)
-        place = lax.broadcasted_iota(jnp.int32, (together, capacity, D), 1)
-        rows = jnp.where((place == capacity - 1) & (most > capacity)[:, :, None], MARK, rows)
-        packed_ref[pl.ds(i * together, together)] = rows.astype(BF)
+    return jnp.max(jnp.sum(asked, axis=1, keepdims=True), axis=0, keepdims=True)
+
+
+def pack_rows(places, slot, most, table, rank_ref, packed_ref):
+    capacity, width = packed_ref.shape[1], table.shape[0]
+    at = lax.broadcasted_iota(jnp.int32, (capacity, width), 0).astype(F32)
+    picked = [
+        jnp.where(rank_ref[pl.ds(place, 1), :] == at, 1.0, 0.0).astype(BF) for place in places
+    ]
+    rows = matmul(jnp.concatenate(picked), table[...]).reshape(len(places), capacity, D)
+    last = lax.broadcasted_iota(jnp.int32, (len(places), capacity, D), 1) == capacity - 1
+    rows = jnp.where(last & (most > capacity)[:, :, None], MARK, rows)
+    packed_ref[slot : slot + len(places)] = rows.astype(BF)
 
 
 def gather_kernel(devices, pieces, *refs):
     matrices = 3
     sources, (needed, notes, table) = refs[:matrices], refs[matrices : matrices + 3]
     outs, (notes_out, rows_out, rank) = refs[6:9], refs[9:12]
-    asked, packed, arrive, beside, leave, local, notes_sem, ask_sem, rows_sem = refs[12:]
+    asked, earlier, packed, arrive, beside, leave, local, notes_sem, ask_sem, rows_sem = refs[12:]
     me = place_of()
     group = max(devices // 8, 1)
     greet_all(devices, me)
@@ -374,25 +379,37 @@
     for copy in own:
         copy.start()
     own_asked.start()
+    earlier[...] = earlier_rows(table.shape[0])
     for piece in range(len(pieces)):
         pass_on(piece, 0)
     own_asked.wait()
     for i in range(2):
         settle(asked.at[pl.ds(0, devices - 1)], ask_sem.at[i])
-    pack_rows(asked[...], table, rank, packed)
-
-    masks = sorted(range(1, devices), key=lambda m: -bin(m).count("1"))
+    most = rank_rows(asked[...], earlier[...], rank)
+
+    masks = sorted(range(devices), key=lambda m: -bin(m).count("1"))
     steps = len(pieces[0][3])
     each = -(-(devices - 1) // (len(pieces) * (steps - 1)))
-    kept_rows = pltpu.make_async_copy(packed.at[me], rows_out.at[me], local.at[matrices + 2])
-    kept_rows.start()
+    kept_rows = pltpu.make_async_copy(
+        packed.at[devices - 1], rows_out.at[me], local.at[matrices + 2]
+    )
+    sent, made, together = 0, 0, 8
     for step in range(1, steps):
         for piece in range(len(pieces)):
+            now = min(sent + each, devices)
+            while made < now:
+                group_now = masks[made : made + together]
+                places = [flipped(me, m) for m in group_now]
+                pack_rows(places, made, most, table, rank, packed)
+                made += together
             pass_on(piece, step)
-            now, masks = masks[:each], masks[each:]
-            for mask in now:
-                target = flipped(me, mask)
-                push(packed.at[target], rows_out.at[me], target, rows_sem.at[0], rows_sem.at[1])
+            for i in range(sent, now):
+                target = flipped(me, masks[i])
+                if masks[i]:
+                    push(packed.at[i], rows_out.at[me], target, rows_sem.at[0], rows_sem.at[1])
+                else:
+                    kept_rows.start()
+            sent = now
     for piece in range(len(pieces)):
         wait(piece, devices // 2, beside.at[piece])
         wait(piece, devices - 1, leave.at[piece])
@@ -429,6 +446,7 @@
         ],
         scratch_shapes=[
             pltpu.VMEM(needed.shape, F32),
+            pltpu.VMEM((table.shape[0], table.shape[0]), BF),
             pltpu.VMEM((devices, capacity, D), BF),
             dma((len(pieces), count)),
             dma((len(pieces),)),
@@ -598,6 +616,418 @@
     return reduced, arrived
 
 
+def product_kernel(devices, pieces, spread, *refs):
+    count, computed = len({p[0] for p in pieces}), 3
+    lefts, rights, others, rows_in = refs[:3], refs[3:6], refs[6 : count + 3], refs[count + 3]
+    refs = refs[count + 4 :]
+    outs, rows_out = refs[:count], refs[count]
+    held, landed = refs[count + 1 : 2 * count + 1], refs[2 * count + 1 : 3 * count + 1]
+    refs = refs[3 * count + 1 :]
+    ready, refs = refs[:computed], refs[computed:]
+    slab, slab_sem, arrive, leave, load, rows_sem, own_sem = refs
+    me = place_of()
+    groups = devices // 4
+    half = groups // 2
+    depth = groups.bit_length() - 1
+    chunk = outs[0].shape[0]
+    greet_all(devices, me)
+
+    def push(source, target_ref, target, send, recv):
+        pltpu.make_async_remote_copy(
+            src_ref=source,
+            dst_ref=target_ref,
+            send_sem=send,
+            recv_sem=recv,
+            device_id=mesh_place(target),
+            device_id_type=pl.DeviceIdType.MESH,
+        ).start()
+
+    def settle(some, semaphore):
+        pltpu.make_async_copy(some, some, semaphore).wait()
+
+    plans, slots, places = [], [], []
+    for piece in pieces:
+        plan = [sum(step, []) for step in reduce_plan(piece[3], 1)]
+        slots.append({m: i for i, m in enumerate(plan[0])})
+        place, at = {}, 0
+        for step, masks in enumerate(plan):
+            for mask in masks:
+                place[step, mask] = at
+                at += 1
+        plans.append(plan)
+        places.append(place)
+
+    def rows_of(piece):
+        return pl.ds(pieces[piece][1], pieces[piece][2])
+
+    def send(piece, step, mask, bit, source):
+        where = places[piece][step, mask & ~(1 << bit)]
+        push(
+            source,
+            landed[pieces[piece][0]].at[where, rows_of(piece)],
+            flipped(me, 1 << bit),
+            leave.at[piece],
+            arrive.at[piece, where],
+        )
+
+    order = sorted(range(1, devices), key=lambda m: -bin(m).count("1"))
+
+    def send_rows(amount):
+        for _ in range(min(amount, len(order))):
+            target = flipped(me, order.pop(0))
+            push(rows_in.at[target], rows_out.at[me], target, rows_sem.at[0], rows_sem.at[1])
+
+    def group_of(turn):
+        own, place = me // 4, 0
+        for bit in range(depth):
+            differs = 1 - (turn // (1 << (depth - 1 - bit))) % 2
+            place = place + ((own // (1 << bit) + differs) % 2) * (1 << bit)
+        return place
+
+    def slab_copy(which, turn):
+        width = 4 * chunk
+        columns = pl.ds(pl.multiple_of(group_of(turn) * width, width), width)
+        return pltpu.make_async_copy(
+            lefts[which].at[:, columns],
+            slab.at[turn % 2, which],
+            slab_sem.at[turn % 2, which],
+        )
+
+    def slot_of(piece, turn, side):
+        if pieces[piece][3][0] == 1:
+            return (1 - side) * groups + turn
+        return (turn // half) * groups + (1 - side) * half + turn % half
+
+    big = [p for p in range(len(pieces)) if pieces[p][0] < computed]
+    small = [p for p in range(len(pieces)) if pieces[p][0] >= computed]
+    own_rows = pltpu.make_async_copy(rows_in.at[me], rows_out.at[me], own_sem)
+    own_rows.start()
+    for which in range(computed):
+        slab_copy(which, 0).start()
+    send_rows(spread[0])
+    for piece in small:
+        source = others[pieces[piece][0] - computed]
+        for mask in plans[piece][0]:
+            send(piece, 0, mask | 1, 0, source.at[flipped(me, mask | 1)])
+            pltpu.make_async_copy(
+                source.at[flipped(me, mask)],
+                held[pieces[piece][0]].at[slots[piece][mask]],
+                load.at[piece],
+            ).start()
+
+    def add(piece, slot, where):
+        which, rows = pieces[piece][0], rows_of(piece)
+        some = landed[which].at[pl.ds(where, 1), rows]
+        settle(some, arrive.at[piece, where])
+        total = held[which][slot, rows].astype(F32)
+        return total + landed[which][where, rows].astype(F32)
+
+    def first_add(turn):
+        for side in (1, 0):
+            for piece in big:
+                which, rows, bits = pieces[piece][0], rows_of(piece), pieces[piece][3]
+                slot = slot_of(piece, turn, side)
+                held[which][slot, rows] = add(piece, slot, slot).astype(BF)
+
+                def on():
+                    sent = len(plans[piece][0])
+                    push(
+                        held[which].at[slot, rows],
+                        landed[which].at[sent + slot, rows],
+                        flipped(me, 1 << bits[0]),
+                        leave.at[piece],
+                        arrive.at[piece, sent + slot],
+                    )
+
+                if bits[0] == 1 and side:
+                    on()
+                elif bits[0] == 2:
+                    pl.when(turn < half)(on)
+
+    @pl.loop(0, groups)
+    def _(turn):
+        @pl.when(turn + 1 < groups)
+        def _():
+            for which in range(computed):
+                slab_copy(which, turn + 1).start()
+
+        near = (me // 2) % 2
+        core = me % 2
+        for which in (0, 2, 1):
+            slab_copy(which, turn).wait()
+            if which == 0:
+                right = rights[0].at[(group_of(turn) * 4 * chunk) // (3 * D)]
+            else:
+                right = rights[which]
+            block = contract_rows(slab[turn % 2, which], right[...])
+            block = block.astype(BF).reshape(4, chunk, D)
+            for side in range(2):
+                for same in range(2):
+                    ready[which][turn * 4 + side * 2 + same] = block[side * 2 + same]
+            for piece in big:
+                if pieces[piece][0] != which:
+                    continue
+                rows = rows_of(piece)
+                for side in range(2):
+                    line = (near + side) % 2
+                    slot = slot_of(piece, turn, side)
+                    kept = ready[which].at[turn * 4 + line * 2 + core, rows]
+                    held[which][slot, rows] = kept[...]
+                    push(
+                        ready[which].at[turn * 4 + line * 2 + 1 - core, rows],
+                        landed[which].at[slot, rows],
+                        flipped(me, 1),
+                        leave.at[piece],
+                        arrive.at[piece, slot],
+                    )
+
+        @pl.when(turn > 0)
+        def _():
+            first_add(turn - 1)
+
+    first_add(groups - 1)
+    turn = 1
+    for step in range(len(pieces[0][3]) + 1):
+        for at in range(len(plans[0][step])):
+            for piece in small if step == 0 else (*big, *small):
+                which, _, _, bits = pieces[piece]
+                rows = rows_of(piece)
+                if step == 0 and at == 0:
+                    settle(held[which].at[pl.ds(0, devices // 2), rows], load.at[piece])
+                mask = plans[piece][step][at]
+                slot = slots[piece][mask]
+                total = add(piece, slot, places[piece][step, mask])
+                if step == len(bits):
+                    outs[which][rows] = total
+                    continue
+                held[which][slot, rows] = total.astype(held[which].dtype)
+                if (mask >> bits[step]) & 1:
+                    send(piece, step + 1, mask, bits[step], held[which].at[slot, rows])
+            if step or at == 0:
+                send_rows(spread[turn] if turn < len(spread) else 0)
+                turn += 1
+    send_rows(devices)
+    for piece in range(len(pieces)):
+        which = pieces[piece][0]
+        settle(landed[which].at[pl.ds(0, devices - 1), rows_of(piece)], leave.at[piece])
+    own_rows.wait()
+    for i in range(2):
+        settle(rows_out.at[pl.ds(0, devices - 1)], rows_sem.at[i])
+
+
+def reduce_products(lefts, rights, others, rows_in):
+    devices = rows_in.shape[0]
+    count, wide = lefts[0].shape
+    chunk = wide // devices
+    bits = devices.bit_length() - 1
+    high = list(range(3, bits))
+    one, other = (1, 2, *high), (2, 1, *high)
+    cut = chunk // 32 * 16
+    pieces = [(0, 0, chunk, one), (2, 0, chunk, other), (1, cut, chunk - cut, one)]
+    pieces += [(1, 0, cut, other), (3, 0, others[0].shape[1], one), (4, 0, others[1].shape[1], other)]
+    spread = [12] + [2] * devices
+    anywhere = pl.BlockSpec(memory_space=pl.ANY)
+    inside = pl.BlockSpec(memory_space=pltpu.VMEM)
+    dma = pltpu.SemaphoreType.DMA
+    kinds = [((chunk, D), BF)] * 3 + [(o.shape[1:], o.dtype) for o in others]
+    *reduced, arrived = pl.pallas_call(
+        lambda *refs: product_kernel(devices, pieces, spread, *refs),
+        in_specs=[anywhere] * 3 + [inside] * 3 + [anywhere] * (len(others) + 1),
+        out_specs=[inside] * len(kinds) + [anywhere],
+        out_shape=[jax.ShapeDtypeStruct(shape, F32) for shape, _ in kinds]
+        + [jax.ShapeDtypeStruct(rows_in.shape, rows_in.dtype)],
+        scratch_shapes=[pltpu.VMEM((devices // 2, *shape), kind) for shape, kind in kinds]
+        + [pltpu.VMEM((devices - 1, *shape), kind) for shape, kind in kinds]
+        + [pltpu.VMEM((devices, chunk, D), BF)] * 3
+        + [pltpu.VMEM((2, 3, count, 4 * chunk), BF), dma((2, 3))]
+        + [dma((len(pieces), devices - 1)), dma((len(pieces),)), dma((len(pieces),)), dma((2,)), dma],
+        compiler_params=pltpu.CompilerParams(
+            collective_id=2, has_side_effects=True, vmem_limit_bytes=60 * 2**20
+        ),
+    )(*lefts, jnp.stack(rights[:2]), *rights[2:], *others, rows_in)
+    return reduced, arrived
+
+
+TOK = 256
+
+
+def normalize(values):
+    average = jnp.mean(values, axis=-1, keepdims=True)
+    centered = values - average
+    inverse = lax.rsqrt(jnp.mean(centered * centered, axis=-1, keepdims=True) + NORM_EPS)
+    return centered * inverse, inverse
+
+
+def normalize_back(upstream, normed, inverse, gain):
+    scaled = upstream * (1.0 + gain)
+    return inverse * (
+        scaled
+        - jnp.mean(scaled, axis=-1, keepdims=True)
+        - normed * jnp.mean(scaled * normed, axis=-1, keepdims=True)
+    )
+
+
+def vector(vec_ref, i):
+    return vec_ref[i : i + 1, :]
+
+
+def first_kernel(looked_ref, place_ref, table_ref, vec_ref, qkv_ref, normed_ref, inv_ref, low_ref, z_ref):
+    hot = place_ref[...] == lax.broadcasted_iota(jnp.int32, (TOK, PMAX), 1)
+    values = looked_ref[...] + matmul(hot.astype(F32).astype(BF), table_ref[...])
+    normed, inverse = normalize(values)
+    normed_ref[...] = normed
+    inv_ref[...] = inverse
+    low = (normed * (1.0 + vector(vec_ref, 0)) + vector(vec_ref, 1)).astype(BF)
+    low_ref[...] = low
+    for part, bias in ((0, 2), (1, None), (2, 3)):
+        at = slice(part * D, (part + 1) * D)
+        mixed = contract_cols(low, qkv_ref[at, :])
+        if bias is not None:
+            mixed = mixed + vector(vec_ref, bias)
+        z_ref[:, at] = mixed.astype(BF)
+
+
+def middle_kernel(
+    context_ref, zero_ref, vec_ref, bias_ref, out_ref, up_ref, down_ref, head_ref, *results
+):
+    one_ref, one_inv_ref, one_low_ref, act_ref, slope_ref = results[:5]
+    two_ref, two_inv_ref, two_low_ref, unit_ref, scale_ref, unit_low_ref = results[5:]
+    hidden = zero_ref[...] * (1.0 + vector(vec_ref, 0)) + vector(vec_ref, 1)
+    hidden = hidden + contract_cols(context_ref[...], out_ref[...]) + vector(vec_ref, 4)
+    normed, inverse = normalize(hidden)
+    one_ref[...] = normed
+    one_inv_ref[...] = inverse
+    hidden = normed * (1.0 + vector(vec_ref, 5)) + vector(vec_ref, 6)
+    low = hidden.astype(BF)
+    one_low_ref[...] = low
+    total = hidden + vector(vec_ref, 7)
+    for part in range(up_ref.shape[0] // D):
+        at = slice(part * D, (part + 1) * D)
+        inner = contract_cols(low, up_ref[at, :]) + bias_ref[:, at]
+        cdf = 0.5 + 0.5 * lax.erf(inner * math.sqrt(0.5))
+        activated = (inner * cdf).astype(BF)
+        act_ref[:, at] = activated
+        pdf = jnp.exp(-0.5 * inner * inner) * (1.0 / math.sqrt(2.0 * math.pi))
+        slope_ref[:, at] = (cdf + inner * pdf).astype(BF)
+        total = total + matmul(activated, down_ref[at, :])
+    normed, inverse = normalize(total)
+    two_ref[...] = normed
+    two_inv_ref[...] = inverse
+    low = (normed * (1.0 + vector(vec_ref, 8)) + vector(vec_ref, 9)).astype(BF)
+    two_low_ref[...] = low
+    projected = matmul(low, head_ref[...])
+    scale = lax.rsqrt(jnp.sum(projected * projected, axis=-1, keepdims=True) + NORM_EPS)
+    unit_ref[...] = projected * scale
+    scale_ref[...] = scale
+    unit_low_ref[...] = (projected * scale).astype(BF)
+
+
+def column_sum(values):
+    return jnp.sum(values, axis=0, keepdims=True)
+
+
+def middle_back_kernel(
+    grad_ref,
+    unit_ref,
+    scale_ref,
+    two_ref,
+    two_inv_ref,
+    slope_ref,
+    one_ref,
+    one_inv_ref,
+    vec_ref,
+    out_ref,
+    up_ref,
+    down_ref,
+    head_ref,
+    *results,
+):
+    proj_ref, dtwo_ref, inner_ref, done_ref, done_low_ref, context_ref, sums_ref, bias_ref = results
+
+    @pl.when(pl.program_id(0) == 0)
+    def _():
+        sums_ref[...] = jnp.zeros_like(sums_ref)
+        bias_ref[...] = jnp.zeros_like(bias_ref)
+
+    grad, unit = grad_ref[...], unit_ref[...]
+    proj = (grad - unit * jnp.sum(grad * unit, axis=-1, keepdims=True)) * scale_ref[...]
+    proj = proj.astype(BF)
+    proj_ref[...] = proj
+    upstream, normed = contract_cols(proj, head_ref[...]), two_ref[...]
+    dtwo = normalize_back(upstream, normed, two_inv_ref[...], vector(vec_ref, 8))
+    sums_ref[0:1, :] += column_sum(upstream * normed)
+    sums_ref[1:2, :] += column_sum(upstream)
+    sums_ref[2:3, :] += column_sum(dtwo)
+    low = dtwo.astype(BF)
+    dtwo_ref[...] = low
+    upstream = dtwo
+    for part in range(up_ref.shape[0] // D):
+        at = slice(part * D, (part + 1) * D)
+        inner = contract_cols(low, down_ref[at, :]) * slope_ref[:, at].astype(F32)
+        bias_ref[:, at] += column_sum(inner)
+        inner = inner.astype(BF)
+        inner_ref[:, at] = inner
+        upstream = upstream + matmul(inner, up_ref[at, :])
+    normed = one_ref[...]
+    done = normalize_back(upstream, normed, one_inv_ref[...], vector(vec_ref, 5))
+    sums_ref[3:4, :] += column_sum(upstream * normed)
+    sums_ref[4:5, :] += column_sum(upstream)
+    sums_ref[5:6, :] += column_sum(done)
+    done_ref[...] = done
+    low = done.astype(BF)
+    done_low_ref[...] = low
+    context_ref[...] = matmul(low, out_ref[...]).astype(BF)
+
+
+def first_back_kernel(
+    z_ref, done_ref, zero_ref, inv_ref, place_ref, vec_ref, qkv_ref, low_ref, places_ref, sums_ref
+):
+    @pl.when(pl.program_id(0) == 0)
+    def _():
+        sums_ref[...] = jnp.zeros_like(sums_ref)
+        places_ref[...] = jnp.zeros_like(places_ref)
+
+    upstream, normed = done_ref[...], zero_ref[...]
+    for part in range(3):
+        at = slice(part * D, (part + 1) * D)
+        upstream = upstream + matmul(z_ref[:, at], qkv_ref[at, :])
+    grad = normalize_back(upstream, normed, inv_ref[...], vector(vec_ref, 0))
+    sums_ref[0:1, :] += column_sum(upstream * normed)
+    sums_ref[1:2, :] += column_sum(upstream)
+    sums_ref[2:3, :] += column_sum(z_ref[:, :D].astype(F32))
+    sums_ref[3:4, :] += column_sum(z_ref[:, 2 * D : 3 * D].astype(F32))
+    low = grad.astype(BF)
+    low_ref[...] = low
+    hot = place_ref[...] == lax.broadcasted_iota(jnp.int32, (TOK, PMAX), 1)
+    places_ref[...] += contract_rows(hot.astype(F32).astype(BF), low)
+
+
+def by_tokens(width):
+    return pl.BlockSpec((TOK, width), lambda i: (i, 0))
+
+
+def resident(rows, width, at=0):
+    return pl.BlockSpec((rows, width), lambda i: (at, 0), pipeline_mode=pl.Buffered(1))
+
+
+def token_call(kernel, count, in_specs, outs, flops):
+    return pl.pallas_call(
+        kernel,
+        grid=(count // TOK,),
+        in_specs=in_specs,
+        out_specs=[
+            by_tokens(width) if rows is None else pl.BlockSpec((rows, width), lambda i: (0, 0))
+            for rows, width, _ in outs
+        ],
+        out_shape=[
+            jax.ShapeDtypeStruct((count if rows is None else rows, width), kind)
+            for rows, width, kind in outs
+        ],
+        compiler_params=pltpu.CompilerParams(vmem_limit_bytes=56 * 2**20),
+        cost_estimate=pl.CostEstimate(flops=flops, bytes_accessed=30000000, transcendentals=0),
+    )
+
+
 def adam_update(weight, moment, second, gradient, rate, count_steps):
     moment_new = BETA_ONE * moment + (1.0 - BETA_ONE) * gradient
     second_new = BETA_TWO * second + (1.0 - BETA_TWO) * gradient * gradient
@@ -715,29 +1145,48 @@
 
     positions = small_all[: PMAX * D].reshape(PMAX, D)
     remainder = small_all[PMAX * D :].astype(F32)
-    pieces = [remainder[i * D : (i + 1) * D] for i in range(10)]
-    bias_up = remainder[10 * D :]
-    position_hot = one_hot(position, PMAX)
-    embedded = looked_up + matmul(position_hot, positions)
-    hidden_zero, norm_zero = layer_norm(embedded, pieces[0], pieces[1])
-    input_zero = hidden_zero.astype(BF)
-    bias_mixed = jnp.concatenate([pieces[2], jnp.zeros((D,), F32), pieces[3]])
-    mixed = (contract_cols(input_zero, attn_rows[: 3 * D]) + bias_mixed).astype(BF)
+    vectors = jnp.pad(remainder[: 10 * D].reshape(10, D), ((0, 6), (0, 0)))
+    bias_up = remainder[None, 10 * D :]
+    inner_width = up_rows.shape[0]
+    place_column = position[:, None]
+    norm_zero, inverse_zero, input_zero, mixed = token_call(
+        first_kernel,
+        count,
+        [by_tokens(D), by_tokens(1), resident(PMAX, D), resident(16, D), resident(3 * D, D)],
+        [(None, D, F32), (None, 1, F32), (None, D, BF), (None, 3 * D, BF)],
+        2 * count * D * (3 * D + PMAX),
+    )(looked_up, place_column, positions, vectors, attn_rows)
     context, kept = attention_forward(segment_column, segment_windows, mixed)
-    hidden_one, norm_one = layer_norm(
-        hidden_zero + contract_cols(context, attn_rows[3 * D :]) + pieces[4], pieces[5], pieces[6]
-    )
-    input_one = hidden_one.astype(BF)
-    inner = contract_cols(input_one, up_rows) + bias_up
-    activated = (0.5 * inner * (1.0 + lax.erf(inner / math.sqrt(2.0)))).astype(BF)
-    hidden_two, norm_two = layer_norm(
-        hidden_one + matmul(activated, down_rows) + pieces[7], pieces[8], pieces[9]
-    )
-    input_two = hidden_two.astype(BF)
-    projected = matmul(input_two, head_full)
-    scale_inverse = lax.rsqrt(jnp.sum(projected * projected, axis=-1, keepdims=True) + NORM_EPS)
-    unit = projected * scale_inverse
-    unit_low = unit.astype(BF)
+    weight_specs = [
+        resident(D, D, 3),
+        resident(inner_width, D),
+        resident(inner_width, D),
+        resident(D, DC),
+    ]
+    weights = (attn_rows, up_rows, down_rows, head_full)
+    middle_flops = 2 * count * D * (D + 2 * inner_width + DC)
+    (
+        norm_one,
+        inverse_one,
+        input_one,
+        activated,
+        slope,
+        norm_two,
+        inverse_two,
+        input_two,
+        unit,
+        scale_inverse,
+        unit_low,
+    ) = token_call(
+        middle_kernel,
+        count,
+        [by_tokens(D), by_tokens(D), resident(16, D), resident(1, inner_width), *weight_specs],
+        [(None, D, F32), (None, 1, F32), (None, D, BF)]
+        + [(None, inner_width, BF)] * 2
+        + [(None, D, F32), (None, 1, F32), (None, D, BF)]
+        + [(None, DC, F32), (None, 1, F32), (None, DC, BF)],
+        middle_flops,
+    )(context, norm_zero, vectors, bias_up, *weights)
 
     units = lax.all_gather(unit_low, "psg", axis=0)
     group_passage = units[:, :ROW]
@@ -797,77 +1246,94 @@
     grad_unit_passage = contract_rows(sims, group_query)
     grad_unit = jnp.concatenate([grad_unit_passage, grad_unit_query])
 
-    grad_proj = (
-        (grad_unit - unit * jnp.sum(grad_unit * unit, axis=-1, keepdims=True)) * scale_inverse
-    ).astype(BF)
-    grad_head = contract_rows(input_two, grad_proj)
     picks = one_hot(assignments[0], NCENT)
     centroid_part = contract_rows(picks, own_passage)
     count_part = jnp.sum(picks.astype(F32), axis=0)
-
-    grad_hidden_two = contract_cols(grad_proj, head_full)
-    grad_sum_two, grad_gain_two, grad_shift_two = norm_back(grad_hidden_two, norm_two, pieces[8])
-    grad_two_low = grad_sum_two.astype(BF)
-    grad_down_rows = contract_rows(activated, grad_two_low)
-    grad_activated = contract_cols(grad_two_low, down_rows)
-    normal_cdf = 0.5 * (1.0 + lax.erf(inner / math.sqrt(2.0)))
-    normal_pdf = jnp.exp(-0.5 * inner * inner) / math.sqrt(2.0 * math.pi)
-    grad_inner = (grad_activated * (normal_cdf + inner * normal_pdf)).astype(BF)
-    grad_up_rows = contract_rows(grad_inner, input_one)
-    grad_bias_up = jnp.sum(grad_inner.astype(F32), axis=0)
-    grad_hidden_one = grad_sum_two + matmul(grad_inner, up_rows)
-    grad_sum_one, grad_gain_one, grad_shift_one = norm_back(grad_hidden_one, norm_one, pieces[5])
-    grad_one_low = grad_sum_one.astype(BF)
-    grad_out_rows = contract_rows(grad_one_low, context)
-    grad_context = matmul(grad_one_low, attn_rows[3 * D :]).astype(BF)
-    grad_mixed = attention_backward(segment_column, segment_windows, mixed, grad_context, kept)
-    grad_qkv_rows = contract_rows(grad_mixed, input_zero)
-    grad_mixed_sum = jnp.sum(grad_mixed.astype(F32), axis=0)
-    grad_hidden_zero = grad_sum_one + matmul(grad_mixed, attn_rows[: 3 * D])
-    grad_embedded, grad_gain_zero, grad_shift_zero = norm_back(
-        grad_hidden_zero, norm_zero, pieces[0]
-    )
-    grad_low = grad_embedded.astype(BF)
-    grad_positions = contract_rows(position_hot, grad_low)
+    (
+        grad_proj,
+        grad_two_low,
+        grad_inner,
+        grad_sum_one,
+        grad_one_low,
+        grad_context,
+        sums,
+        grad_bias_up,
+    ) = token_call(
+        middle_back_kernel,
+        count,
+        [by_tokens(DC), by_tokens(DC), by_tokens(1), by_tokens(D), by_tokens(1)]
+        + [by_tokens(inner_width), by_tokens(D), by_tokens(1), resident(16, D), *weight_specs],
+        [(None, DC, BF), (None, D, BF), (None, inner_width, BF), (None, D, F32)]
+        + [(None, D, BF), (None, D, BF), (8, D, F32), (1, inner_width, F32)],
+        middle_flops,
+    )(
+        grad_unit,
+        unit,
+        scale_inverse,
+        norm_two,
+        inverse_two,
+        slope,
+        norm_one,
+        inverse_one,
+        vectors,
+        *weights,
+    )
+    grad_head = contract_rows(input_two, grad_proj)
+    grad_attn = attention_backward(
+        segment_column, segment_windows, mixed, grad_context, kept, grad_one_low
+    )
+    grad_low, grad_positions, sums_zero = token_call(
+        first_back_kernel,
+        count,
+        [by_tokens(3 * D), by_tokens(D), by_tokens(D), by_tokens(1), by_tokens(1)]
+        + [resident(16, D), resident(3 * D, D)],
+        [(None, D, BF), (PMAX, D, F32), (8, D, F32)],
+        2 * count * D * (3 * D + PMAX),
+    )(grad_attn, grad_sum_one, norm_zero, inverse_zero, place_column, vectors, attn_rows)
     grad_slots = contract_rows(slot_hot, grad_low).astype(BF).reshape(devices, capacity, D)
     grad_small = jnp.concatenate(
         [
             grad_positions.reshape(-1),
-            grad_gain_zero,
-            grad_shift_zero,
-            grad_mixed_sum[:D],
-            grad_mixed_sum[2 * D :],
-            jnp.sum(grad_sum_one, axis=0),
-            grad_gain_one,
-            grad_shift_one,
-            jnp.sum(grad_sum_two, axis=0),
-            grad_gain_two,
-            grad_shift_two,
-            grad_bias_up,
+            sums_zero[:4].reshape(-1),
+            sums[5],
+            sums[3],
+            sums[4],
+            sums[2],
+            sums[0],
+            sums[1],
+            grad_bias_up[0],
         ]
     )
-
-    def chunks(rows):
-        rows = rows.astype(BF).reshape(devices, matrix_rows, D)
-        return jnp.pad(rows, ((0, 0), (0, -matrix_rows % 16), (0, 0)))
 
     def side_by_side(parts, sublanes):
         joined = jnp.concatenate([p.reshape(devices, -1) for p in parts], axis=1)
         joined = jnp.pad(joined, ((0, 0), (0, -joined.shape[1] % (sublanes * 128))))
         return joined.reshape(devices, -1, 128)
 
-    reduced, grad_slots = reduce_all(
-        [
-            chunks(jnp.concatenate([grad_qkv_rows.astype(BF), grad_out_rows.astype(BF)])),
-            chunks(grad_up_rows),
-            chunks(grad_down_rows),
-            side_by_side([centroid_part.astype(BF), grad_head.astype(BF)], 16),
-            side_by_side(
-                [grad_small, count_part, jnp.broadcast_to(numerator, (devices, 1))], 8
-            ),
-        ],
-        grad_slots,
-    )
+    lefts = [grad_attn, grad_inner, activated]
+    rights = [input_zero, context, input_one, grad_two_low]
+    others = [
+        side_by_side([centroid_part.astype(BF), grad_head.astype(BF)], 16),
+        side_by_side([grad_small, count_part, jnp.broadcast_to(numerator, (devices, 1))], 8),
+    ]
+    if members * matrix_rows % 128 == 0 and members == 4:
+        reduced, grad_slots = reduce_products(lefts, rights, others, grad_slots)
+    else:
+        right_of = [rights[:2], rights[2:3], rights[3:]]
+        sums = []
+        for left, right in zip(lefts, right_of):
+            if len(right) == 2:
+                rows = jnp.concatenate(
+                    [
+                        contract_rows(left[:, : 3 * D], right[0]),
+                        contract_rows(left[:, 3 * D :], right[1]),
+                    ]
+                )
+            else:
+                rows = contract_rows(left, right[0])
+            rows = rows.astype(BF).reshape(devices, matrix_rows, D)
+            sums.append(jnp.pad(rows, ((0, 0), (0, -matrix_rows % 16), (0, 0))))
+        reduced, grad_slots = reduce_all(sums + others, grad_slots)
     attn_reduced, up_reduced, down_reduced = (r[:matrix_rows] for r in reduced[:3])
     wide, fine = reduced[3].reshape(-1), reduced[4].reshape(-1)
     centroid_rows = NCENT // devices
@@ -878,7 +1344,7 @@
     loss = fine[small_size + centroid_rows] / pair_floor
 
     def whole_table():
-        table = jnp.zeros((shard_rows * devices, D), F32).at[tokens].add(grad_embedded)
+        table = jnp.zeros((shard_rows * devices, D), F32).at[tokens].add(grad_low.astype(F32))
         return lax.psum_scatter(table, ALL, scatter_dimension=0, tiled=True)
 
     def own_rows():

time: 579 us -> 506 us (0.87); the launches traced: 569 us -> 503 us
  matrix products: 157 us -> 41.6 us
  Pallas kernels: 274 us -> 360 us
  local copies, waits for them, and re-layouts: 51 us -> 23.6 us
  other arithmetic: 49.2 us -> 32.5 us
  loops' own time: 0.47 us -> 11.3 us
    pallas_call x1 -> x5, Pallas kernels: 116 us -> 201 us  [the longest x1 120 us: reduce_products(): pl.pallas_call(lambda *refs: product_kernel(devices, pieces, spread, *ref...]
    dot_general x10 -> x4, matrix products: 54.2 us -> 11.1 us  [matmul(): return jnp.dot(lhs_mat, rhs_mat, preferred_element_type=jnp.float32)]
    dot_general x6 -> x1, matrix products: 41.6 us -> 0.7 us  [contract_cols(): lax.dot_general(lhs_mat, rhs_mat, (((1,), (1,)), ((), ())), preferred_ele...]
    dot_general x11 -> x6, matrix products: 53.5 us -> 22.3 us  [contract_rows(): lax.dot_general(lhs_mat, rhs_mat, (((0,), (0,)), ((), ())), preferred_ele...]
    reduce_sum x8 -> x0, other arithmetic: 11.6 us -> none  [the longest x1 4.59 us: norm_back(): return (back, jnp.sum(upstream * normed, axis=0), jnp.sum(upstream, axis=0))]
    another operation x1, loops' own time: 0.45 us -> 11.3 us  [on_device(): lax.cond(overflow, lambda: lax.all_gather(embed_table.astype(BF), ALL, ax...]
    slice x4 -> x3, local copies, waits for them, and re-layouts: 6.79 us -> 0.06 us  [the longest x1 0.05 us: on_device(): sums[1]]
    unnamed x245 -> x108, local copies, waits for them, and re-layouts: 16.6 us -> 10.5 us
  transfers between devices with their start and end apart: 1 -> 1, of which waited for: 1 -> 1; matrix products, arithmetic and copies ran while one was open for 1% -> 2% of each run, Pallas kernels for 0% -> 0%
where the time goes in v4:
time: 506 us; the launch traced here: 503 us
  Pallas kernels  360 us (71%)
  matrix products  41.6 us (8%)
  other arithmetic  32.5 us (6%)
  local copies, waits for them, and re-layouts  23.6 us (5%)
  between operations  20.4 us (4%)
  loops' own time  11.3 us (2%)
  waiting for transfers between devices  8.99 us (2%)
  blocking collectives  5.39 us (1%)
    pallas_call x1, Pallas kernels, reduce_products(): pl.pallas_call(lambda *refs: product_kernel(devices, pieces, spread, *ref...  120 us
    pallas_call x1, Pallas kernels, gather_all(): pl.pallas_call(lambda *refs: gather_kernel(devices, pieces, *refs), in_sp...  108 us
    pallas_call x1, Pallas kernels, attention_backward(): pl.pallas_call(lambda *refs: attn_backward_kernel(count, blocks, *refs),...  37 us
    pallas_call x1, Pallas kernels, on_device(): token_call(middle_kernel, count, [by_tokens(D), by_tokens(D), resident(16...  29.1 us
    pallas_call x1, Pallas kernels, on_device(): token_call(middle_back_kernel, count, [by_tokens(DC), by_tokens(DC), by_t...  27.8 us
    dot_general x6, matrix products, contract_rows(): lax.dot_general(lhs_mat, rhs_mat, (((0,), (0,)), ((), ())), preferred_ele...  22.3 us
    sub x6, other arithmetic, adam_update(): weight - rate * (corrected / (jnp.sqrt(scaled) + ADAM_EPS) + WEIGHT_DECAY...  15 us
    pallas_call x1, Pallas kernels, attention_forward(): pl.pallas_call(lambda *refs: attn_forward_kernel(count, *refs), grid=(blo...  13.5 us
  transfers between devices with their start and end apart: 1, of which 1 were waited for; matrix products, arithmetic and copies ran while one was open for 2% of the time, Pallas kernels for 0%

profile of v4, /device:TPU:0, one launch (start us, length us, event | category | flops | bytes accessed | tf_op | source)
XLA Modules:
  0.0 503.5 jit_solution(1211028846750787112)
XLA Ops:
  17.5 107.7 %shard_map.409 = (bf16[32,96,768]{2,1,0:T(8,128)(2,1)}, bf16[32,96,768]{2,1,0:T(8,128)(2,1)}, bf16[32,96,768]{2,1,0:T(8,128)(2,1)}, bf16[32,48,128]{2,1,0:T(8,12...) custom-call(bf16[96,768]{1,0:T(8,128)(2,1)S(1)} %get-tuple-element.176.refs_0_, ...), custom_call_target="tpu_custom_call" | custom-call | tf_op jit(solution)/shard_map/pallas_call | solution.py:438
  127.1 2.7 fusion.8
  135.8 19.2 %conditional.2 = (f32[1280,768]{1,0:T(8,128)}) conditional(s32[]{:T(128)} %convert_element_type.178, (bf16[32,48,768]{2,1,0:T(8,128)(2,1)}, bf16[1280,1536]{1,0:T(8,128)(2,1)}) %tuple.20, (f32[960,768]{1,0:T(8,128)}, s32[1280]{0:T(1024)S(1)}) %tuple.21), branch_computations={%region_5.6_spmd, %region_6.7_spmd} | conditional | flops 3019898880 | bytes 160264224 | solution.py:1140
  147.1 8.0 %fusion.103 = f32[1280,768]{1,0:T(8,128)} fusion(bf16[1280,1536]{1,0:T(8,128)(2,1)} %get-tuple-element.24, bf16[1536,768]{1,0:T(8,128)(2,1)} %bitcast.137), kind=kOutput, calls=%fused_computation.207 | convolution fusion | flops 3019898880 | bytes 10223616 | tf_op jit(solution)/shard_map/cond/branch_0_fun/dot_general | solution.py:40
  155.0 11.7 %shard_map.410 = (f32[1280,768]{1,0:T(8,128)}, f32[1280,1]{1,0:T(8,128)}, bf16[1280,768]{1,0:T(8,128)(2,1)}, bf16[1280,2304]{1,0:T(8,128)(2,1)}) custom-call(f32[1280,768]{1,0:T(8,128)} %get-tuple-element.219.looked_ref, s32[1280,1]{1,0:T(8,128)} %broadcast_in_dim.22.place_ref, bf16[64,768]{1,0:T(8,128)(2,1)} %slice.161.table_ref, ...), custom_call_target="tpu_custom_call" | custom-call | flops 4655677440 | bytes 30000000 | tf_op jit(solution)/shard_map/pallas_call | solution.py:1152
  166.8 2.7 copy-done
  169.4 13.5 %shard_map.411 = (bf16[1280,768]{1,0:T(8,128)(2,1)S(1)}, f32[1280,128]{1,0:T(8,128)S(1)}) custom-call(s32[1280,1]{1,0:T(8,128)S(1)} %broadcast_in_dim.21.refs_0_, s32[10,1,256]{2,1,0:T(1,128)S(1)} %constant_dynamic-update-slice_fusion.refs_1_, bf16[1280,2304]{1,0:T(8,128)(2,1)S(1)} %copy-done), custom_call_target="tpu_custom_call" | custom-call | flops 2013265920 | bytes 12000000 | tf_op jit(solution)/shard_map/pallas_call | solution.py:196
  185.1 29.1 %shard_map.412 = (f32[1280,768]{1,0:T(8,128)}, f32[1280,1]{1,0:T(8,128)}, bf16[1280,768]{1,0:T(8,128)(2,1)}, bf16[1280,3072]{1,0:T(8,128)(2,1)}, bf16[1280,3072]...) custom-call(bf16[1280,768]{1,0:T(8,128)(2,1)} %copy-done.2, ...), custom_call_target="tpu_custom_call" | custom-call | flops 13841203200 | bytes 30000000 | tf_op jit(solution)/shard_map/pallas_call | solution.py:1180
  214.9 2.4 fusion.31
  219.8 3.9 pad_maximum_fusion.refs_3_
  223.7 9.0 %all-gather.6.cloned.1.call-done = bf16[5120,128]{1,0:T(8,128)(2,1)} async-done(((bf16[1280,128]{1,0:T(8,128)(2,1)}), bf16[5120,128]{1,0:T(8,128)(2,1)}) %all-gather.6.cloned.1.call-update) | async-done | bytes 1310736 | tf_op jit(solution)/shard_map/all_gather | solution.py:1191
  238.4 5.4 %all_gather.14 = f32[32,128]{1,0:T(8,128)S(1)} all-gather(f32[8,128]{1,0:T(8,128)S(1)} %select_subtract_fusion), channel_id=1, replica_groups=mesh['grp'=8,'psg'=4] {'psg'}, dimensions={0}, use_global_device_ids=true | all-gather | bytes 20480 | tf_op jit(solution)/shard_map/all_gather | solution.py:1228
  248.1 5.2 %fusion.29 = f32[1024,128]{1,0:T(8,128)} fusion(bf16[1024,128]{1,0:T(8,128)(2,1)S(1)} %bitcast.128, f32[1024,1024]{1,0:T(8,128)} %copy-done.8, bf16[1024,32]{0,1:T(8,128)(2,1)S(1)} %fusion.43, s32[1024]{0:T(1024)S(1)} %get-tuple-element.174), kind=kOutput, calls=%fused_computation.48 | convolution fusion | flops 339771392 | bytes 5050368 | tf_op jit(solution)/shard_map/dot_general | solution.py:44
  253.8 3.9 fusion.36
  258.6 27.8 %shard_map.413 = (bf16[1280,128]{1,0:T(8,128)(2,1)}, bf16[1280,768]{1,0:T(8,128)(2,1)}, bf16[1280,3072]{1,0:T(8,128)(2,1)}, f32[1280,768]{1,0:T(8,128)}, bf16[12...) custom-call(f32[1280,128]{1,0:T(8,128)} %pad_maximum_fusion.1.grad_ref, ...), custom_call_target="tpu_custom_call" | custom-call | flops 13841203200 | bytes 30000000 | tf_op jit(solution)/shard_map/pallas_call | solution.py:1261
  286.4 37.0 %shard_map.414.z_ref.refs_0_ = bf16[1280,3072]{1,0:T(8,128)(2,1)} custom-call(s32[1280,1]{1,0:T(8,128)} %copy-done.1, s32[10,1,256]{2,1,0:T(1,128)} %copy-done.5, bf16[1280,2304]{1,0:T(8,128)(2,1)} %get-tuple-element.96.refs_2_, bf16[1280,768]{1,0:T(8,128)(2,1)} %get-tuple-element.109.refs_3_, f32[1280,128]{1,0:T(8,128)} %copy-done.4, ...), custom_call_target="tpu_custom_call" | custom-call | flops 5033164800 | bytes 18000000 | tf_op jit(solution)/shard_map/pallas_call | solution.py:218
  323.4 12.6 %shard_map.415 = (bf16[1280,768]{1,0:T(8,128)(2,1)S(1)}, f32[64,768]{1,0:T(8,128)}, f32[8,768]{1,0:T(8,128)}) custom-call(bf16[1280,3072]{1,0:T(8,128)(2,1)} %shard_map.414.z_ref.refs_0_, f32[1280,768]{1,0:T(8,128)} %get-tuple-element.119.done_ref, f32[1280,768]{1,0:T(8,128)} %get-tuple-element.98.zero_ref, f32[1280,1]{1,0:T(8,128)} %get-tuple-element.120.inv_ref, ...), custom_call_target="tpu_custom_call" | custom-call | flops 4655677440 | bytes 30000000 | tf_op jit(solution)/shard_map/pallas_call | solution.py:1285
  336.1 5.0 %fusion.19 = bf16[1536,768]{1,0:T(8,128)(2,1)} fusion(bf16[1280,768]{1,0:T(8,128)(2,1)S(1)} %get-tuple-element.125, s32[1280]{0:T(1024)S(1)} %get-tuple-element.159), kind=kOutput, calls=%fused_computation.39 | convolution fusion | flops 3023044608 | bytes 4330496 | tf_op jit(solution)/shard_map/dot_general | solution.py:44
  343.1 2.3 convolution_convert_fusion
  346.4 120.2 %shard_map.416 = (f32[96,768]{1,0:T(8,128)}, f32[96,768]{1,0:T(8,128)}, f32[96,768]{1,0:T(8,128)}, f32[64,128]{1,0:T(8,128)}, f32[16,128]{1,0:T(8,128)}, /*index=5*/bf16[32,48,768]{2,1,0:T(8,128)(2,1)}) custom-call(bf16[1280,3072]{1,0:T(8,128)(2,1)} %shard_map.414.z_ref.refs_0_, bf16[1280,3072]{1,0:T(8,128)(2,1)} %get-tuple-element.112.refs_1_, ...), custom_call_target="tpu_custom_call" | custom-call | tf_op jit(solution)/shard_map/pallas_call | solution.py:833
  471.1 6.3 %conditional.3 = (f32[960,768]{1,0:T(8,128)}) conditional(s32[]{:T(128)} %convert_element_type.178, (f32[32,1024]{1,0:T(8,128)S(1)}, bf16[32,48,768]{2,1,0:T(8,128)(2,1)}) %tuple.66, (s32[1280]{0:T(1024)S(1)}, bf16[1280,768]{1,0:T(8,128)(2,1)S(1)}) %tuple.23), branch_computations={%region_18.19_spmd, %region_19.22_spmd} | conditional | flops 2266398720 | bytes 404044864 | solution.py:1358
  471.2 6.3 %fusion.4 = f32[960,768]{1,0:T(8,128)} fusion(bf16[32,48,768]{2,1,0:T(8,128)(2,1)} %get-tuple-element.29, f32[32,960]{1,0:T(8,128)S(1)} %bitcast.151, f32[48]{0:T(128)S(1)} %iota_convert_fusion), kind=kOutput, calls=%fused_computation.6 | convolution fusion | flops 2266398720 | bytes 5431488 | tf_op jit(solution)/shard_map/cond/branch_0_fun/dot_general | solution.py:44
  477.5 2.3 multiply_subtract_fusion.3
  486.3 6.3 %multiply_subtract_fusion = (f32[960,768]{1,0:T(8,128)}, f32[960,768]{1,0:T(8,128)}) fusion(f32[960,768]{1,0:T(8,128)S(1)} %copy-done.7, f32[960,768]{1,0:T(8,128)} %get-tuple-element.220, f32[960,768]{1,0:T(8,128)} %param.39, f32[]{:T(128)} %bitcast.39, f32[]{:T(128)} %bitcast.38, f32[960,768]{1,0:T(8,128)} %param.40), kind=kLoop, calls=%fused_computation.41 | loop fusion | flops 11059200 | bytes 17694728 | tf_op jit(solution)/shard_map/sub | solution.py:1036
  (200 shorter events, 46.9 us)
Async XLA Ops:
  16.0 111.0 %copy-start.27 = (s32[1,1024]{1,0:T(1,128)S(1)}, s32[1,1024]{1,0:T(1,128)}, u32[]{:S(2)}) copy-start(s32[1,1024]{1,0:T(1,128)} %param.31) | copy-start | bytes 12292
  134.1 32.7 %copy-start.5 = (s32[10,1,256]{2,1,0:T(1,128)}, s32[10,1,256]{2,1,0:T(1,128)S(1)}, u32[]{:S(2)}) copy-start(s32[10,1,256]{2,1,0:T(1,128)S(1)} %constant_dynamic-update-slice_fusion.refs_1_) | copy-start | bytes 30724
  134.3 32.4 %copy-start.1 = (s32[1280,1]{1,0:T(8,128)}, s32[1280,1]{1,0:T(8,128)S(1)}, u32[]{:S(2)}) copy-start(s32[1280,1]{1,0:T(8,128)S(1)} %broadcast_in_dim.21.refs_0_) | copy-start | bytes 15364
  155.0 77.7 %all-gather.6.cloned.1.call-start = ((), (), s32[]{:S(2)}) async-start(), calls=%async_computation.3 | async-start | bytes 1638400 | tf_op jit(solution)/shard_map/all_gather | solution.py:1191
  185.1 29.3 %copy-start.38 = (s32[1,1024]{1,0:T(1,128)S(1)}, s32[1,1024]{1,0:T(1,128)}, u32[]{:S(2)}) copy-start(s32[1,1024]{1,0:T(1,128)} %param.36) | copy-start | bytes 12292
  214.2 5.6 %copy-start.3 = (bf16[1280,768]{1,0:T(8,128)(2,1)S(1)}, bf16[1280,768]{1,0:T(8,128)(2,1)}, u32[]{:S(2)}) copy-start(bf16[1280,768]{1,0:T(8,128)(2,1)} %copy-done.2) | copy-start | bytes 5898244
  219.8 12.9 %copy-start.11 = (bf16[1280,128]{1,0:T(8,128)(2,1)S(1)}, bf16[1280,128]{1,0:T(8,128)(2,1)}, u32[]{:S(2)}) copy-start(bf16[1280,128]{1,0:T(8,128)(2,1)} %get-tuple-element.101) | copy-start | bytes 983044
  336.0 5.2 %copy-start.28 = (f32[8,768]{1,0:T(8,128)S(1)}, f32[8,768]{1,0:T(8,128)}, u32[]{:S(2)}) copy-start(f32[8,768]{1,0:T(8,128)} %get-tuple-element.123) | copy-start | bytes 73732
  336.1 5.3 %copy-start.29 = (f32[1,3072]{1,0:T(1,128)S(1)}, f32[1,3072]{1,0:T(1,128)}, u32[]{:S(2)}) copy-start(f32[1,3072]{1,0:T(1,128)} %get-tuple-element.124) | copy-start | bytes 36868
  336.1 7.0 %copy-start.40 = (bf16[1280,128]{1,0:T(8,128)(2,1)S(1)}, bf16[1280,128]{1,0:T(8,128)(2,1)}, u32[]{:S(2)}) copy-start(bf16[1280,128]{1,0:T(8,128)(2,1)} %get-tuple-element.118) | copy-start | bytes 983044
  346.4 124.7 %copy-start.37 = (f32[32,1024]{1,0:T(8,128)S(1)}, f32[32,1024]{1,0:T(8,128)}, u32[]{:S(2)}) copy-start(f32[32,1024]{1,0:T(8,128)} %get-tuple-element.128) | copy-start | bytes 393220
  471.1 6.4 %copy-start.13 = (f32[768,96]{0,1:T(8,128)S(1)}, f32[768,96]{0,1:T(8,128)}, u32[]{:S(2)}) copy-start(f32[768,96]{0,1:T(8,128)} %param.41) | copy-start | bytes 884740
  471.1 8.7 %copy-start.14 = (f32[768,96]{0,1:T(8,128)S(1)}, f32[768,96]{0,1:T(8,128)}, u32[]{:S(2)}) copy-start(f32[768,96]{0,1:T(8,128)} %param.44) | copy-start | bytes 884740
  477.4 6.8 %copy-start.22 = (f32[24,128]{1,0:T(8,128)S(1)}, f32[24,128]{1,0:T(8,128)}, u32[]{:S(2)}) copy-start(f32[24,128]{1,0:T(8,128)} %param.50) | copy-start | bytes 36868
  477.4 8.8 %copy-start.7 = (f32[960,768]{1,0:T(8,128)S(1)}, f32[960,768]{1,0:T(8,128)}, u32[]{:S(2)}) copy-start(f32[960,768]{1,0:T(8,128)} %param.38) | copy-start | bytes 8847364
  477.4 6.8 %copy-start.30 = (f32[24,128]{1,0:T(8,128)S(1)}, f32[24,128]{1,0:T(8,128)}, u32[]{:S(2)}) copy-start(f32[24,128]{1,0:T(8,128)} %param.51) | copy-start | bytes 36868
  477.4 6.8 %copy-start.31 = (f32[24,128]{1,0:T(8,128)S(1)}, f32[24,128]{1,0:T(8,128)}, u32[]{:S(2)}) copy-start(f32[24,128]{1,0:T(8,128)} %param.52) | copy-start | bytes 36868
  477.5 8.1 %copy-start.24 = (f32[1872]{0:T(1024)S(1)}, f32[1872]{0:T(1024)}, u32[]{:S(2)}) copy-start(f32[1872]{0:T(1024)} %param.53) | copy-start | bytes 22468
  477.5 8.1 %copy-start.32 = (f32[1872]{0:T(1024)S(1)}, f32[1872]{0:T(1024)}, u32[]{:S(2)}) copy-start(f32[1872]{0:T(1024)} %param.54) | copy-start | bytes 22468
  477.5 8.1 %copy-start.33 = (f32[1872]{0:T(1024)S(1)}, f32[1872]{0:T(1024)}, u32[]{:S(2)}) copy-start(f32[1872]{0:T(1024)} %param.55) | copy-start | bytes 22468
  477.5 8.1 %copy-start.34 = (f32[16,128]{1,0:T(8,128)S(1)}, f32[16,128]{1,0:T(8,128)}, u32[]{:S(2)}) copy-start(f32[16,128]{1,0:T(8,128)} %get-tuple-element.126) | copy-start | bytes 24580
  486.2 6.3 %copy-start.18 = (f32[96,768]{1,0:T(8,128)S(1)}, f32[96,768]{1,0:T(8,128)}, u32[]{:S(2)}) copy-start(f32[96,768]{1,0:T(8,128)} %get-tuple-element.130) | copy-start | bytes 884740
  486.3 7.0 %copy-start.17 = (f32[96,768]{1,0:T(8,128)S(1)}, f32[96,768]{1,0:T(8,128)}, u32[]{:S(2)}) copy-start(f32[96,768]{1,0:T(8,128)} %get-tuple-element.131) | copy-start | bytes 884740
  486.3 7.8 %copy-start.16 = (f32[96,768]{1,0:T(8,128)S(1)}, f32[96,768]{1,0:T(8,128)}, u32[]{:S(2)}) copy-start(f32[96,768]{1,0:T(8,128)} %get-tuple-element.211) | copy-start | bytes 884740
  (18 other events, 48.2 us)
Sparse Core Ops, SparseCore 1:
  214.3 18.3 all-gather.5

commit v5 on v4

--- a/solution.py
+++ b/solution.py
@@ -130,11 +130,11 @@
             parts.append(matmul(probs, value))
             kept = jnp.where(lane_head == 2 * pair + half, top + jnp.log(total), kept)
         o_ref[:, at : at + 2 * HD] = jnp.where(lane < HD, parts[0], parts[1]).astype(BF)
-    lse_ref[...] = kept
+    lse_ref[...] = kept.T[:16]
 
 
 def attn_backward_kernel(
-    count, blocks, segc_ref, segw_ref, z_ref, do_ref, lse_ref, one_ref, dz_ref, dk_ref, dv_ref
+    count, blocks, segr_ref, segw_ref, z_ref, do_ref, lse_ref, one_ref, dz_ref, dk_ref, dv_ref
 ):
     block = pl.program_id(0)
     row = pl.multiple_of(block * BLK, BLK)
@@ -145,9 +145,8 @@
         dk_ref[...] = jnp.zeros_like(dk_ref)
         dv_ref[...] = jnp.zeros_like(dv_ref)
 
-    allowed = segc_ref[...] == segw_ref[0]
+    allowed = segw_ref[0] == segr_ref[0]
     lane = lax.broadcasted_iota(jnp.int32, (BLK, 2 * HD), 1)
-    kept = lse_ref[...]
     for pair in range(HEADS // 2):
         at = pair * 2 * HD
         query = z_ref[pl.ds(row, BLK), at : at + 2 * HD] * BF(HD ** (-0.5))
@@ -161,14 +160,15 @@
             mine = (lane >= half * HD) & (lane < (half + 1) * HD)
             query_own = jnp.where(mine, query, BF(0))
             up_own = jnp.where(mine, upstream, BF(0))
-            scores = jnp.where(allowed, contract_cols(query_own, key), -1000000000.0)
-            probs = jnp.exp(scores - kept[:, 2 * pair + half : 2 * pair + half + 1])
-            grad_probs = contract_cols(up_own, value)
-            grad_value = grad_value + contract_rows(probs.astype(BF), up_own)
-            inner = jnp.sum(grad_probs * probs, axis=-1, keepdims=True)
+            head = 2 * pair + half
+            scores = jnp.where(allowed, contract_cols(key, query_own), -1000000000.0)
+            probs = jnp.exp(scores - lse_ref[head : head + 1, :])
+            grad_probs = contract_cols(value, up_own)
+            grad_value = grad_value + matmul(probs.astype(BF), up_own)
+            inner = jnp.sum(grad_probs * probs, axis=0, keepdims=True)
             grad_scores = (probs * (grad_probs - inner)).astype(BF)
-            grad_query.append(matmul(grad_scores, key))
-            grad_key = grad_key + contract_rows(grad_scores, query_own)
+            grad_query.append(contract_rows(grad_scores, key))
+            grad_key = grad_key + matmul(grad_scores, query_own)
         own = jnp.where(lane < HD, grad_query[0], grad_query[1]) * HD ** (-0.5)
         dz_ref[pl.ds(row, BLK), at : at + 2 * HD] = own.astype(BF)
         dk_ref[pl.ds(first, WIN), at : at + 2 * HD] += grad_key
@@ -199,11 +199,11 @@
         in_specs=attention_specs(count),
         out_specs=[
             pl.BlockSpec((BLK, D), lambda i: (i, 0)),
-            pl.BlockSpec((BLK, 128), lambda i: (i, 0)),
+            pl.BlockSpec((16, BLK), lambda i: (0, i)),
         ],
         out_shape=[
             jax.ShapeDtypeStruct((count, D), BF),
-            jax.ShapeDtypeStruct((count, 128), F32),
+            jax.ShapeDtypeStruct((16, count), F32),
         ],
         compiler_params=pltpu.CompilerParams(vmem_limit_bytes=40 * 2**20),
         cost_estimate=pl.CostEstimate(
@@ -212,16 +212,18 @@
     )(segment_column, segment_windows, mixed)
 
 
-def attention_backward(segment_column, segment_windows, mixed, upstream, kept, beside):
+def attention_backward(segment_rows, segment_windows, mixed, upstream, kept, beside):
     count = mixed.shape[0]
     blocks = count // BLK
     return pl.pallas_call(
         lambda *refs: attn_backward_kernel(count, blocks, *refs),
         grid=(blocks,),
-        in_specs=attention_specs(count)
-        + [
+        in_specs=[
+            pl.BlockSpec((1, 1, BLK), lambda i: (i, 0, 0)),
+            pl.BlockSpec((1, WIN, 1), lambda i: (i, 0, 0)),
+            pl.BlockSpec((count, 3 * D), lambda i: (0, 0), pipeline_mode=pl.Buffered(1)),
             pl.BlockSpec((BLK, D), lambda i: (i, 0)),
-            pl.BlockSpec((BLK, 128), lambda i: (i, 0)),
+            pl.BlockSpec((16, BLK), lambda i: (0, i)),
             pl.BlockSpec((BLK, D), lambda i: (i, 0)),
         ],
         out_specs=pl.BlockSpec((count, 4 * D), lambda i: (0, 0)),
@@ -231,7 +233,7 @@
         cost_estimate=pl.CostEstimate(
             flops=10 * count * WIN * 128 * HEADS, bytes_accessed=18000000, transcendentals=0
         ),
-    )(segment_column, segment_windows, mixed, upstream, kept, beside)
+    )(segment_rows, segment_windows, mixed, upstream, kept, beside)
 
 
 def place_of():
@@ -301,10 +303,10 @@
 
 
 def gather_kernel(devices, pieces, *refs):
-    matrices = 3
-    sources, (needed, notes, table) = refs[:matrices], refs[matrices : matrices + 3]
-    outs, (notes_out, rows_out, rank) = refs[6:9], refs[9:12]
-    asked, earlier, packed, arrive, beside, leave, local, notes_sem, ask_sem, rows_sem = refs[12:]
+    matrices = 4
+    sources, (needed, table) = refs[:matrices], refs[matrices : matrices + 2]
+    outs, (rows_out, rank) = refs[6:10], refs[10:12]
+    asked, earlier, packed, arrive, beside, leave, local, ask_sem, rows_sem = refs[12:]
     me = place_of()
     group = max(devices // 8, 1)
     greet_all(devices, me)
@@ -365,17 +367,11 @@
     for piece in range(len(pieces)):
         send_on(piece, 0, -1)
 
-    @pl.loop(1, devices)
-    def _(i):
-        target = (me + i) % devices
-        push(notes, notes_out.at[me], target, notes_sem.at[0], notes_sem.at[1])
-
     own = [
         pltpu.make_async_copy(source, out.at[me], local.at[i])
         for i, (source, out) in enumerate(zip(sources, outs))
     ]
-    own.append(pltpu.make_async_copy(notes, notes_out.at[me], local.at[matrices]))
-    own_asked = pltpu.make_async_copy(needed.at[me], asked.at[me], local.at[matrices + 1])
+    own_asked = pltpu.make_async_copy(needed.at[me], asked.at[me], local.at[matrices])
     for copy in own:
         copy.start()
     own_asked.start()
@@ -391,7 +387,7 @@
     steps = len(pieces[0][3])
     each = -(-(devices - 1) // (len(pieces) * (steps - 1)))
     kept_rows = pltpu.make_async_copy(
-        packed.at[devices - 1], rows_out.at[me], local.at[matrices + 2]
+        packed.at[devices - 1], rows_out.at[me], local.at[matrices + 1]
     )
     sent, made, together = 0, 0, 8
     for step in range(1, steps):
@@ -417,11 +413,10 @@
         copy.wait()
     kept_rows.wait()
     for i in range(2):
-        settle(notes_out.at[pl.ds(0, devices - 1)], notes_sem.at[i])
         settle(rows_out.at[pl.ds(0, devices - 1)], rows_sem.at[i])
 
 
-def gather_all(sources, needed, notes, table, capacity):
+def gather_all(sources, needed, table, capacity):
     devices = needed.shape[0]
     rows = sources[0].shape[0]
     bits = devices.bit_length() - 1
@@ -431,15 +426,16 @@
     pieces = [(0, 0, rows, one), (2, 0, rows, other), (1, cut, rows - cut, one)]
     if cut:
         pieces.append((1, 0, cut, other))
+    pieces.append((3, 0, sources[3].shape[0], one))
     count = max(sum(map(len, gather_plan(p[3], max(devices // 8, 1)))) for p in pieces)
     anywhere = pl.BlockSpec(memory_space=pl.ANY)
     inside = pl.BlockSpec(memory_space=pltpu.VMEM)
     dma = pltpu.SemaphoreType.DMA
-    *gathered, noted, arrived, rank = pl.pallas_call(
+    *gathered, arrived, rank = pl.pallas_call(
         lambda *refs: gather_kernel(devices, pieces, *refs),
-        in_specs=[anywhere] * 3 + [inside] * 3,
+        in_specs=[anywhere] * 4 + [inside] * 2,
         out_specs=[anywhere] * 5 + [inside],
-        out_shape=[jax.ShapeDtypeStruct((devices, *s.shape), s.dtype) for s in (*sources, notes)]
+        out_shape=[jax.ShapeDtypeStruct((devices, *s.shape), s.dtype) for s in sources]
         + [
             jax.ShapeDtypeStruct((devices, capacity, D), BF),
             jax.ShapeDtypeStruct((devices, table.shape[0]), F32),
@@ -454,13 +450,12 @@
             dma((6,)),
             dma((2,)),
             dma((2,)),
-            dma((2,)),
         ],
         compiler_params=pltpu.CompilerParams(
             collective_id=0, has_side_effects=True, vmem_limit_bytes=48 * 2**20
         ),
-    )(*sources, needed, notes, table)
-    return gathered, noted, arrived, rank
+    )(*sources, needed, table)
+    return gathered, arrived, rank
 
 
 def reduce_plan(order, group):
@@ -618,8 +613,8 @@
 
 def product_kernel(devices, pieces, spread, *refs):
     count, computed = len({p[0] for p in pieces}), 3
-    lefts, rights, others, rows_in = refs[:3], refs[3:6], refs[6 : count + 3], refs[count + 3]
-    refs = refs[count + 4 :]
+    lefts, rights, others, rows_in = refs[:3], refs[3:7], refs[7 : count + 4], refs[count + 4]
+    refs = refs[count + 5 :]
     outs, rows_out = refs[:count], refs[count]
     held, landed = refs[count + 1 : 2 * count + 1], refs[2 * count + 1 : 3 * count + 1]
     refs = refs[3 * count + 1 :]
@@ -694,9 +689,11 @@
         )
 
     def slot_of(piece, turn, side):
-        if pieces[piece][3][0] == 1:
-            return (1 - side) * groups + turn
-        return (turn // half) * groups + (1 - side) * half + turn % half
+        slot = 0
+        for bit in pieces[piece][3]:
+            digit = 1 - side if bit == 1 else (turn // (1 << (depth + 1 - bit))) % 2
+            slot = slot * 2 + digit
+        return slot
 
     big = [p for p in range(len(pieces)) if pieces[p][0] < computed]
     small = [p for p in range(len(pieces)) if pieces[p][0] >= computed]
@@ -715,6 +712,9 @@
                 load.at[piece],
             ).start()
 
+    near = (me // 2) % 2
+    core = me % 2
+
     def add(piece, slot, where):
         which, rows = pieces[piece][0], rows_of(piece)
         some = landed[which].at[pl.ds(where, 1), rows]
@@ -727,7 +727,11 @@
             for piece in big:
                 which, rows, bits = pieces[piece][0], rows_of(piece), pieces[piece][3]
                 slot = slot_of(piece, turn, side)
-                held[which][slot, rows] = add(piece, slot, slot).astype(BF)
+                line = (near + side) % 2
+                settle(landed[which].at[pl.ds(slot, 1), rows], arrive.at[piece, slot])
+                total = ready[which][turn * 4 + line * 2 + core, rows].astype(F32)
+                total = total + landed[which][slot, rows].astype(F32)
+                held[which][slot, rows] = total.astype(BF)
 
                 def on():
                     sent = len(plans[piece][0])
@@ -751,19 +755,21 @@
             for which in range(computed):
                 slab_copy(which, turn + 1).start()
 
-        near = (me // 2) % 2
-        core = me % 2
         for which in (0, 2, 1):
             slab_copy(which, turn).wait()
+
+            def product(right):
+                block = contract_rows(slab[turn % 2, which], right[...])
+                block = block.astype(BF).reshape(4, chunk, D)
+                for i in range(4):
+                    ready[which][turn * 4 + i] = block[i]
+
             if which == 0:
-                right = rights[0].at[(group_of(turn) * 4 * chunk) // (3 * D)]
+                first = group_of(turn) * 4 * chunk < 3 * D
+                pl.when(first)(lambda: product(rights[0]))
+                pl.when(jnp.logical_not(first))(lambda: product(rights[1]))
             else:
-                right = rights[which]
-            block = contract_rows(slab[turn % 2, which], right[...])
-            block = block.astype(BF).reshape(4, chunk, D)
-            for side in range(2):
-                for same in range(2):
-                    ready[which][turn * 4 + side * 2 + same] = block[side * 2 + same]
+                product(rights[which + 1])
             for piece in big:
                 if pieces[piece][0] != which:
                     continue
@@ -771,8 +777,6 @@
                 for side in range(2):
                     line = (near + side) % 2
                     slot = slot_of(piece, turn, side)
-                    kept = ready[which].at[turn * 4 + line * 2 + core, rows]
-                    held[which][slot, rows] = kept[...]
                     push(
                         ready[which].at[turn * 4 + line * 2 + 1 - core, rows],
                         landed[which].at[slot, rows],
@@ -822,17 +826,18 @@
     bits = devices.bit_length() - 1
     high = list(range(3, bits))
     one, other = (1, 2, *high), (2, 1, *high)
+    one_early, other_early = (1, *high, 2), (2, *high, 1)
     cut = chunk // 32 * 16
-    pieces = [(0, 0, chunk, one), (2, 0, chunk, other), (1, cut, chunk - cut, one)]
+    pieces = [(0, 0, chunk, one), (2, 0, chunk, other_early), (1, cut, chunk - cut, one_early)]
     pieces += [(1, 0, cut, other), (3, 0, others[0].shape[1], one), (4, 0, others[1].shape[1], other)]
-    spread = [12] + [2] * devices
+    spread = [devices]
     anywhere = pl.BlockSpec(memory_space=pl.ANY)
     inside = pl.BlockSpec(memory_space=pltpu.VMEM)
     dma = pltpu.SemaphoreType.DMA
     kinds = [((chunk, D), BF)] * 3 + [(o.shape[1:], o.dtype) for o in others]
     *reduced, arrived = pl.pallas_call(
         lambda *refs: product_kernel(devices, pieces, spread, *refs),
-        in_specs=[anywhere] * 3 + [inside] * 3 + [anywhere] * (len(others) + 1),
+        in_specs=[anywhere] * 3 + [inside] * 4 + [anywhere] * (len(others) + 1),
         out_specs=[inside] * len(kinds) + [anywhere],
         out_shape=[jax.ShapeDtypeStruct(shape, F32) for shape, _ in kinds]
         + [jax.ShapeDtypeStruct(rows_in.shape, rows_in.dtype)],
@@ -844,7 +849,7 @@
         compiler_params=pltpu.CompilerParams(
             collective_id=2, has_side_effects=True, vmem_limit_bytes=60 * 2**20
         ),
-    )(*lefts, jnp.stack(rights[:2]), *rights[2:], *others, rows_in)
+    )(*lefts, *rights, *others, rows_in)
     return reduced, arrived
 
 
@@ -871,9 +876,16 @@
     return vec_ref[i : i + 1, :]
 
 
-def first_kernel(looked_ref, place_ref, table_ref, vec_ref, qkv_ref, normed_ref, inv_ref, low_ref, z_ref):
-    hot = place_ref[...] == lax.broadcasted_iota(jnp.int32, (TOK, PMAX), 1)
-    values = looked_ref[...] + matmul(hot.astype(F32).astype(BF), table_ref[...])
+def hot_rows(index, depth):
+    hot = index == lax.broadcasted_iota(jnp.int32, (TOK, depth), 1)
+    return hot.astype(F32).astype(BF)
+
+
+def first_kernel(
+    row_ref, place_ref, packed_ref, table_ref, vec_ref, qkv_ref, normed_ref, inv_ref, low_ref, z_ref
+):
+    values = matmul(hot_rows(row_ref[...], packed_ref.shape[0]), packed_ref[...])
+    values = values + matmul(hot_rows(place_ref[...], PMAX), table_ref[...])
     normed, inverse = normalize(values)
     normed_ref[...] = normed
     inv_ref[...] = inverse
@@ -998,8 +1010,7 @@
     sums_ref[3:4, :] += column_sum(z_ref[:, 2 * D : 3 * D].astype(F32))
     low = grad.astype(BF)
     low_ref[...] = low
-    hot = place_ref[...] == lax.broadcasted_iota(jnp.int32, (TOK, PMAX), 1)
-    places_ref[...] += contract_rows(hot.astype(F32).astype(BF), low)
+    places_ref[...] += contract_rows(hot_rows(place_ref[...], PMAX), low)
 
 
 def by_tokens(width):
@@ -1112,10 +1123,9 @@
         ]
     )
     notes = jnp.pad(notes, (0, -notes.size % 2048)).reshape(-1, 128)
-    gathered, noted, packed, asked_rank = gather_all(
-        shards,
+    (*gathered, noted), packed, asked_rank = gather_all(
+        [*shards, notes],
         jnp.pad(needed, ((0, 0), (0, width - shard_rows))).reshape(devices, width // 128, 128),
-        notes,
         table,
         capacity,
     )
@@ -1131,17 +1141,19 @@
     pair_floor = jnp.maximum(jnp.sum(pairs_all.astype(F32)), 1.0)
     place_row = jnp.arange(shard_rows, dtype=jnp.int32)
     earlier = (place_row[:, None] < place_row[None, :]).astype(BF)
-    overflow = jnp.max(packed[:, capacity - 1, :].astype(F32)) > 0.5 * MARK
+    overflow = jnp.max(packed[:, capacity - 1, :1].astype(F32)) > 0.5 * MARK
     packed = packed.reshape(devices * capacity, D)
     needed_rank = jnp.minimum(matmul(needed.astype(BF), earlier), 255.0)
     token_rank = jnp.sum(matmul(owner_hot, needed_rank.astype(BF)) * row_hot.astype(F32), axis=1)
     slot = owner * capacity + jnp.minimum(token_rank.astype(jnp.int32), capacity - 1)
     slot_hot = one_hot(slot, devices * capacity)
-    looked_up = lax.cond(
-        overflow,
-        lambda: lax.all_gather(embed_table.astype(BF), ALL, axis=0, tiled=True)[tokens].astype(F32),
-        lambda: matmul(slot_hot, packed),
-    )
+
+    def whole_lookup():
+        rows = lax.all_gather(embed_table.astype(BF), ALL, axis=0, tiled=True)[tokens]
+        rows = jnp.pad(rows, ((0, devices * capacity - count), (0, 0)))
+        return rows, jnp.arange(count, dtype=jnp.int32)
+
+    packed, row_of = lax.cond(overflow, whole_lookup, lambda: (packed, slot))
 
     positions = small_all[: PMAX * D].reshape(PMAX, D)
     remainder = small_all[PMAX * D :].astype(F32)
@@ -1152,10 +1164,11 @@
     norm_zero, inverse_zero, input_zero, mixed = token_call(
         first_kernel,
         count,
-        [by_tokens(D), by_tokens(1), resident(PMAX, D), resident(16, D), resident(3 * D, D)],
+        [by_tokens(1), by_tokens(1), resident(devices * capacity, D)]
+        + [resident(PMAX, D), resident(16, D), resident(3 * D, D)],
         [(None, D, F32), (None, 1, F32), (None, D, BF), (None, 3 * D, BF)],
         2 * count * D * (3 * D + PMAX),
-    )(looked_up, place_column, positions, vectors, attn_rows)
+    )(row_of[:, None], place_column, packed, positions, vectors, attn_rows)
     context, kept = attention_forward(segment_column, segment_windows, mixed)
     weight_specs = [
         resident(D, D, 3),
@@ -1280,7 +1293,12 @@
     )
     grad_head = contract_rows(input_two, grad_proj)
     grad_attn = attention_backward(
-        segment_column, segment_windows, mixed, grad_context, kept, grad_one_low
+        segment.reshape(-1, 1, BLK),
+        segment_windows.transpose(0, 2, 1),
+        mixed,
+        grad_context,
+        kept,
+        grad_one_low,
     )
     grad_low, grad_positions, sums_zero = token_call(
         first_back_kernel,

time: 506 us -> 484 us (0.957); the launches traced: 503 us -> 475 us
  loops' own time: 11.3 us -> 0.02 us
  matrix products: 41.6 us -> 31.3 us
  other arithmetic: 32.5 us -> 24.8 us
  Pallas kernels: 360 us -> 354 us
  local copies, waits for them, and re-layouts: 23.6 us -> 29 us
    another operation x1, loops' own time: 11.3 us -> 0.01 us  [on_device(): packed, row_of = lax.cond(overflow, whole_lookup, lambda: (packed, slot))]
    dot_general x4 -> x3, matrix products: 11.1 us -> 3.11 us  [matmul(): return jnp.dot(lhs_mat, rhs_mat, preferred_element_type=jnp.float32)]
    pallas_call x1, Pallas kernels: 11.7 us -> 18.3 us  [on_device(): token_call(first_kernel, count, [by_tokens(1), by_tokens(1), resident(dev...]
    pallas_call x1, Pallas kernels: 108 us -> 102 us  [gather_all(): pl.pallas_call(lambda *refs: gather_kernel(devices, pieces, *refs), in_sp...]
    unnamed x108 -> x102, local copies, waits for them, and re-layouts: 10.5 us -> 11.3 us
  transfers between devices with their start and end apart: 1 -> 1, of which waited for: 1 -> 1; matrix products, arithmetic and copies ran while one was open for 2% -> 1% of each run, Pallas kernels for 0% -> 0%
where the time goes in v5:
time: 484 us; the launch traced here: 475 us
  Pallas kernels  354 us (73%)
  matrix products  31.3 us (6%)
  local copies, waits for them, and re-layouts  29 us (6%)
  other arithmetic  24.8 us (5%)
  between operations  20.5 us (4%)
  waiting for transfers between devices  9.76 us (2%)
  blocking collectives  5.17 us (1%)
    pallas_call x1, Pallas kernels, reduce_products(): pl.pallas_call(lambda *refs: product_kernel(devices, pieces, spread, *ref...  118 us
    pallas_call x1, Pallas kernels, gather_all(): pl.pallas_call(lambda *refs: gather_kernel(devices, pieces, *refs), in_sp...  102 us
    pallas_call x1, Pallas kernels, attention_backward(): pl.pallas_call(lambda *refs: attn_backward_kernel(count, blocks, *refs),...  33.3 us
    pallas_call x1, Pallas kernels, on_device(): token_call(middle_kernel, count, [by_tokens(D), by_tokens(D), resident(16...  29.6 us
    pallas_call x1, Pallas kernels, on_device(): token_call(middle_back_kernel, count, [by_tokens(DC), by_tokens(DC), by_t...  27.6 us
    dot_general x6, matrix products, contract_rows(): lax.dot_general(lhs_mat, rhs_mat, (((0,), (0,)), ((), ())), preferred_ele...  20 us
    pallas_call x1, Pallas kernels, on_device(): token_call(first_kernel, count, [by_tokens(1), by_tokens(1), resident(dev...  18.3 us
    sub x6, other arithmetic, adam_update(): weight - rate * (corrected / (jnp.sqrt(scaled) + ADAM_EPS) + WEIGHT_DECAY...  14.8 us
  transfers between devices with their start and end apart: 1, of which 1 were waited for; matrix products, arithmetic and copies ran while one was open for 1% of the time, Pallas kernels for 0%

profile of v5, /device:TPU:0, one launch (start us, length us, event | category | flops | bytes accessed | tf_op | source)
XLA Modules:
  0.0 475.2 jit_solution(468388908838749657)
XLA Ops:
  16.3 1.5 pad.32.refs_5_
  17.8 101.6 %shard_map.409 = (bf16[32,96,768]{2,1,0:T(8,128)(2,1)}, bf16[32,96,768]{2,1,0:T(8,128)(2,1)}, bf16[32,96,768]{2,1,0:T(8,128)(2,1)}, bf16[32,48,128]{2,1,0:T(8,12...) custom-call(bf16[96,768]{1,0:T(8,128)(2,1)S(1)} %get-tuple-element.213.refs_0_, ...), custom_call_target="tpu_custom_call" | custom-call | tf_op jit(solution)/shard_map/pallas_call | solution.py:434
  128.1 18.3 %shard_map.410 = (f32[1280,768]{1,0:T(8,128)}, f32[1280,1]{1,0:T(8,128)}, bf16[1280,768]{1,0:T(8,128)(2,1)}, bf16[1280,2304]{1,0:T(8,128)(2,1)}) custom-call(s32[1280,1]{1,0:T(8,128)} %get-tuple-element.168.row_ref, s32[1280,1]{1,0:T(8,128)} %broadcast_in_dim.25.place_ref, bf16[1536,768]{1,0:T(8,128)(2,1)} %get-tuple-element.128.packed_ref, ...), custom_call_target="tpu_custom_call" | custom-call | flops 4655677440 | bytes 30000000 | tf_op jit(solution)/shard_map/pallas_call | solution.py:1164
  146.4 2.7 copy-done
  149.1 13.6 %shard_map.411 = (bf16[1280,768]{1,0:T(8,128)(2,1)S(1)}, f32[16,1280]{1,0:T(8,128)S(1)}) custom-call(s32[1280,1]{1,0:T(8,128)S(1)} %broadcast_in_dim.23.refs_0_, s32[10,1,256]{2,1,0:T(1,128)S(1)} %constant_dynamic-update-slice_fusion.refs_1_, bf16[1280,2304]{1,0:T(8,128)(2,1)S(1)} %copy-done), custom_call_target="tpu_custom_call" | custom-call | flops 2013265920 | bytes 12000000 | tf_op jit(solution)/shard_map/pallas_call | solution.py:196
  164.5 29.6 %shard_map.412 = (f32[1280,768]{1,0:T(8,128)}, f32[1280,1]{1,0:T(8,128)}, bf16[1280,768]{1,0:T(8,128)(2,1)}, bf16[1280,3072]{1,0:T(8,128)(2,1)}, bf16[1280,3072]...) custom-call(bf16[1280,768]{1,0:T(8,128)(2,1)} %copy-done.1, ...), custom_call_target="tpu_custom_call" | custom-call | flops 13841203200 | bytes 30000000 | tf_op jit(solution)/shard_map/pallas_call | solution.py:1193
  194.9 1.5 copy.83.refs_1_
  197.0 2.4 fusion.33
  201.9 9.7 %all-gather.6.cloned.1.call-done = bf16[5120,128]{1,0:T(8,128)(2,1)} async-done(((bf16[1280,128]{1,0:T(8,128)(2,1)}), bf16[5120,128]{1,0:T(8,128)(2,1)}) %all-gather.6.cloned.1.call-update) | async-done | bytes 1310736 | tf_op jit(solution)/shard_map/all_gather | solution.py:1204
  211.6 2.0 fusion.51
  217.4 5.2 %all_gather.14 = f32[32,128]{1,0:T(8,128)S(1)} all-gather(f32[8,128]{1,0:T(8,128)S(1)} %select_subtract_fusion), channel_id=1, replica_groups=mesh['grp'=8,'psg'=4] {'psg'}, dimensions={0}, use_global_device_ids=true | all-gather | bytes 20480 | tf_op jit(solution)/shard_map/all_gather | solution.py:1241
  226.8 4.4 fusion.31
  231.7 3.9 fusion.38
  236.5 27.6 %shard_map.413 = (bf16[1280,128]{1,0:T(8,128)(2,1)}, bf16[1280,768]{1,0:T(8,128)(2,1)}, bf16[1280,3072]{1,0:T(8,128)(2,1)}, f32[1280,768]{1,0:T(8,128)}, bf16[12...) custom-call(f32[1280,128]{1,0:T(8,128)} %pad_maximum_fusion.grad_ref, ...), custom_call_target="tpu_custom_call" | custom-call | flops 13841203200 | bytes 30000000 | tf_op jit(solution)/shard_map/pallas_call | solution.py:1274
  264.1 33.3 %shard_map.414.z_ref.refs_0_ = bf16[1280,3072]{1,0:T(8,128)(2,1)} custom-call(s32[10,1,128]{2,1,0:T(1,128)} %reshape.400.refs_0_, s32[10,256,1]{2,1,0:T(8,128)} %copy.83.refs_1_, bf16[1280,2304]{1,0:T(8,128)(2,1)} %get-tuple-element.131.refs_2_, bf16[1280,768]{1,0:T(8,128)(2,1)} %get-tuple-element.144.refs_3_, f32[16,1280]{1,0:T(8,128)} %copy-done.2, ...), custom_call_target="tpu_custom_call" | custom-call | flops 5033164800 | bytes 18000000 | tf_op jit(solution)/shard_map/pallas_call | solution.py:218
  297.4 12.7 %shard_map.415 = (bf16[1280,768]{1,0:T(8,128)(2,1)S(1)}, f32[64,768]{1,0:T(8,128)}, f32[8,768]{1,0:T(8,128)}) custom-call(bf16[1280,3072]{1,0:T(8,128)(2,1)} %shard_map.414.z_ref.refs_0_, f32[1280,768]{1,0:T(8,128)} %get-tuple-element.154.done_ref, f32[1280,768]{1,0:T(8,128)} %get-tuple-element.133.zero_ref, f32[1280,1]{1,0:T(8,128)} %get-tuple-element.155.inv_ref, ...), custom_call_target="tpu_custom_call" | custom-call | flops 4655677440 | bytes 30000000 | tf_op jit(solution)/shard_map/pallas_call | solution.py:1303
  313.7 5.0 %fusion.21 = bf16[1536,768]{1,0:T(8,128)(2,1)} fusion(bf16[1280,768]{1,0:T(8,128)(2,1)S(1)} %get-tuple-element.160, s32[1280]{0:T(1024)S(1)} %get-tuple-element.194), kind=kOutput, calls=%fused_computation.43 | convolution fusion | flops 3023044608 | bytes 4330496 | tf_op jit(solution)/shard_map/dot_general | solution.py:44
  320.5 117.8 %shard_map.416 = (f32[96,768]{1,0:T(8,128)}, f32[96,768]{1,0:T(8,128)}, f32[96,768]{1,0:T(8,128)}, f32[64,128]{1,0:T(8,128)}, f32[16,128]{1,0:T(8,128)}, /*index=5*/bf16[32,48,768]{2,1,0:T(8,128)(2,1)}) custom-call(bf16[1280,3072]{1,0:T(8,128)(2,1)} %shard_map.414.z_ref.refs_0_, bf16[1280,3072]{1,0:T(8,128)(2,1)} %get-tuple-element.147.refs_1_, ...), custom_call_target="tpu_custom_call" | custom-call | tf_op jit(solution)/shard_map/pallas_call | solution.py:838
  442.8 6.3 %conditional.3 = (f32[960,768]{1,0:T(8,128)}) conditional(s32[]{:T(128)} %convert_element_type.175, (f32[32,1024]{1,0:T(8,128)S(1)}, bf16[32,48,768]{2,1,0:T(8,128)(2,1)}) %tuple.75, (s32[1280]{0:T(1024)S(1)}, bf16[1280,768]{1,0:T(8,128)(2,1)S(1)}) %tuple.27), branch_computations={%region_18.19_spmd, %region_19.22_spmd} | conditional | flops 2266398720 | bytes 404044864 | solution.py:1376
  442.9 6.3 %fusion.7 = f32[960,768]{1,0:T(8,128)} fusion(bf16[32,48,768]{2,1,0:T(8,128)(2,1)} %get-tuple-element.60, f32[32,960]{1,0:T(8,128)S(1)} %bitcast.147, f32[48]{0:T(128)S(1)} %iota_convert_fusion), kind=kOutput, calls=%fused_computation.12 | convolution fusion | flops 2266398720 | bytes 5431488 | tf_op jit(solution)/shard_map/cond/branch_0_fun/dot_general | solution.py:44
  449.2 2.3 multiply_subtract_fusion.3
  451.5 2.2 multiply_subtract_fusion.2
  453.7 2.1 multiply_subtract_fusion.1
  457.8 6.3 %multiply_subtract_fusion = (f32[960,768]{1,0:T(8,128)}, f32[960,768]{1,0:T(8,128)}) fusion(f32[960,768]{1,0:T(8,128)S(1)} %copy-done.4, f32[960,768]{1,0:T(8,128)} %get-tuple-element.265, f32[960,768]{1,0:T(8,128)} %param.39, f32[]{:T(128)} %bitcast.38, f32[]{:T(128)} %bitcast.37, f32[960,768]{1,0:T(8,128)} %param.40), kind=kLoop, calls=%fused_computation.45 | loop fusion | flops 11059200 | bytes 17694728 | tf_op jit(solution)/shard_map/sub | solution.py:1047
  (197 shorter events, 44.1 us)
Async XLA Ops:
  12.2 3.1 copy-start.9
  127.9 83.8 %all-gather.6.cloned.1.call-start = ((), (), s32[]{:S(2)}) async-start(), calls=%async_computation.3 | async-start | bytes 1638400 | tf_op jit(solution)/shard_map/all_gather | solution.py:1204
  146.4 2.7 copy-start
  164.5 31.9 %copy-start.34 = (s32[1,1024]{1,0:T(1,128)S(1)}, s32[1,1024]{1,0:T(1,128)}, u32[]{:S(2)}) copy-start(s32[1,1024]{1,0:T(1,128)} %param.36) | copy-start | bytes 12292
  194.2 17.5 %copy-start.8 = (bf16[1280,128]{1,0:T(8,128)(2,1)S(1)}, bf16[1280,128]{1,0:T(8,128)(2,1)}, u32[]{:S(2)}) copy-start(bf16[1280,128]{1,0:T(8,128)(2,1)} %get-tuple-element.136) | copy-start | bytes 983044
  297.4 14.4 %copy-start.24 = (f32[8,768]{1,0:T(8,128)S(1)}, f32[8,768]{1,0:T(8,128)}, u32[]{:S(2)}) copy-start(f32[8,768]{1,0:T(8,128)} %get-tuple-element.158) | copy-start | bytes 73732
  297.4 14.5 %copy-start.25 = (f32[1,3072]{1,0:T(1,128)S(1)}, f32[1,3072]{1,0:T(1,128)}, u32[]{:S(2)}) copy-start(f32[1,3072]{1,0:T(1,128)} %get-tuple-element.159) | copy-start | bytes 36868
  313.7 5.0 %copy-start.36 = (bf16[1280,768]{1,0:T(8,128)(2,1)S(1)}, bf16[1280,768]{1,0:T(8,128)(2,1)}, u32[]{:S(2)}) copy-start(bf16[1280,768]{1,0:T(8,128)(2,1)} %get-tuple-element.152) | copy-start | bytes 5898244
  313.7 5.0 %copy-start.37 = (bf16[1280,128]{1,0:T(8,128)(2,1)S(1)}, bf16[1280,128]{1,0:T(8,128)(2,1)}, u32[]{:S(2)}) copy-start(bf16[1280,128]{1,0:T(8,128)(2,1)} %get-tuple-element.153) | copy-start | bytes 983044
  320.5 122.3 %copy-start.33 = (f32[32,1024]{1,0:T(8,128)S(1)}, f32[32,1024]{1,0:T(8,128)}, u32[]{:S(2)}) copy-start(f32[32,1024]{1,0:T(8,128)} %get-tuple-element.163) | copy-start | bytes 393220
  442.8 6.4 %copy-start.10 = (f32[768,96]{0,1:T(8,128)S(1)}, f32[768,96]{0,1:T(8,128)}, u32[]{:S(2)}) copy-start(f32[768,96]{0,1:T(8,128)} %param.41) | copy-start | bytes 884740
  442.8 8.7 %copy-start.11 = (f32[768,96]{0,1:T(8,128)S(1)}, f32[768,96]{0,1:T(8,128)}, u32[]{:S(2)}) copy-start(f32[768,96]{0,1:T(8,128)} %param.44) | copy-start | bytes 884740
  449.1 8.7 %copy-start.4 = (f32[960,768]{1,0:T(8,128)S(1)}, f32[960,768]{1,0:T(8,128)}, u32[]{:S(2)}) copy-start(f32[960,768]{1,0:T(8,128)} %param.38) | copy-start | bytes 8847364
  449.1 4.6 copy-start.13
  449.1 4.6 copy-start.14
  449.1 6.6 %copy-start.18 = (f32[24,128]{1,0:T(8,128)S(1)}, f32[24,128]{1,0:T(8,128)}, u32[]{:S(2)}) copy-start(f32[24,128]{1,0:T(8,128)} %param.50) | copy-start | bytes 36868
  449.1 6.6 %copy-start.26 = (f32[24,128]{1,0:T(8,128)S(1)}, f32[24,128]{1,0:T(8,128)}, u32[]{:S(2)}) copy-start(f32[24,128]{1,0:T(8,128)} %param.51) | copy-start | bytes 36868
  449.2 6.6 %copy-start.27 = (f32[24,128]{1,0:T(8,128)S(1)}, f32[24,128]{1,0:T(8,128)}, u32[]{:S(2)}) copy-start(f32[24,128]{1,0:T(8,128)} %param.52) | copy-start | bytes 36868
  449.2 8.0 %copy-start.20 = (f32[1872]{0:T(1024)S(1)}, f32[1872]{0:T(1024)}, u32[]{:S(2)}) copy-start(f32[1872]{0:T(1024)} %param.53) | copy-start | bytes 22468
  449.2 8.0 %copy-start.28 = (f32[1872]{0:T(1024)S(1)}, f32[1872]{0:T(1024)}, u32[]{:S(2)}) copy-start(f32[1872]{0:T(1024)} %param.54) | copy-start | bytes 22468
  449.2 7.9 %copy-start.29 = (f32[1872]{0:T(1024)S(1)}, f32[1872]{0:T(1024)}, u32[]{:S(2)}) copy-start(f32[1872]{0:T(1024)} %param.55) | copy-start | bytes 22468
  449.2 7.9 %copy-start.30 = (f32[16,128]{1,0:T(8,128)S(1)}, f32[16,128]{1,0:T(8,128)}, u32[]{:S(2)}) copy-start(f32[16,128]{1,0:T(8,128)} %get-tuple-element.161) | copy-start | bytes 24580
  457.8 6.3 %copy-start.16 = (f32[96,768]{1,0:T(8,128)S(1)}, f32[96,768]{1,0:T(8,128)}, u32[]{:S(2)}) copy-start(f32[96,768]{1,0:T(8,128)} %get-tuple-element.165) | copy-start | bytes 884740
  457.8 7.0 %copy-start.15 = (f32[96,768]{1,0:T(8,128)S(1)}, f32[96,768]{1,0:T(8,128)}, u32[]{:S(2)}) copy-start(f32[96,768]{1,0:T(8,128)} %get-tuple-element.166) | copy-start | bytes 884740
  (15 other events, 26.3 us)
Sparse Core Ops, SparseCore 1:
  194.3 17.3 all-gather.5

commit v6 on v5

--- a/solution.py
+++ b/solution.py
@@ -903,7 +903,22 @@
     context_ref, zero_ref, vec_ref, bias_ref, out_ref, up_ref, down_ref, head_ref, *results
 ):
     one_ref, one_inv_ref, one_low_ref, act_ref, slope_ref = results[:5]
-    two_ref, two_inv_ref, two_low_ref, unit_ref, scale_ref, unit_low_ref = results[5:]
+    two_ref, two_inv_ref, two_low_ref, unit_ref, scale_ref = results[5:10]
+    unit_low_ref, units_ref, mine_ref, sems = results[10:]
+    step = pl.program_id(0)
+    members = lax.axis_size("psg")
+    member = lax.axis_index("psg")
+    peers = [(lax.axis_index("grp"), (member + i) % members) for i in range(1, members)]
+
+    @pl.when(step == 0)
+    def _():
+        barrier = pltpu.get_barrier_semaphore()
+        for peer in peers:
+            pl.semaphore_signal(
+                barrier, inc=1, device_id=peer, device_id_type=pl.DeviceIdType.MESH
+            )
+        pl.semaphore_wait(barrier, members - 1)
+
     hidden = zero_ref[...] * (1.0 + vector(vec_ref, 0)) + vector(vec_ref, 1)
     hidden = hidden + contract_cols(context_ref[...], out_ref[...]) + vector(vec_ref, 4)
     normed, inverse = normalize(hidden)
@@ -931,7 +946,27 @@
     scale = lax.rsqrt(jnp.sum(projected * projected, axis=-1, keepdims=True) + NORM_EPS)
     unit_ref[...] = projected * scale
     scale_ref[...] = scale
-    unit_low_ref[...] = (projected * scale).astype(BF)
+    unit_low = (projected * scale).astype(BF)
+    unit_low_ref[...] = unit_low
+    mine_ref[step] = unit_low
+    there = units_ref.at[member, pl.ds(pl.multiple_of(step * TOK, TOK), TOK)]
+    for peer in peers:
+        pltpu.make_async_remote_copy(
+            src_ref=mine_ref.at[step],
+            dst_ref=there,
+            send_sem=sems.at[0],
+            recv_sem=sems.at[1],
+            device_id=peer,
+            device_id_type=pl.DeviceIdType.MESH,
+        ).start()
+    pltpu.make_async_copy(mine_ref.at[step], there, sems.at[2]).start()
+
+    @pl.when(step == mine_ref.shape[0] - 1)
+    def _():
+        for i in range(2):
+            some = units_ref.at[pl.ds(0, members - 1)]
+            pltpu.make_async_copy(some, some, sems.at[i]).wait()
+        pltpu.make_async_copy(units_ref.at[0], units_ref.at[0], sems.at[2]).wait()
 
 
 def column_sum(values):
@@ -1021,7 +1056,7 @@
     return pl.BlockSpec((rows, width), lambda i: (at, 0), pipeline_mode=pl.Buffered(1))
 
 
-def token_call(kernel, count, in_specs, outs, flops):
+def token_call(kernel, count, in_specs, outs, flops, whole=(), scratch=(), **params):
     return pl.pallas_call(
         kernel,
         grid=(count // TOK,),
@@ -1029,23 +1064,31 @@
         out_specs=[
             by_tokens(width) if rows is None else pl.BlockSpec((rows, width), lambda i: (0, 0))
             for rows, width, _ in outs
-        ],
+        ]
+        + [pl.BlockSpec(memory_space=pl.ANY) for _ in whole],
         out_shape=[
             jax.ShapeDtypeStruct((count if rows is None else rows, width), kind)
             for rows, width, kind in outs
-        ],
-        compiler_params=pltpu.CompilerParams(vmem_limit_bytes=56 * 2**20),
+        ]
+        + list(whole),
+        scratch_shapes=list(scratch),
+        compiler_params=pltpu.CompilerParams(vmem_limit_bytes=56 * 2**20, **params),
         cost_estimate=pl.CostEstimate(flops=flops, bytes_accessed=30000000, transcendentals=0),
     )
 
 
-def adam_update(weight, moment, second, gradient, rate, count_steps):
+def adam_step(weight, moment, second, gradient, rate, share_one, share_two):
     moment_new = BETA_ONE * moment + (1.0 - BETA_ONE) * gradient
     second_new = BETA_TWO * second + (1.0 - BETA_TWO) * gradient * gradient
-    corrected = moment_new / (1.0 - BETA_ONE**count_steps)
-    scaled = second_new / (1.0 - BETA_TWO**count_steps)
+    corrected = moment_new / share_one
+    scaled = second_new / share_two
     weight_new = weight - rate * (corrected / (jnp.sqrt(scaled) + ADAM_EPS) + WEIGHT_DECAY * weight)
     return (weight_new, second_new)
+
+
+def adam_update(weight, moment, second, gradient, rate, count_steps):
+    share_one, share_two = 1.0 - BETA_ONE**count_steps, 1.0 - BETA_TWO**count_steps
+    return adam_step(weight, moment, second, gradient, rate, share_one, share_two)
 
 
 def on_device(
@@ -1190,6 +1233,7 @@
         unit,
         scale_inverse,
         unit_low,
+        units,
     ) = token_call(
         middle_kernel,
         count,
@@ -1199,9 +1243,12 @@
         + [(None, D, F32), (None, 1, F32), (None, D, BF)]
         + [(None, DC, F32), (None, 1, F32), (None, DC, BF)],
         middle_flops,
+        [jax.ShapeDtypeStruct((members, count, DC), BF)],
+        [pltpu.VMEM((count // TOK, TOK, DC), BF), pltpu.SemaphoreType.DMA((3,))],
+        collective_id=3,
+        has_side_effects=True,
     )(context, norm_zero, vectors, bias_up, *weights)
 
-    units = lax.all_gather(unit_low, "psg", axis=0)
     group_passage = units[:, :ROW]
     group_query = units[:, ROW:].reshape(members * query_rows, DC)
     own_query = unit_low[ROW:]

time: 484 us -> 472 us (0.975)
  waiting for transfers between devices: 9.76 us -> 0 us
  Pallas kernels: 354 us -> 359 us
    all_gather x1 -> x0, waiting for transfers between devices: 9.74 us -> none  [on_device(): units = lax.all_gather(unit_low, 'psg', axis=0)]
    pallas_call x1, Pallas kernels: 29.6 us -> 35.5 us  [on_device(): token_call(middle_kernel, count, [by_tokens(D), by_tokens(D), resident(16...]
    unnamed x102 -> x116, local copies, waits for them, and re-layouts: 11.3 us -> 11.4 us
  transfers between devices with their start and end apart: 1 -> 0, of which waited for: 1 -> 0; matrix products, arithmetic and copies ran while one was open for 1% -> 0% of each run, Pallas kernels for 0% -> 0%
where the time goes in v6:
time: 472 us; the launch traced here: 465 us
  Pallas kernels  359 us (76%)
  matrix products  35 us (7%)
  local copies, waits for them, and re-layouts  25 us (5%)
  other arithmetic  20.4 us (4%)
  between operations  19.3 us (4%)
  blocking collectives  5.92 us (1%)
    pallas_call x1, Pallas kernels, reduce_products(): pl.pallas_call(lambda *refs: product_kernel(devices, pieces, spread, *ref...  117 us
    pallas_call x1, Pallas kernels, gather_all(): pl.pallas_call(lambda *refs: gather_kernel(devices, pieces, *refs), in_sp...  101 us
    pallas_call x1, Pallas kernels, on_device(): token_call(middle_kernel, count, [by_tokens(D), by_tokens(D), resident(16...  35.5 us
    pallas_call x1, Pallas kernels, attention_backward(): pl.pallas_call(lambda *refs: attn_backward_kernel(count, blocks, *refs),...  33.3 us
    pallas_call x1, Pallas kernels, on_device(): token_call(middle_back_kernel, count, [by_tokens(DC), by_tokens(DC), by_t...  27.6 us
    dot_general x6, matrix products, contract_rows(): lax.dot_general(lhs_mat, rhs_mat, (((0,), (0,)), ((), ())), preferred_ele...  19.3 us
    pallas_call x1, Pallas kernels, on_device(): token_call(first_kernel, count, [by_tokens(1), by_tokens(1), resident(dev...  18.2 us
    pallas_call x1, Pallas kernels, attention_forward(): pl.pallas_call(lambda *refs: attn_forward_kernel(count, *refs), grid=(blo...  13.6 us

profile of v6, /device:TPU:0, one launch (start us, length us, event | category | flops | bytes accessed | tf_op | source)
XLA Modules:
  0.0 464.5 jit_solution(9580798714749368243)
XLA Ops:
  9.9 1.3 multiply_reduce_fusion
  11.5 2.0 convert_element_type.174
  15.0 100.9 %shard_map.409 = (bf16[32,96,768]{2,1,0:T(8,128)(2,1)}, bf16[32,96,768]{2,1,0:T(8,128)(2,1)}, bf16[32,96,768]{2,1,0:T(8,128)(2,1)}, bf16[32,48,128]{2,1,0:T(8,12...) custom-call(bf16[96,768]{1,0:T(8,128)(2,1)S(1)} %get-tuple-element.215.refs_0_, ...), custom_call_target="tpu_custom_call" | custom-call | tf_op jit(solution)/shard_map/pallas_call | solution.py:434
  116.0 1.4 copy-done.40
  122.4 18.2 %shard_map.410 = (f32[1280,768]{1,0:T(8,128)}, f32[1280,1]{1,0:T(8,128)}, bf16[1280,768]{1,0:T(8,128)(2,1)}, bf16[1280,2304]{1,0:T(8,128)(2,1)}) custom-call(s32[1280,1]{1,0:T(8,128)S(1)} %get-tuple-element.170.row_ref, s32[1280,1]{1,0:T(8,128)} %broadcast_in_dim.25.place_ref, bf16[1536,768]{1,0:T(8,128)(2,1)} %get-tuple-element.129.packed_ref, ...), custom_call_target="tpu_custom_call" | custom-call | flops 4655677440 | bytes 30000000 | tf_op jit(solution)/shard_map/pallas_call | solution.py:1207
  141.0 2.7 copy-done
  143.7 13.6 %shard_map.411 = (bf16[1280,768]{1,0:T(8,128)(2,1)S(1)}, f32[16,1280]{1,0:T(8,128)S(1)}) custom-call(s32[1280,1]{1,0:T(8,128)S(1)} %broadcast_in_dim.23.refs_0_, s32[10,1,256]{2,1,0:T(1,128)S(1)} %constant_dynamic-update-slice_fusion.refs_1_, bf16[1280,2304]{1,0:T(8,128)(2,1)S(1)} %copy-done), custom_call_target="tpu_custom_call" | custom-call | flops 2013265920 | bytes 12000000 | tf_op jit(solution)/shard_map/pallas_call | solution.py:196
  157.3 1.3 copy-done.1
  160.9 35.5 %shard_map.412 = (f32[1280,768]{1,0:T(8,128)}, f32[1280,1]{1,0:T(8,128)}, bf16[1280,768]{1,0:T(8,128)(2,1)}, bf16[1280,3072]{1,0:T(8,128)(2,1)}, bf16[1280,3072]...) custom-call(bf16[1280,768]{1,0:T(8,128)(2,1)} %copy-done.1, ...), custom_call_target="tpu_custom_call" | custom-call | flops 13841203200 | bytes 30000000 | tf_op jit(solution)/shard_map/pallas_call | solution.py:1237
  196.4 4.0 fusion.51
  200.8 3.3 fusion.29
  207.8 5.9 %all_gather.6 = f32[32,128]{1,0:T(8,128)S(1)} all-gather(f32[8,128]{1,0:T(8,128)S(1)} %select_subtract_fusion), channel_id=1, replica_groups=mesh['grp'=8,'psg'=4] {'psg'}, dimensions={0}, use_global_device_ids=true | all-gather | bytes 20480 | tf_op jit(solution)/shard_map/all_gather | solution.py:1288
  218.0 4.4 fusion.31
  223.0 3.9 fusion.38
  227.9 27.6 %shard_map.413 = (bf16[1280,128]{1,0:T(8,128)(2,1)}, bf16[1280,768]{1,0:T(8,128)(2,1)}, bf16[1280,3072]{1,0:T(8,128)(2,1)}, f32[1280,768]{1,0:T(8,128)}, bf16[12...) custom-call(f32[1280,128]{1,0:T(8,128)} %pad_maximum_fusion.grad_ref, ...), custom_call_target="tpu_custom_call" | custom-call | flops 13841203200 | bytes 30000000 | tf_op jit(solution)/shard_map/pallas_call | solution.py:1321
  255.5 1.5 copy.83.refs_1_
  257.6 33.3 %shard_map.414.z_ref.refs_0_ = bf16[1280,3072]{1,0:T(8,128)(2,1)} custom-call(s32[10,1,128]{2,1,0:T(1,128)} %reshape.400.refs_0_, s32[10,256,1]{2,1,0:T(8,128)} %copy.83.refs_1_, bf16[1280,2304]{1,0:T(8,128)(2,1)} %get-tuple-element.132.refs_2_, bf16[1280,768]{1,0:T(8,128)(2,1)} %get-tuple-element.146.refs_3_, f32[16,1280]{1,0:T(8,128)} %copy-done.2, ...), custom_call_target="tpu_custom_call" | custom-call | flops 5033164800 | bytes 18000000 | tf_op jit(solution)/shard_map/pallas_call | solution.py:218
  290.9 12.7 %shard_map.415 = (bf16[1280,768]{1,0:T(8,128)(2,1)S(1)}, f32[64,768]{1,0:T(8,128)}, f32[8,768]{1,0:T(8,128)}) custom-call(bf16[1280,3072]{1,0:T(8,128)(2,1)} %shard_map.414.z_ref.refs_0_, f32[1280,768]{1,0:T(8,128)} %get-tuple-element.156.done_ref, f32[1280,768]{1,0:T(8,128)} %get-tuple-element.134.zero_ref, f32[1280,1]{1,0:T(8,128)} %get-tuple-element.157.inv_ref, ...), custom_call_target="tpu_custom_call" | custom-call | flops 4655677440 | bytes 30000000 | tf_op jit(solution)/shard_map/pallas_call | solution.py:1350
  307.9 5.2 %fusion.21 = bf16[1536,768]{1,0:T(8,128)(2,1)} fusion(bf16[1280,768]{1,0:T(8,128)(2,1)S(1)} %get-tuple-element.162, s32[1280]{0:T(1024)S(1)} %get-tuple-element.196), kind=kOutput, calls=%fused_computation.43 | convolution fusion | flops 3023044608 | bytes 4330496 | tf_op jit(solution)/shard_map/dot_general | solution.py:44
  314.0 1.4 fusion.33
  316.5 116.9 %shard_map.416 = (f32[96,768]{1,0:T(8,128)}, f32[96,768]{1,0:T(8,128)}, f32[96,768]{1,0:T(8,128)}, f32[64,128]{1,0:T(8,128)}, f32[16,128]{1,0:T(8,128)}, /*index=5*/bf16[32,48,768]{2,1,0:T(8,128)(2,1)}) custom-call(bf16[1280,3072]{1,0:T(8,128)(2,1)} %shard_map.414.z_ref.refs_0_, bf16[1280,3072]{1,0:T(8,128)(2,1)} %get-tuple-element.149.refs_1_, ...), custom_call_target="tpu_custom_call" | custom-call | tf_op jit(solution)/shard_map/pallas_call | solution.py:838
  433.4 6.4 %conditional.3 = (f32[960,768]{1,0:T(8,128)}) conditional(s32[]{:T(128)} %convert_element_type.175, (f32[32,1024]{1,0:T(8,128)S(1)}, bf16[32,48,768]{2,1,0:T(8,128)(2,1)}) %tuple.26, (s32[1280]{0:T(1024)S(1)}, bf16[1280,768]{1,0:T(8,128)(2,1)}) %tuple.72), branch_computations={%region_18.19_spmd, %region_19.22_spmd} | conditional | flops 2266398720 | bytes 404044864 | solution.py:1423
  433.4 6.4 %fusion.7 = f32[960,768]{1,0:T(8,128)} fusion(bf16[32,48,768]{2,1,0:T(8,128)(2,1)} %get-tuple-element.60, f32[32,960]{1,0:T(8,128)S(1)} %bitcast.143, f32[48]{0:T(128)S(1)} %iota_convert_fusion), kind=kOutput, calls=%fused_computation.12 | convolution fusion | flops 2266398720 | bytes 5431488 | tf_op jit(solution)/shard_map/cond/branch_0_fun/dot_general | solution.py:44
  440.6 6.4 %multiply_subtract_fusion = (f32[960,768]{1,0:T(8,128)}, f32[960,768]{1,0:T(8,128)}) fusion(f32[960,768]{1,0:T(8,128)S(1)} %copy-done.3, f32[960,768]{1,0:T(8,128)} %get-tuple-element.267, f32[960,768]{1,0:T(8,128)} %param.39, f32[]{:T(128)} %bitcast.37, f32[]{:T(128)} %bitcast.36, f32[960,768]{1,0:T(8,128)} %param.40), kind=kLoop, calls=%fused_computation.45 | loop fusion | flops 11059200 | bytes 17694728 | tf_op jit(solution)/shard_map/sub | solution.py:1085
  (208 shorter events, 35.9 us)
Async XLA Ops:
  200.5 3.6 copy-start.5
  204.1 10.2 %copy-start.7 = (bf16[4,1280,128]{2,1,0:T(8,128)(2,1)S(1)}, bf16[4,1280,128]{2,1,0:T(8,128)(2,1)}, u32[]{:S(2)}) copy-start(bf16[4,1280,128]{2,1,0:T(8,128)(2,1)} %get-tuple-element.137) | copy-start | bytes 3932164
  204.2 10.2 %copy-start.17 = (bf16[1280,128]{1,0:T(8,128)(2,1)S(1)}, bf16[1280,128]{1,0:T(8,128)(2,1)}, u32[]{:S(2)}) copy-start(bf16[1280,128]{1,0:T(8,128)(2,1)} %get-tuple-element.138) | copy-start | bytes 983044
  290.8 14.6 %copy-start.32 = (f32[8,768]{1,0:T(8,128)S(1)}, f32[8,768]{1,0:T(8,128)}, u32[]{:S(2)}) copy-start(f32[8,768]{1,0:T(8,128)} %get-tuple-element.160) | copy-start | bytes 73732
  290.8 14.8 %copy-start.33 = (f32[1,3072]{1,0:T(1,128)S(1)}, f32[1,3072]{1,0:T(1,128)}, u32[]{:S(2)}) copy-start(f32[1,3072]{1,0:T(1,128)} %get-tuple-element.161) | copy-start | bytes 36868
  290.9 15.6 %copy-start.41 = (s32[1,1024]{1,0:T(1,128)S(1)}, s32[1,1024]{1,0:T(1,128)}, u32[]{:S(2)}) copy-start(s32[1,1024]{1,0:T(1,128)} %param.36) | copy-start | bytes 12292
  303.5 9.6 %copy-start.6 = (bf16[1280,768]{1,0:T(8,128)(2,1)}, bf16[1280,768]{1,0:T(8,128)(2,1)S(1)}, u32[]{:S(2)}) copy-start(bf16[1280,768]{1,0:T(8,128)(2,1)S(1)} %get-tuple-element.162) | copy-start | bytes 5898244
  307.9 5.2 %copy-start.43 = (bf16[1280,768]{1,0:T(8,128)(2,1)S(1)}, bf16[1280,768]{1,0:T(8,128)(2,1)}, u32[]{:S(2)}) copy-start(bf16[1280,768]{1,0:T(8,128)(2,1)} %get-tuple-element.154) | copy-start | bytes 5898244
  307.9 5.2 %copy-start.44 = (bf16[1280,128]{1,0:T(8,128)(2,1)S(1)}, bf16[1280,128]{1,0:T(8,128)(2,1)}, u32[]{:S(2)}) copy-start(bf16[1280,128]{1,0:T(8,128)(2,1)} %get-tuple-element.155) | copy-start | bytes 983044
  433.4 7.2 %copy-start.3 = (f32[960,768]{1,0:T(8,128)S(1)}, f32[960,768]{1,0:T(8,128)}, u32[]{:S(2)}) copy-start(f32[960,768]{1,0:T(8,128)} %param.38) | copy-start | bytes 8847364
  440.5 6.6 %copy-start.9 = (f32[768,96]{0,1:T(8,128)S(1)}, f32[768,96]{0,1:T(8,128)}, u32[]{:S(2)}) copy-start(f32[768,96]{0,1:T(8,128)} %param.41) | copy-start | bytes 884740
  440.6 6.6 %copy-start.16 = (f32[96,768]{1,0:T(8,128)S(1)}, f32[96,768]{1,0:T(8,128)}, u32[]{:S(2)}) copy-start(f32[96,768]{1,0:T(8,128)} %get-tuple-element.167) | copy-start | bytes 884740
  440.6 6.6 %copy-start.18 = (f32[768,96]{0,1:T(8,128)S(1)}, f32[768,96]{0,1:T(8,128)}, u32[]{:S(2)}) copy-start(f32[768,96]{0,1:T(8,128)} %param.42) | copy-start | bytes 884740
  440.6 6.6 %copy-start.19 = (f32[768,96]{0,1:T(8,128)S(1)}, f32[768,96]{0,1:T(8,128)}, u32[]{:S(2)}) copy-start(f32[768,96]{0,1:T(8,128)} %param.43) | copy-start | bytes 884740
  440.6 7.6 %copy-start.11 = (f32[768,96]{0,1:T(8,128)S(1)}, f32[768,96]{0,1:T(8,128)}, u32[]{:S(2)}) copy-start(f32[768,96]{0,1:T(8,128)} %param.44) | copy-start | bytes 884740
  440.6 7.6 %copy-start.15 = (f32[96,768]{1,0:T(8,128)S(1)}, f32[96,768]{1,0:T(8,128)}, u32[]{:S(2)}) copy-start(f32[96,768]{1,0:T(8,128)} %get-tuple-element.168) | copy-start | bytes 884740
  440.6 7.6 %copy-start.20 = (f32[768,96]{0,1:T(8,128)S(1)}, f32[768,96]{0,1:T(8,128)}, u32[]{:S(2)}) copy-start(f32[768,96]{0,1:T(8,128)} %param.45) | copy-start | bytes 884740
  440.6 7.6 %copy-start.21 = (f32[768,96]{0,1:T(8,128)S(1)}, f32[768,96]{0,1:T(8,128)}, u32[]{:S(2)}) copy-start(f32[768,96]{0,1:T(8,128)} %param.46) | copy-start | bytes 884740
  447.0 3.3 copy-start.25
  447.1 3.2 copy-start.28
  447.1 3.9 copy-start.27
  447.1 3.9 copy-start.36
  447.1 3.8 copy-start.37
  447.1 3.8 copy-start.38
  (21 other events, 43.1 us)
